TPU v7x, 32 devices: a whole 2x2x4 slice. The times are simulated.
32 devices in a mesh: rep: 4 (over y, x), tr: 4 (over z), tc: 2 (over core).
Axes of the slice: x: 2, y: 2, z: 4, core: 2. Of those that a mesh axis runs over, the one named last changes fastest.
Arguments:
- tokens: bfloat16 [128, 16, 8, 1600], P(('rep', 'tr'), None, None, 'tc'), may hold values from -6 to 6
- prefix_kv: bfloat16 [128, 256, 512], P(('rep', 'tr'), None, 'tc')
- ssm_state: float32 [128, 16, 3200], P(('rep', 'tr'), None, 'tc'), may hold values from -6 to 6
- conv_state: float32 [128, 3, 3200], P(('rep', 'tr'), None, 'tc'), may hold values from -6 to 6
- prefix_len: int32 [128], replicated, may hold values from 1 to 256
- group_size: int32 [128], replicated, may hold values from 8 to 16
- serve_replica: int32 [128], replicated, may hold values from 0 to 3, as said below
- in_gain: float32 [1600], P('tc'), may hold values from 0.5 to 1.5
- w_query: bfloat16 [1600, 1024], P(('rep', 'tr'), 'tc'), may hold values from -0.15625 to 0.15625
- w_keyval: bfloat16 [1600, 512], P(('rep', 'tr'), 'tc'), may hold values from -0.15625 to 0.15625
- w_inner: bfloat16 [1600, 2, 3200], P(('rep', 'tr'), None, 'tc'), may hold values from -0.15625 to 0.15625
- conv_weight: float32 [4, 3200], P(None, 'tc'), may hold values from -3 to 3
- conv_bias: float32 [3200], P('tc'), may hold values from -3 to 3
- w_xproj: bfloat16 [3200, 132], P('tc'), may hold values from -0.109375 to 0.109375
- dt_weight: bfloat16 [100, 3200], P(None, 'tc'), may hold values from -0.625 to 0.625
- dt_bias: float32 [3200], P('tc'), may hold values from -4.5 to -1
- decay_log: float32 [16, 3200], P(None, 'tc'), may hold values from -1 to 2.5
- skip_gain: float32 [3200], P('tc'), may hold values from 0.5 to 1.5
- w_attn_out: bfloat16 [1024, 1600], P('tc', ('rep', 'tr'))
- w_ssm_out: bfloat16 [3200, 1600], P('tc', ('rep', 'tr'))
- attn_gain: float32 [1600], replicated, may hold values from 0.5 to 1.5
- ssm_gain: float32 [1600], replicated, may hold values from 0.5 to 1.5
Outputs:
- mixed: bfloat16 [128, 16, 8, 1600], P(('rep', 'tr'), None, None, 'tc')
Inputs may be any that keep to these rules, and one draw needn't show every extreme that they name: `serve_replica`: within each aligned block of 8 groups every replica is named equally often.
All inputs are finite; a program needn't handle non-finite values.
Results may differ from a plain program's by a relative error of at most 0.013.
Values may be sent and summed in bfloat16 or wider, within the bound.
No kernel may reach another device: no remote copies, remote signals or barrier semaphores. Data moves between devices by JAX's collectives and lax.ppermute only.
A program may use at most 192 MiB of HBM per device.

v0:
```python
import jax
import jax.numpy as jnp
from jax import lax
from jax.sharding import PartitionSpec as P

D = 1600
HD = 64
QH = 16
KVH = 4


EPSILON = 1e-06


def table_pick(served, table):
    matches = served[:, None] == jnp.arange(table.shape[0], dtype=jnp.int32)[None, :]
    return jnp.sum(jnp.where(matches, table[None, :], 0), axis=1)


def prefix_scores(group_query, key_block, length, score_scale):
    scores = (
        jnp.einsum("rtkjd,pkd->rtkjp", group_query, key_block, preferred_element_type=jnp.float32)
        * score_scale
    )
    positions = jnp.arange(key_block.shape[0], dtype=jnp.int32)
    return jnp.where(positions < length, scores, -jnp.inf)


def local(
    tokens,
    prefix_kv,
    ssm_state,
    conv_state,
    prefix_len,
    group_size,
    serve_replica,
    in_gain,
    w_query,
    w_keyval,
    w_inner,
    conv_weight,
    conv_bias,
    w_xproj,
    dt_weight,
    dt_bias,
    decay_log,
    skip_gain,
    w_attn_out,
    w_ssm_out,
    attn_gain,
    ssm_gain,
):
    rep_count = lax.axis_size("rep")
    my_replica = lax.axis_index("rep")
    row_axis = lax.axis_size("tr")
    my_row = lax.axis_index("tr")
    tensor_count = lax.axis_size("tc")
    tensor_index = lax.axis_index("tc")
    group_count, slot_count, new_count, width_part = tokens.shape
    pair_count = group_count // rep_count
    head_dim = HD
    kv_here = KVH // tensor_count
    per_kv = QH // KVH
    heads_here = QH // tensor_count
    score_scale = head_dim ** (-0.5)
    row_count = group_count * slot_count * new_count
    request_count = group_count * slot_count
    route_plan = serve_replica.reshape(rep_count, row_axis, group_count)
    column = lax.dynamic_index_in_dim(route_plan, my_row, 1, keepdims=False)
    orders = jnp.argsort(column, axis=1, stable=True)
    send_order = lax.dynamic_index_in_dim(orders, my_replica, 0, keepdims=False)
    picked = lax.dynamic_slice_in_dim(orders, my_replica * pair_count, pair_count, 1)
    block_ids = jnp.arange(rep_count, dtype=jnp.int32) * row_axis + my_row
    served = (block_ids[:, None] * group_count + picked).reshape(group_count)
    lengths = table_pick(served, prefix_len)
    live_sizes = table_pick(served, group_size)
    moved_tokens, moved_cache = (
        lax.all_to_all(
            jnp.take(tokens, send_order, axis=0), "rep", split_axis=0, concat_axis=0, tiled=True
        ),
        lax.all_to_all(
            jnp.take(prefix_kv, send_order, axis=0), "rep", split_axis=0, concat_axis=0, tiled=True
        ),
    )
    moved_state, moved_conv = (
        lax.all_to_all(
            jnp.take(ssm_state, send_order, axis=0).astype(jnp.bfloat16),
            "rep",
            split_axis=0,
            concat_axis=0,
            tiled=True,
        ).astype(jnp.float32),
        lax.all_to_all(
            jnp.take(conv_state, send_order, axis=0).astype(jnp.bfloat16),
            "rep",
            split_axis=0,
            concat_axis=0,
            tiled=True,
        ).astype(jnp.float32),
    )
    x_rows = moved_tokens.reshape(row_count, width_part).astype(jnp.float32)
    square_sums = lax.psum(jnp.sum(x_rows * x_rows, axis=1), "tc")
    inv_rms = lax.rsqrt(square_sums / D + EPSILON)
    normed_part = (x_rows * inv_rms[:, None] * in_gain[None, :]).astype(jnp.bfloat16)
    normed = lax.all_gather(normed_part, "tc", axis=1, tiled=True)
    channels = w_inner.shape[2]
    inner_cols = w_inner.reshape(w_inner.shape[0], 2 * channels)
    pieces = (
        lax.all_gather(w_query, ("rep", "tr"), axis=0, tiled=True),
        lax.all_gather(w_keyval, ("rep", "tr"), axis=0, tiled=True),
        lax.all_gather(inner_cols, ("rep", "tr"), axis=0, tiled=True),
    )
    query_run = jnp.dot(normed, pieces[0], preferred_element_type=jnp.float32)
    keyval_run = jnp.dot(normed, pieces[1], preferred_element_type=jnp.float32)
    inner_run = jnp.dot(normed, pieces[2], preferred_element_type=jnp.float32)
    query = query_run.astype(jnp.bfloat16).reshape(
        group_count, slot_count, new_count, kv_here, per_kv, head_dim
    )
    keyval = keyval_run.astype(jnp.bfloat16).reshape(
        group_count, slot_count, new_count, kv_here, 2, head_dim
    )
    cache_len = moved_cache.shape[1]
    cache_heads = moved_cache.reshape(group_count, cache_len, kv_here, 2, head_dim)
    causal = jnp.arange(new_count)[None, :] <= jnp.arange(new_count)[:, None]

    def attend(group_args):
        group_query, group_kv, group_cache, length = group_args
        key_all = group_cache[:, :, 0]
        value_all = group_cache[:, :, 1]
        own_scores = (
            jnp.einsum(
                "rtkjd,rskd->rtkjs",
                group_query,
                group_kv[:, :, :, 0],
                preferred_element_type=jnp.float32,
            )
            * score_scale
        )
        own_scores = jnp.where(causal[None, :, None, None, :], own_scores, -jnp.inf)
        own_max = jnp.max(own_scores, axis=4)
        scores = prefix_scores(group_query, key_all, length, score_scale)
        row_max = jnp.maximum(jnp.max(scores, axis=4), own_max)
        prefix_weights = jnp.exp(scores - row_max[..., None])
        row_totals = jnp.sum(prefix_weights, axis=4)
        weighted = jnp.einsum(
            "rtkjp,pkd->rtkjd",
            prefix_weights.astype(jnp.bfloat16),
            value_all,
            preferred_element_type=jnp.float32,
        )
        own_weights = jnp.exp(own_scores - row_max[..., None])
        row_totals = row_totals + jnp.sum(own_weights, axis=4)
        weighted = weighted + jnp.einsum(
            "rtkjs,rskd->rtkjd",
            own_weights.astype(jnp.bfloat16),
            group_kv[:, :, :, 1],
            preferred_element_type=jnp.float32,
        )
        return (
            (weighted / row_totals[..., None])
            .astype(jnp.bfloat16)
            .reshape(slot_count, new_count, heads_here * head_dim)
        )

    heads = lax.map(attend, (query, keyval, cache_heads, lengths)).reshape(
        row_count, heads_here * head_dim
    )
    inner = inner_run.reshape(group_count, slot_count, new_count, 2, channels)
    conv_in = inner[:, :, :, 0]
    gate = inner[:, :, :, 1].reshape(row_count, channels)
    history = jnp.broadcast_to(
        moved_conv[:, None], (group_count, slot_count, moved_conv.shape[1], channels)
    )
    sequence = jnp.concatenate([history, conv_in], axis=2)
    conv_sum = jnp.broadcast_to(conv_bias, (group_count, slot_count, new_count, channels))
    for tap_index in range(conv_weight.shape[0]):
        conv_sum = (
            conv_sum + conv_weight[tap_index] * sequence[:, :, tap_index : tap_index + new_count]
        )
    conv_out = jax.nn.silu(conv_sum).astype(jnp.bfloat16).reshape(row_count, channels)
    projected = lax.psum(
        jnp.dot(conv_out, w_xproj, preferred_element_type=jnp.float32).astype(jnp.bfloat16), "tc"
    ).astype(jnp.float32)
    rank_width = dt_weight.shape[0]
    state_size = decay_log.shape[0]
    step_in = projected[:, :rank_width].astype(jnp.bfloat16)
    input_mix = projected[:, rank_width : rank_width + state_size]
    output_mix = projected[:, rank_width + state_size :]
    step_size = jax.nn.softplus(
        jnp.dot(step_in, dt_weight, preferred_element_type=jnp.float32) + dt_bias
    )
    decay_rate = -jnp.exp(decay_log)

    def token_major(values):
        return values.reshape(request_count, new_count, values.shape[1]).swapaxes(0, 1)

    start_state = jnp.broadcast_to(
        moved_state[:, None], (group_count, slot_count, state_size, channels)
    ).reshape(request_count, state_size, channels)

    def advance(carried, inputs):
        step_now, value_now, mix_in, mix_out = inputs
        carried = (
            jnp.exp(step_now[:, None, :] * decay_rate[None]) * carried
            + (step_now * value_now)[:, None, :] * mix_in[:, :, None]
        )
        result = jnp.sum(carried * mix_out[:, :, None], axis=1) + skip_gain * value_now
        return (carried, result)

    last_state, outputs = lax.scan(
        advance,
        start_state,
        (
            token_major(step_size),
            token_major(conv_out.astype(jnp.float32)),
            token_major(input_mix),
            token_major(output_mix),
        ),
    )
    ssm_out = outputs.swapaxes(0, 1).reshape(row_count, channels)
    gated = (ssm_out * jax.nn.silu(gate)).astype(jnp.bfloat16)
    pieces = (
        lax.all_gather(w_attn_out, ("rep", "tr"), axis=1, tiled=True),
        lax.all_gather(w_ssm_out, ("rep", "tr"), axis=1, tiled=True),
    )
    attn_part = jnp.dot(heads, pieces[0], preferred_element_type=jnp.float32)
    ssm_part = jnp.dot(gated, pieces[1], preferred_element_type=jnp.float32)
    attn_cols, ssm_cols = (
        lax.psum_scatter(
            attn_part.astype(jnp.bfloat16), "tc", scatter_dimension=1, tiled=True
        ).astype(jnp.float32),
        lax.psum_scatter(
            ssm_part.astype(jnp.bfloat16), "tc", scatter_dimension=1, tiled=True
        ).astype(jnp.float32),
    )
    attn_sq, ssm_sq = lax.psum(
        (jnp.sum(attn_cols * attn_cols, axis=1), jnp.sum(ssm_cols * ssm_cols, axis=1)), "tc"
    )
    attn_share = lax.dynamic_slice_in_dim(attn_gain, tensor_index * width_part, width_part, 0)
    ssm_share = lax.dynamic_slice_in_dim(ssm_gain, tensor_index * width_part, width_part, 0)
    attn_rms = lax.rsqrt(attn_sq / D + EPSILON)[:, None]
    ssm_rms = lax.rsqrt(ssm_sq / D + EPSILON)[:, None]
    branch = 0.5 * (attn_share * attn_cols * attn_rms + ssm_share * ssm_cols * ssm_rms)
    live = jnp.arange(slot_count)[None, :] < live_sizes[:, None]
    live_rows = jnp.broadcast_to(live[:, :, None], (group_count, slot_count, new_count)).reshape(
        row_count, 1
    )
    mixed = jnp.where(live_rows, x_rows + branch, 0.0).astype(jnp.bfloat16)
    return mixed.reshape(group_count, slot_count, new_count, width_part)


def solution(mesh):
    placed = (
        P(("rep", "tr"), None, None, "tc"),
        P(("rep", "tr"), None, "tc"),
        P(("rep", "tr"), None, "tc"),
        P(("rep", "tr"), None, "tc"),
        P(),
        P(),
        P(),
        P("tc"),
        P(("rep", "tr"), "tc"),
        P(("rep", "tr"), "tc"),
        P(("rep", "tr"), None, "tc"),
        P(None, "tc"),
        P("tc"),
        P("tc", None),
        P(None, "tc"),
        P("tc"),
        P(None, "tc"),
        P("tc"),
        P("tc", ("rep", "tr")),
        P("tc", ("rep", "tr")),
        P(),
        P(),
    )
    return jax.shard_map(
        local,
        mesh=mesh,
        in_specs=placed,
        out_specs=P(("rep", "tr"), None, None, "tc"),
        check_vma=False,
    )
```

profile of v0, /device:TPU:0, one launch (start us, length us, event | category | flops | bytes accessed | tf_op | source)
XLA Modules:
  0.0 642.6 jit_solution(9718963318840832552)
XLA Ops:
  14.1 28.3 %all_to_all.20 = bf16[8,16,8,800]{3,2,1,0:T(8,128)(2,1)S(1)} all-to-all(bf16[8,16,8,800]{3,2,1,0:T(8,128)(2,1)S(1)} %broadcast_select_fusion), channel_id=1, replica_groups=mesh['rep'=4,'tr'=4,'tc'=2] {'rep'}, dimensions={0} | all-to-all | bytes 3276800 | tf_op jit(solution)/shard_map/all_to_all | solution.py:78
  61.2 51.1 %all-gather.1 = bf16[16,100,256]{2,1,0:T(8,128)(2,1)S(1)} all-gather(bf16[1,100,256]{2,1,0:T(8,128)(2,1)S(1)} %bitcast.197), channel_id=1, replica_groups=mesh['rep'=4,'tr'=4,'tc'=2] {'rep','tr'}, dimensions={0}, use_global_device_ids=true | all-gather | bytes 870400 | tf_op jit(solution)/shard_map/all_gather | solution.py:110
  127.3 13.0 %all-gather.15.cloned.1.call-done = bf16[16,100,512]{2,1,0:T(8,128)(2,1)} async-done(((bf16[1,100,512]{2,1,0:T(8,128)(2,1)}), bf16[16,100,512]{2,1,0:T(8,128)(2,1)}) %all-gather.15.cloned.1.call-update) | async-done | bytes 1638416 | tf_op jit(solution)/shard_map/all_gather | solution.py:223
  143.7 9.4 %all-gather.11.cloned.1.call-done = bf16[1024,1600]{0,1:T(8,128)(2,1)} async-done(((bf16[1024,800]{0,1:T(8,128)(2,1)}), bf16[1024,1600]{0,1:T(8,128)(2,1)}) %all-gather.11.cloned.1.call-update) | async-done | bytes 3276816 | tf_op jit(solution)/shard_map/all_gather | solution.py:105
  153.0 5.0 convolution_convert_fusion.2
  158.0 4.7 reshape.169
  167.3 76.5 %while.24 = (s32[]{:T(128)}, bf16[8,16,8,512]{3,2,1,0:T(8,128)(2,1)}, bf16[8,256,2,2,64]{1,4,3,2,0:T(8,128)(2,1)}, s32[8]{0:T(128)}, bf16[8,16,8,2,4,64]{5,4,3,2...) while((s32[]{:T(128)}, bf16[8,16,8,512]{3,2,1,0:T(8,128)(2,1)}, ...), condition=%wide.region_10.11_spmd.clone, body=%wide.region_5.10_spmd.clone.sunk | while | flops 71293248 | bytes 7227317 | solution.py:165
  243.8 46.8 %all-gather.17.cloned.1.call-done = bf16[16,100,3200]{2,1,0:T(8,128)(2,1)} async-done(((bf16[1,100,3200]{2,1,0:T(8,128)(2,1)}), bf16[16,100,3200]{2,1,0:T(8,128)(2,1)}) %all-gather.17.cloned.1.call-update) | async-done | bytes 10240016 | tf_op jit(solution)/shard_map/all_gather | solution.py:111
  290.6 10.7 %reshape.222 = bf16[1600,3200]{1,0:T(8,128)(2,1)} reshape(bf16[16,100,3200]{2,1,0:T(8,128)(2,1)} %all-gather.17.cloned.1.call-done) | data formatting | bytes 20480000
  301.3 19.0 %fusion.50 = f32[1024,3200]{1,0:T(8,128)} fusion(bf16[1024,1600]{0,1:T(8,128)(2,1)} %all-gather.11.cloned.1.call-done, bf16[1600,3200]{1,0:T(8,128)(2,1)} %reshape.222), kind=kOutput, calls=%fused_computation.123 | convolution fusion | flops 10485760000 | bytes 26624000 | tf_op jit(solution)/shard_map/dot_general | solution.py:115
  320.4 17.3 %reshape.174 = f32[8,16,8,2,1600]{4,3,2,1,0:T(2,128)} reshape(f32[1024,3200]{1,0:T(8,128)} %fusion.50) | data formatting | bytes 26214400 | tf_op jit(solution)/shard_map/reshape | solution.py:168
  337.6 16.0 %fusion.48 = (f32[8,16,8,1,1600]{4,3,2,1,0:T(1,128)S(1)}, f32[8,16,8,1,1600]{4,3,2,1,0:T(1,128)}) fusion(f32[8,16,8,2,1600]{4,3,2,1,0:T(2,128)} %reshape.174), kind=kLoop, calls=%fused_computation.121 | loop fusion | bytes 26214400 | tf_op jit(solution)/shard_map/slice | solution.py:169
  361.7 15.4 %multiply_convert_fusion = bf16[8,16,8,1600]{3,2,1,0:T(8,128)(2,1)S(1)} fusion(f32[8,16,8,1600]{3,2,1,0:T(8,128)} %bitcast.184, f32[8,16,3,1600]{3,2,1,0:T(4,128)S(1)} %broadcast_in_dim.169, f32[1600]{0:T(1024)S(1)} %copy-done.10, f32[1600]{0:T(1024)S(1)} %copy-done.11, f32[1600]{0:T(1024)S(1)} %copy-done.9, f32[1600]{0:T(1024)S(1)} %get-tuple-element.203, ...), kind=kLoop, calls=%fused_computation.71 | loop fusion | flops 26214400 | bytes 12320000 | tf_op jit(solution)/shard_map/convert_element_type | solution.py:180
  381.1 4.8 convolution_convert_fusion.1
  386.0 8.3 %reshape.224 = bf16[1600,1600]{1,0:T(8,128)(2,1)} reshape(bf16[16,100,1600]{2,1,0:T(8,128)(2,1)} %all-gather.19.cloned.1.call-done) | data formatting | bytes 10240000
  394.3 5.3 copy.176
  399.6 6.3 copy.198
  405.9 7.6 %compare_select_fusion = f32[1024,1600]{0,1:T(8,128)} fusion(bf16[100,1600]{1,0:T(8,128)(2,1)S(1)} %copy-done.23, f32[1600]{0:T(1024)S(1)} %copy-done.24, bf16[1024,132]{0,1:T(8,128)(2,1)} %all-reduce.3.cloned.1.call-done), kind=kOutput, calls=%fused_computation.49 | convolution fusion | flops 339148800 | bytes 7092992 | tf_op jit(solution)/shard_map/dot_general | solution.py:190
  413.5 7.6 %copy.175 = f32[1024,1600]{1,0:T(8,128)} copy(f32[1024,1600]{0,1:T(8,128)} %compare_select_fusion) | data formatting | bytes 13107200 | tf_op jit(solution)/shard_map/jit(softplus)/select_n | solution.py:189
  423.2 5.9 broadcast_in_dim.164
  429.2 164.7 %while.23 = (s32[]{:T(128)}, f32[128,16,1600]{2,1,0:T(8,128)}, f32[8,128,1600]{2,1,0:T(8,128)}, f32[8,128,1600]{2,0,1:T(8,128)}, f32[16,1600]{1,0:T(8,128)S(1)},...) while((s32[]{:T(128)}, f32[128,16,1600]{2,1,0:T(8,128)}, ...), condition=%wide.region_17.18_spmd, body=%wide.region_15.17_spmd.sunk | while | flops 20070400 | bytes 37087612 | solution.py:210
  435.2 12.4 %multiply_reduce_fusion.3 = (f32[128,1600]{1,0:T(8,128)S(1)}, f32[128,16,1600]{2,1,0:T(8,128)}) fusion(f32[128,16]{1,0:T(8,128)S(1)} %bitcast.191, f32[128,16]{1,0:T(8,128)S(1)} %bitcast.192, f32[128,1600]{1,0:T(8,128)S(1)} %bitcast_multiply_fusion.3, f32[128,16,1600]{2,1,0:T(8,128)} %get-tuple-element.397, f32[16,1600]{1,0:T(8,128)S(1)} %get-tuple-element.410, ...), kind=kLoop, calls=%fused_computation.5.clone.1 | loop fusion | flops 19456000 | bytes 28790784 | tf_op jit(solution)/shard_map/while/body/eval_jaxpr/reduce_sum | solution.py:207
  455.7 12.4 %multiply_reduce_fusion.3 = (f32[128,1600]{1,0:T(8,128)S(1)}, f32[128,16,1600]{2,1,0:T(8,128)}) fusion(f32[128,16]{1,0:T(8,128)S(1)} %bitcast.191, f32[128,16]{1,0:T(8,128)S(1)} %bitcast.192, f32[128,1600]{1,0:T(8,128)S(1)} %bitcast_multiply_fusion.3, f32[128,16,1600]{2,1,0:T(8,128)} %get-tuple-element.397, f32[16,1600]{1,0:T(8,128)S(1)} %get-tuple-element.410, ...), kind=kLoop, calls=%fused_computation.5.clone.1 | loop fusion | flops 19456000 | bytes 28790784 | tf_op jit(solution)/shard_map/while/body/eval_jaxpr/reduce_sum | solution.py:207
  476.3 12.4 %multiply_reduce_fusion.3 = (f32[128,1600]{1,0:T(8,128)S(1)}, f32[128,16,1600]{2,1,0:T(8,128)}) fusion(f32[128,16]{1,0:T(8,128)S(1)} %bitcast.191, f32[128,16]{1,0:T(8,128)S(1)} %bitcast.192, f32[128,1600]{1,0:T(8,128)S(1)} %bitcast_multiply_fusion.3, f32[128,16,1600]{2,1,0:T(8,128)} %get-tuple-element.397, f32[16,1600]{1,0:T(8,128)S(1)} %get-tuple-element.410, ...), kind=kLoop, calls=%fused_computation.5.clone.1 | loop fusion | flops 19456000 | bytes 28790784 | tf_op jit(solution)/shard_map/while/body/eval_jaxpr/reduce_sum | solution.py:207
  496.9 12.4 %multiply_reduce_fusion.3 = (f32[128,1600]{1,0:T(8,128)S(1)}, f32[128,16,1600]{2,1,0:T(8,128)}) fusion(f32[128,16]{1,0:T(8,128)S(1)} %bitcast.191, f32[128,16]{1,0:T(8,128)S(1)} %bitcast.192, f32[128,1600]{1,0:T(8,128)S(1)} %bitcast_multiply_fusion.3, f32[128,16,1600]{2,1,0:T(8,128)} %get-tuple-element.397, f32[16,1600]{1,0:T(8,128)S(1)} %get-tuple-element.410, ...), kind=kLoop, calls=%fused_computation.5.clone.1 | loop fusion | flops 19456000 | bytes 28790784 | tf_op jit(solution)/shard_map/while/body/eval_jaxpr/reduce_sum | solution.py:207
  517.4 12.4 %multiply_reduce_fusion.3 = (f32[128,1600]{1,0:T(8,128)S(1)}, f32[128,16,1600]{2,1,0:T(8,128)}) fusion(f32[128,16]{1,0:T(8,128)S(1)} %bitcast.191, f32[128,16]{1,0:T(8,128)S(1)} %bitcast.192, f32[128,1600]{1,0:T(8,128)S(1)} %bitcast_multiply_fusion.3, f32[128,16,1600]{2,1,0:T(8,128)} %get-tuple-element.397, f32[16,1600]{1,0:T(8,128)S(1)} %get-tuple-element.410, ...), kind=kLoop, calls=%fused_computation.5.clone.1 | loop fusion | flops 19456000 | bytes 28790784 | tf_op jit(solution)/shard_map/while/body/eval_jaxpr/reduce_sum | solution.py:207
  538.0 12.4 %multiply_reduce_fusion.3 = (f32[128,1600]{1,0:T(8,128)S(1)}, f32[128,16,1600]{2,1,0:T(8,128)}) fusion(f32[128,16]{1,0:T(8,128)S(1)} %bitcast.191, f32[128,16]{1,0:T(8,128)S(1)} %bitcast.192, f32[128,1600]{1,0:T(8,128)S(1)} %bitcast_multiply_fusion.3, f32[128,16,1600]{2,1,0:T(8,128)} %get-tuple-element.397, f32[16,1600]{1,0:T(8,128)S(1)} %get-tuple-element.410, ...), kind=kLoop, calls=%fused_computation.5.clone.1 | loop fusion | flops 19456000 | bytes 28790784 | tf_op jit(solution)/shard_map/while/body/eval_jaxpr/reduce_sum | solution.py:207
  558.6 12.4 %multiply_reduce_fusion.3 = (f32[128,1600]{1,0:T(8,128)S(1)}, f32[128,16,1600]{2,1,0:T(8,128)}) fusion(f32[128,16]{1,0:T(8,128)S(1)} %bitcast.191, f32[128,16]{1,0:T(8,128)S(1)} %bitcast.192, f32[128,1600]{1,0:T(8,128)S(1)} %bitcast_multiply_fusion.3, f32[128,16,1600]{2,1,0:T(8,128)} %get-tuple-element.397, f32[16,1600]{1,0:T(8,128)S(1)} %get-tuple-element.410, ...), kind=kLoop, calls=%fused_computation.5.clone.1 | loop fusion | flops 19456000 | bytes 28790784 | tf_op jit(solution)/shard_map/while/body/eval_jaxpr/reduce_sum | solution.py:207
  579.3 12.4 %multiply_reduce_fusion.3 = (f32[128,1600]{1,0:T(8,128)S(1)}, f32[128,16,1600]{2,1,0:T(8,128)}) fusion(f32[128,16]{1,0:T(8,128)S(1)} %bitcast.191, f32[128,16]{1,0:T(8,128)S(1)} %bitcast.192, f32[128,1600]{1,0:T(8,128)S(1)} %bitcast_multiply_fusion.3, f32[128,16,1600]{2,1,0:T(8,128)} %get-tuple-element.397, f32[16,1600]{1,0:T(8,128)S(1)} %get-tuple-element.410, ...), kind=kLoop, calls=%fused_computation.5.clone.1 | loop fusion | flops 19456000 | bytes 28790784 | tf_op jit(solution)/shard_map/while/body/eval_jaxpr/reduce_sum | solution.py:207
  593.9 8.9 %fusion.34 = bf16[1024,1600]{1,0:T(8,128)(2,1)S(1)} fusion(f32[8,16,8,1,1600]{4,2,1,0,3:T(8,128)} %copy.198, f32[128,8,1600]{2,0,1:T(8,128)} %bitcast.190), kind=kLoop, calls=%fused_computation.72 | loop fusion | flops 9830400 | bytes 16384000 | tf_op jit(solution)/shard_map/convert_element_type | solution.py:221
  602.8 10.2 %convolution_convert_fusion = bf16[1024,1600]{0,1:T(8,128)(2,1)} fusion(bf16[1024,1600]{1,0:T(8,128)(2,1)S(1)} %fusion.34, bf16[1600,1600]{1,0:T(8,128)(2,1)} %reshape.224), kind=kOutput, calls=%fused_computation.77 | convolution fusion | flops 5244518400 | bytes 11673600 | tf_op jit(solution)/shard_map/dot_general | solution.py:227
  613.5 4.9 copy.184
  (350 shorter events, 221.7 us)
Async XLA Ops:
  6.5 118.4 %all-gather.13.cloned.1.call-start = ((), (), s32[]{:S(2)}) async-start(), calls=%async_computation.10 | async-start | bytes 1810432 | tf_op jit(solution)/shard_map/all_gather | solution.py:109
  7.3 133.0 %all-gather.15.cloned.1.call-start = ((), (), s32[]{:S(2)}) async-start(), calls=%async_computation.11 | async-start | bytes 1810432 | tf_op jit(solution)/shard_map/all_gather | solution.py:223
  8.0 145.0 %all-gather.11.cloned.1.call-start = ((), (), s32[]{:S(2)}) async-start(), calls=%async_computation.6 | async-start | bytes 4915200 | tf_op jit(solution)/shard_map/all_gather | solution.py:105
  9.6 4.5 copy-start.16
  45.5 7.6 %copy-start.6 = (bf16[100,2,1600]{2,1,0:T(2,128)(2,1)S(1)}, bf16[100,2,1600]{2,1,0:T(2,128)(2,1)}, u32[]{:S(2)}) copy-start(bf16[100,2,1600]{2,1,0:T(2,128)(2,1)} %param.36) | copy-start | bytes 1920004
  45.5 9.0 %copy-start.5 = (bf16[8,256,256]{2,1,0:T(8,128)(2,1)S(1)}, bf16[8,256,256]{2,1,0:T(8,128)(2,1)}, u32[]{:S(2)}) copy-start(bf16[8,256,256]{2,1,0:T(8,128)(2,1)} %param.27) | copy-start | bytes 3145732
  49.2 5.9 copy-start.15
  53.0 8.3 %copy-start.8 = (bf16[100,256]{1,0:T(8,128)(2,1)S(1)}, bf16[100,256]{1,0:T(8,128)(2,1)}, u32[]{:S(2)}) copy-start(bf16[100,256]{1,0:T(8,128)(2,1)} %param.35) | copy-start | bytes 153604
  53.0 237.6 %all-gather.17.cloned.1.call-start = ((), (), s32[]{:S(2)}) async-start(), calls=%async_computation.12 | async-start | bytes 11315200 | tf_op jit(solution)/shard_map/all_gather | solution.py:111
  54.4 59.9 %copy-start.3 = (f32[8,3,1600]{2,0,1:T(8,128)S(1)}, f32[8,3,1600]{2,0,1:T(8,128)}, u32[]{:S(2)}) copy-start(f32[8,3,1600]{2,0,1:T(8,128)} %param.29) | copy-start | bytes 460804
  54.4 61.5 %copy-start.12 = (f32[4,1600]{1,0:T(4,128)S(1)}, f32[4,1600]{1,0:T(4,128)}, u32[]{:S(2)}) copy-start(f32[4,1600]{1,0:T(4,128)} %param.37) | copy-start | bytes 76804
  55.1 61.5 %copy-start.19 = (s32[128]{0:T(128)S(1)}, s32[128]{0:T(128)}, u32[]{:S(2)}) copy-start(s32[128]{0:T(128)} %param.31) | copy-start | bytes 1540
  55.1 61.5 %copy-start.20 = (s32[128]{0:T(128)S(1)}, s32[128]{0:T(128)}, u32[]{:S(2)}) copy-start(s32[128]{0:T(128)} %param.30) | copy-start | bytes 1540
  56.2 62.9 %all-to-all-start.1 = ((bf16[8,256,256]{2,1,0:T(8,128)(2,1)}), bf16[8,256,256]{2,1,0:T(8,128)(2,1)S(1)}, u32[]{:S(2)}, u32[]{:S(2)}) async-start(bf16[8,256,256]{2,1,0:T(8,128)(2,1)} %broadcast_select_fusion.1), calls=%async_computation.1 | async-start | bytes 2097152 | tf_op jit(solution)/shard_map/all_to_all | solution.py:81
  59.8 326.2 %all-gather.19.cloned.1.call-start = ((), (), s32[]{:S(2)}) async-start(), calls=%async_computation.13 | async-start | bytes 5883904 | tf_op jit(solution)/shard_map/all_gather | solution.py:224
  119.2 237.9 %all-to-all-start.3 = ((bf16[8,3,1600]{2,1,0:T(4,128)(2,1)}), bf16[8,3,1600]{2,1,0:T(4,128)(2,1)}, u32[]{:S(2)}, u32[]{:S(2)}) async-start(bf16[8,3,1600]{2,1,0:T(4,128)(2,1)} %copy.174), calls=%async_computation.4 | async-start | bytes 212992 | tf_op jit(solution)/shard_map/all_to_all | solution.py:93
  353.6 8.1 %copy-start.9 = (f32[1600]{0:T(1024)S(1)}, f32[1600]{0:T(1024)}, u32[]{:S(2)}) copy-start(f32[1600]{0:T(1024)} %get-tuple-element.204) | copy-start | bytes 19204
  353.6 8.1 %copy-start.10 = (f32[1600]{0:T(1024)S(1)}, f32[1600]{0:T(1024)}, u32[]{:S(2)}) copy-start(f32[1600]{0:T(1024)} %get-tuple-element.205) | copy-start | bytes 19204
  353.6 8.1 %copy-start.11 = (f32[1600]{0:T(1024)S(1)}, f32[1600]{0:T(1024)}, u32[]{:S(2)}) copy-start(f32[1600]{0:T(1024)} %get-tuple-element.206) | copy-start | bytes 19204
  353.6 8.1 %copy-start.13 = (f32[1600]{0:T(1024)S(1)}, f32[1600]{0:T(1024)}, u32[]{:S(2)}) copy-start(f32[1600]{0:T(1024)} %param.38) | copy-start | bytes 19204
  357.0 66.2 %all-to-all-start.2 = ((bf16[8,16,1600]{2,1,0:T(8,128)(2,1)}), bf16[8,16,1600]{2,1,0:T(8,128)(2,1)S(1)}, u32[]{:S(2)}, u32[]{:S(2)}) async-start(bf16[8,16,1600]{2,1,0:T(8,128)(2,1)} %select_convert_fusion), calls=%async_computation.3 | async-start | bytes 851968 | tf_op jit(solution)/shard_map/all_to_all | solution.py:86
  360.5 45.4 %all-reduce.3.cloned.1.call-start = ((), (), s32[]{:S(2)}) async-start(), calls=%async_computation.8 | async-start | bytes 557056 | tf_op jit(solution)/shard_map/psum | solution.py:181
  361.7 17.2 %copy-start.22 = (bf16[1600,132]{0,1:T(8,128)(2,1)S(1)}, bf16[1600,132]{0,1:T(8,128)(2,1)}, u32[]{:S(2)}) copy-start(bf16[1600,132]{0,1:T(8,128)(2,1)} %param.39) | copy-start | bytes 1267204
  381.0 237.4 %reduce-scatter.3.cloned.1.call-start = ((), (), s32[]{:S(2)}) async-start(), calls=%async_computation.7 | async-start | bytes 4915200 | tf_op jit(solution)/shard_map/reduce_scatter | solution.py:229
  385.9 238.7 %reduce-scatter.5.cloned.1.call-start = ((), (), s32[]{:S(2)}) async-start(), calls=%async_computation.9 | async-start | bytes 4915200 | tf_op jit(solution)/shard_map/reduce_scatter | solution.py:232
  399.6 6.3 copy-start.23
  399.6 6.3 copy-start.24
  423.2 5.9 copy-start.7
  602.7 10.3 %copy-start.17 = (f32[1600]{0:T(1024)S(1)}, f32[1600]{0:T(1024)}, u32[]{:S(2)}) copy-start(f32[1600]{0:T(1024)} %param.47) | copy-start | bytes 19204
  602.8 10.4 %copy-start.18 = (f32[1600]{0:T(1024)S(1)}, f32[1600]{0:T(1024)}, u32[]{:S(2)}) copy-start(f32[1600]{0:T(1024)} %param.46) | copy-start | bytes 19204
  602.8 10.4 %copy-start.21 = (s32[8]{0:T(128)S(1)}, s32[8]{0:T(128)}, u32[]{:S(2)}) copy-start(s32[8]{0:T(128)} %get-tuple-element.207) | copy-start | bytes 100
  628.9 6.7 %copy-start.1 = (bf16[8,16,8,800]{3,2,1,0:T(8,128)(2,1)S(1)}, bf16[8,16,8,800]{3,2,1,0:T(8,128)(2,1)}, u32[]{:S(2)}) copy-start(bf16[8,16,8,800]{3,2,1,0:T(8,128)(2,1)} %param.26) | copy-start | bytes 4915204
  (4 other events, 9.6 us)
Sparse Core Ops, SparseCore 0:
  10.1 71.3 all-gather.12
  84.2 56.0 all-gather.14
  141.8 11.1 all-gather.10
  155.6 134.9 all-gather.16
  293.1 89.7 all-gather.18
  385.1 16.1 all-reduce.2
  403.6 12.2 reduce-scatter.2
  613.1 11.3 reduce-scatter.4
where the time goes:
time: 651 us; the launch traced here: 643 us
  local copies, waits for them, and re-layouts  203 us (31%)
  other arithmetic  182 us (28%)
  blocking collectives  84.4 us (13%)
  waiting for transfers between devices  75.1 us (12%)
  matrix products  72.2 us (11%)
  between operations  14.2 us (2%)
  starting transfers between devices  11.7 us (2%)
    reduce_sum x8, other arithmetic, advance(): jnp.sum(carried * mix_out[:, :, None], axis=1) + skip_gain * value_now  99.4 us
    all_gather x1, blocking collectives, local(): lax.all_gather(w_keyval, ('rep', 'tr'), axis=0, tiled=True)  51.1 us
    all_gather x1, waiting for transfers between devices, local(): lax.all_gather(inner_cols, ('rep', 'tr'), axis=0, tiled=True)  46.8 us
    unnamed x58, local copies, waits for them, and re-layouts  38.4 us
    dynamic_slice x24, local copies, waits for them, and re-layouts, local(): lax.scan(advance, start_state, (token_major(step_size), token_major(conv_...  37.8 us
    all_to_all x1, blocking collectives, local(): lax.all_to_all(jnp.take(tokens, send_order, axis=0), 'rep', split_axis=0,...  28.3 us
    dynamic_slice x32, local copies, waits for them, and re-layouts, local(): lax.map(attend, (query, keyval, cache_heads, lengths))  26.9 us
    dot_general x1, matrix products, local(): inner_run = jnp.dot(normed, pieces[2], preferred_element_type=jnp.float32)  19 us
  transfers between devices with their start and end apart: 11, of which 4 were waited for; matrix products, arithmetic and copies ran while one was open for 69% of the time, Pallas kernels for 0%

commit v1 on v0

v1 whole, which is shorter than its diff:
```python
import functools

import jax
import jax.numpy as jnp
import numpy as np
from jax import lax
from jax.experimental import pallas as pl
from jax.experimental.pallas import tpu as pltpu
from jax.sharding import PartitionSpec as P

D = 1600
HD = 64
QH = 16
KVH = 4

EPSILON = 1e-06
LOG2_E = 1.4426950408889634

X_PAIRS = ((0, 1), (1, 0), (2, 3), (3, 2))
Y_PAIRS = ((0, 2), (2, 0), (1, 3), (3, 1))
D_PAIRS = ((0, 3), (3, 0), (1, 2), (2, 1))
Z_OUTER = ((0, 1), (1, 0), (2, 3), (3, 2))
Z_INNER = ((1, 2), (2, 1))
Z_ENDS = ((1, 0), (2, 3))
Z_FAR = ((2, 0), (1, 3))
Z_SLOTS = ((0, 1, 2, 3), (1, 0, 2, 3), (2, 3, 1, 0), (3, 2, 1, 0))

VMEM_LIMIT = 56 * 1024 * 1024


def params():
    return pltpu.CompilerParams(vmem_limit_bytes=VMEM_LIMIT)


def cost(flops, size):
    return pl.CostEstimate(flops=int(flops), bytes_accessed=int(size), transcendentals=0)


def after(values, earlier):
    count = len(values)
    return lax.optimization_barrier(tuple(values) + tuple(earlier))[:count]


def swap_x(value):
    return lax.ppermute(value, "rep", X_PAIRS)


def swap_y(value):
    return lax.ppermute(value, "rep", Y_PAIRS)


def along_z(value, pairs):
    return lax.ppermute(value, "tr", pairs)


def other_core(value):
    return lax.ppermute(value, "tc", ((0, 1), (1, 0)))


def load_rows(pieces, target, sems, starts):
    copies = []
    for index, (piece, start) in enumerate(zip(pieces, starts)):
        copies.append(
            pltpu.make_async_copy(
                piece, target.at[pl.ds(start, piece.shape[0]), :], sems.at[index]
            )
        )
    for copy in copies:
        copy.start()
    return copies


def row_starts(pieces):
    starts = [0]
    for piece in pieces:
        starts.append(starts[-1] + piece.shape[0])
    return starts[:-1]


def spread_kernel(own, other, x_own, a_own, a_other, b_own, b_other, keep, out_a, out_b, out_x):
    mine = own[...]
    theirs = other[...]

    def both(first, second):
        return jnp.dot(mine, first[...], preferred_element_type=jnp.float32) + jnp.dot(
            theirs, second[...], preferred_element_type=jnp.float32
        )

    out_a[...] = both(a_own, a_other).astype(jnp.bfloat16)
    out_b[...] = both(b_own, b_other).astype(jnp.bfloat16)
    out_x[...] = jnp.dot(x_own[...], keep[...], preferred_element_type=jnp.float32).astype(
        jnp.bfloat16
    )


def attention_kernel(
    slots, kv_here, per_kv, count, lengths, rows, cache, *rest
):
    pieces, (out, weight, sems) = rest[:count], rest[count:]
    group = pl.program_id(0)

    @pl.when(group == 0)
    def _():
        for copy in load_rows(pieces, weight, sems, row_starts(pieces)):
            copy.wait()

    length = lengths[group]
    made = jnp.dot(rows[...], weight[...], preferred_element_type=jnp.float32).astype(jnp.bfloat16)
    total_rows = made.shape[0]
    query_width = kv_here * per_kv * HD
    positions = cache.shape[1]
    stacked = per_kv * total_rows
    row_id = lax.broadcasted_iota(jnp.int32, (stacked, total_rows), 0) % total_rows
    column_id = lax.broadcasted_iota(jnp.int32, (stacked, total_rows), 1)
    own_mask = (row_id % slots == column_id % slots) & (column_id // slots <= row_id // slots)
    prefix_mask = lax.broadcasted_iota(jnp.int32, (stacked, positions), 1) < length
    contract = (((1,), (1,)), ((), ()))
    results = []
    for head in range(kv_here):
        query = jnp.concatenate(
            [
                made[:, (head * per_kv + j) * HD : (head * per_kv + j + 1) * HD]
                for j in range(per_kv)
            ],
            axis=0,
        )
        base = query_width + head * 2 * HD
        key_new = made[:, base : base + HD]
        value_new = made[:, base + HD : base + 2 * HD]
        key_old = cache[0, :, head * 2 * HD : head * 2 * HD + HD]
        value_old = cache[0, :, head * 2 * HD + HD : (head + 1) * 2 * HD]
        scale = HD ** (-0.5)
        old = lax.dot_general(query, key_old, contract, preferred_element_type=jnp.float32) * scale
        new = lax.dot_general(query, key_new, contract, preferred_element_type=jnp.float32) * scale
        old = jnp.where(prefix_mask, old, -jnp.inf)
        new = jnp.where(own_mask, new, -jnp.inf)
        top = jnp.maximum(
            jnp.max(old, axis=1, keepdims=True), jnp.max(new, axis=1, keepdims=True)
        )
        old = jnp.exp(old - top)
        new = jnp.exp(new - top)
        total = jnp.sum(old, axis=1, keepdims=True) + jnp.sum(new, axis=1, keepdims=True)
        value = jnp.dot(
            old.astype(jnp.bfloat16), value_old, preferred_element_type=jnp.float32
        ) + jnp.dot(new.astype(jnp.bfloat16), value_new, preferred_element_type=jnp.float32)
        value = (value / total).astype(jnp.bfloat16)
        for j in range(per_kv):
            results.append(value[j * total_rows : (j + 1) * total_rows])
    out[...] = jnp.concatenate(results, axis=1)


def conv_kernel(slots, count, rows, history, taps, bias, mix_weight, *rest):
    pieces, (out, out_mix, weight, sems) = rest[:count], rest[count:]

    @pl.when(pl.program_id(0) == 0)
    def _():
        for copy in load_rows(pieces, weight, sems, row_starts(pieces)):
            copy.wait()

    made = jnp.dot(rows[...], weight[...], preferred_element_type=jnp.float32)
    steps = made.shape[0] // slots
    tap_count = taps.shape[0]
    past = history.shape[1]
    sequence = [
        jnp.broadcast_to(history[0, index : index + 1, :], (slots, made.shape[1]))
        for index in range(past)
    ] + [made[step * slots : (step + 1) * slots] for step in range(steps)]
    for step in range(steps):
        value = bias[...]
        for tap in range(tap_count):
            value = value + taps[tap : tap + 1, :] * sequence[step + tap]
        out[step * slots : (step + 1) * slots, :] = jax.nn.silu(value).astype(jnp.bfloat16)
    out_mix[...] = jnp.dot(
        out[...], mix_weight[...], preferred_element_type=jnp.float32
    ).astype(jnp.bfloat16)


def scan_kernel(
    slots,
    conv,
    mix_own,
    mix_other,
    step_weight,
    step_bias,
    decay_log,
    skip,
    state,
    out,
    step_scratch,
    drive_scratch,
    out_scratch,
    rate_scratch,
    state_scratch,
    in_scratch,
    out_mix_scratch,
):
    lanes = 128
    rank = step_weight.shape[0]
    states, channels = decay_log.shape
    total_rows = conv.shape[0]
    steps = total_rows // slots
    block = 8
    mix = mix_own[...].astype(jnp.float32) + mix_other[...].astype(jnp.float32)
    raw = (
        jnp.dot(
            mix[:, :rank].astype(jnp.bfloat16), step_weight[...], preferred_element_type=jnp.float32
        )
        + step_bias[...]
    )
    step = jax.nn.softplus(raw)
    value = conv[...].astype(jnp.float32)
    step_scratch[:, :channels] = step
    drive_scratch[:, :channels] = step * value
    rate_scratch[:, :channels] = -jnp.exp(decay_log[...]) * LOG2_E
    state_scratch[:, :channels] = state[0]
    for n in range(states):
        in_scratch[n] = jnp.broadcast_to(mix[:, rank + n : rank + n + 1], (total_rows, lanes))
        out_mix_scratch[n] = jnp.broadcast_to(
            mix[:, rank + states + n : rank + states + n + 1], (total_rows, lanes)
        )
    chunks = step_scratch.shape[1] // lanes

    def one(index, carry):
        chunk = index // (slots // block)
        part = index % (slots // block)
        columns = pl.ds(pl.multiple_of(chunk * lanes, lanes), lanes)
        held = [
            jnp.broadcast_to(state_scratch[n : n + 1, columns], (block, lanes))
            for n in range(states)
        ]
        for t in range(steps):
            where = pl.ds(pl.multiple_of(t * slots + part * block, block), block)
            size = step_scratch[where, columns]
            drive = drive_scratch[where, columns]
            total = None
            for n in range(states):
                rate = jnp.broadcast_to(rate_scratch[n : n + 1, columns], (block, lanes))
                held[n] = jnp.exp2(size * rate) * held[n] + drive * in_scratch[n, where, :]
                term = held[n] * out_mix_scratch[n, where, :]
                total = term if total is None else total + term
            out_scratch[where, columns] = total
        return carry

    lax.fori_loop(0, chunks * (slots // block), one, 0)
    out[...] = out_scratch[:, :channels] + skip[...] * value


def branch_kernel(gate_count, ssm_count, attn_count, half_start, rows, scanned, heads, *rest):
    gate_pieces = rest[:gate_count]
    ssm_pieces = rest[gate_count : gate_count + ssm_count]
    attn_pieces = rest[gate_count + ssm_count : gate_count + ssm_count + attn_count]
    (
        keep_ssm,
        send_ssm,
        keep_attn,
        send_attn,
        gate_weight,
        ssm_weight,
        attn_weight,
        gate_sems,
        ssm_sems,
        attn_sems,
    ) = rest[gate_count + ssm_count + attn_count :]
    width = ssm_weight.shape[0]
    half = width // 2

    def starts(pieces):
        first = half_start[0] * half
        return [
            pl.multiple_of(start + first if start < half else start - first, 16)
            for start in row_starts(pieces)
        ]

    @pl.when(pl.program_id(0) == 0)
    def _():
        copies = load_rows(gate_pieces, gate_weight, gate_sems, row_starts(gate_pieces))
        copies += load_rows(ssm_pieces, ssm_weight, ssm_sems, starts(ssm_pieces))
        copies += load_rows(attn_pieces, attn_weight, attn_sems, starts(attn_pieces))
        for copy in copies:
            copy.wait()

    gate = jnp.dot(rows[...], gate_weight[...], preferred_element_type=jnp.float32)
    gated = (scanned[...] * jax.nn.silu(gate)).astype(jnp.bfloat16)
    attended = heads[...]
    contract = (((1,), (1,)), ((), ()))

    def product(left, right):
        return lax.dot_general(left, right, contract, preferred_element_type=jnp.float32).astype(
            jnp.bfloat16
        )

    send_ssm[...] = product(gated, ssm_weight[half:, :])
    keep_ssm[...] = product(gated, ssm_weight[:half, :])
    send_attn[...] = product(attended, attn_weight[half:, :])
    keep_attn[...] = product(attended, attn_weight[:half, :])


def square_kernel(keep_ssm, got_ssm, keep_attn, got_attn, out):
    ssm = keep_ssm[...].astype(jnp.float32) + got_ssm[...].astype(jnp.float32)
    attn = keep_attn[...].astype(jnp.float32) + got_attn[...].astype(jnp.float32)
    out[:, 0:1] = jnp.sum(attn * attn, axis=1, keepdims=True)
    out[:, 1:2] = jnp.sum(ssm * ssm, axis=1, keepdims=True)


def mixed_kernel(
    slots,
    places,
    sizes,
    x_rows,
    keep_ssm,
    got_ssm,
    keep_attn,
    got_attn,
    squares,
    attn_gain,
    ssm_gain,
    features,
    out,
):
    group = pl.program_id(0)
    ssm = keep_ssm[...].astype(jnp.float32) + got_ssm[...].astype(jnp.float32)
    attn = keep_attn[...].astype(jnp.float32) + got_attn[...].astype(jnp.float32)
    scales = lax.rsqrt(squares[...] / D + EPSILON)
    branch = 0.5 * (
        attn_gain[...] * attn * scales[:, 0:1] + ssm_gain[...] * ssm * scales[:, 1:2]
    )
    mixed = x_rows[...].astype(jnp.float32) + branch
    count = mixed.shape[0]
    slot = lax.broadcasted_iota(jnp.int32, (count, 1), 0) % slots
    mixed = jnp.where(slot < sizes[group], mixed, 0.0).astype(jnp.bfloat16)
    steps = count // slots
    to_row = lax.broadcasted_iota(jnp.int32, (count, count), 0)
    from_row = lax.broadcasted_iota(jnp.int32, (count, count), 1)
    mover = jnp.where(
        from_row == (to_row % steps) * slots + to_row // steps, 1.0, 0.0
    ).astype(jnp.bfloat16)
    placed = jnp.dot(mixed, features[...], preferred_element_type=jnp.float32).astype(jnp.bfloat16)
    out[0] = jnp.dot(mover, placed, preferred_element_type=jnp.float32).astype(jnp.bfloat16)


def local(
    tokens,
    prefix_kv,
    ssm_state,
    conv_state,
    prefix_len,
    group_size,
    serve_replica,
    in_gain,
    w_query,
    w_keyval,
    w_inner,
    conv_weight,
    conv_bias,
    w_xproj,
    dt_weight,
    dt_bias,
    decay_log,
    skip_gain,
    w_attn_out,
    w_ssm_out,
    attn_gain,
    ssm_gain,
):
    rep_count = lax.axis_size("rep")
    row_axis = lax.axis_size("tr")
    tensor_count = lax.axis_size("tc")
    rep = lax.axis_index("rep")
    row = lax.axis_index("tr")
    core = lax.axis_index("tc")
    groups, slots, steps, width = tokens.shape
    pairs = groups // rep_count
    kv_here = KVH // tensor_count
    per_kv = QH // KVH
    heads_width = QH // tensor_count * HD
    group_rows = slots * steps
    rows = groups * group_rows
    channels = w_inner.shape[2]
    shards = rep_count * row_axis
    shard = w_query.shape[0]
    pad = -(-shard // 8) * 8
    depth = shards * pad
    half = depth // 2
    by_links = rep_count == 4 and row_axis == 4
    bf16 = jnp.bfloat16
    f32 = jnp.float32

    def padded(value):
        return jnp.pad(value, ((0, pad - shard), (0, 0)))

    gate_shard = padded(w_inner[:, 1])
    qkv_shard = padded(jnp.concatenate([w_query, w_keyval], axis=1))
    conv_shard = padded(w_inner[:, 0])
    out_shard = padded(jnp.concatenate([w_attn_out.T, w_ssm_out.T], axis=1))

    slot_table = jnp.asarray(Z_SLOTS, jnp.int32)
    block_ids = jnp.arange(shards, dtype=jnp.int32)
    if by_links:
        order = jnp.sum(
            jnp.where(jnp.arange(4)[:, None] == row, slot_table, 0), axis=0
        )
        reps_here = jnp.arange(rep_count, dtype=jnp.int32) ^ rep
        pieces_a = (reps_here[:, None] * row_axis + order[None, :]).reshape(shards)
        pieces_b = (reps_here[None, :] * row_axis + order[:, None]).reshape(shards)
        second = (rep // 2) ^ core
    else:
        pieces_a = block_ids
        pieces_b = block_ids
        second = core

    def sources(pieces):
        offset = jnp.arange(pad, dtype=jnp.int32)
        return jnp.where(offset < shard, pieces[:, None] * shard + offset, -1).reshape(depth)

    source_a = sources(pieces_a)
    source_b = sources(pieces_b)
    keep_source = lax.dynamic_slice_in_dim(source_a, second * half, half, 0)
    own_features = core * width + jnp.arange(width, dtype=jnp.int32)
    other_features = (1 - core) * width + jnp.arange(width, dtype=jnp.int32)

    def pick(features, source):
        return (features[:, None] == source[None, :]).astype(bf16)

    spread_keep = pick(own_features, keep_source)
    features_keep = (keep_source[:, None] == own_features[None, :]).astype(bf16)

    def gain_columns(gain):
        matches = keep_source[:, None] == jnp.arange(gain.shape[0], dtype=jnp.int32)[None, :]
        return jnp.sum(jnp.where(matches, gain[None, :], 0.0), axis=1)[None, :]

    attn_gain_here = gain_columns(attn_gain)
    ssm_gain_here = gain_columns(ssm_gain)

    first_group = (rep * row_axis + row) * groups
    lengths = lax.dynamic_slice_in_dim(prefix_len, first_group, groups, 0)
    sizes = lax.dynamic_slice_in_dim(group_size, first_group, groups, 0)
    served = lax.dynamic_slice_in_dim(serve_replica, first_group, groups, 0)
    target = served ^ rep if by_links else served
    same = (served[:, None] == served[None, :]) & (
        jnp.arange(groups)[None, :] < jnp.arange(groups)[:, None]
    )
    places = (target * pairs + jnp.sum(same.astype(jnp.int32), axis=1)).astype(jnp.int32)

    x_bf = tokens.transpose(0, 2, 1, 3).reshape(rows, width)
    x_rows = x_bf.astype(f32)
    square_sums = lax.psum(jnp.sum(x_rows * x_rows, axis=1), "tc")
    inv_rms = lax.rsqrt(square_sums / D + EPSILON)
    normed_own = (x_rows * inv_rms[:, None] * in_gain[None, :]).astype(bf16)
    normed_other = other_core(normed_own)

    def row_block(columns):
        return pl.BlockSpec((group_rows, columns), lambda g, *_: (g, 0))

    def whole(*shape):
        return pl.BlockSpec(shape, lambda g, *_: (0,) * len(shape))

    anywhere = pl.BlockSpec(memory_space=pl.ANY)

    rows_a, rows_b, x_keep = pl.pallas_call(
        spread_kernel,
        grid=(groups,),
        in_specs=[row_block(width)] * 3 + [whole(width, depth)] * 4 + [whole(width, half)],
        out_specs=[row_block(depth), row_block(depth), row_block(half)],
        out_shape=[
            jax.ShapeDtypeStruct((rows, depth), bf16),
            jax.ShapeDtypeStruct((rows, depth), bf16),
            jax.ShapeDtypeStruct((rows, half), bf16),
        ],
        compiler_params=params(),
        cost_estimate=cost(2 * rows * depth * D * 3, rows * D * 10),
        name="spread_rows",
    )(
        normed_own,
        normed_other,
        x_bf,
        pick(own_features, source_a),
        pick(other_features, source_a),
        pick(own_features, source_b),
        pick(other_features, source_b),
        spread_keep,
    )

    def attention(pieces):
        return pl.pallas_call(
            functools.partial(attention_kernel, slots, kv_here, per_kv, len(pieces)),
            grid_spec=pltpu.PrefetchScalarGridSpec(
                num_scalar_prefetch=1,
                grid=(groups,),
                in_specs=[
                    row_block(depth),
                    pl.BlockSpec((1,) + prefix_kv.shape[1:], lambda g, *_: (g, 0, 0)),
                ]
                + [anywhere] * len(pieces),
                out_specs=row_block(heads_width),
                scratch_shapes=[
                    pltpu.VMEM((depth, pieces[0].shape[1]), bf16),
                    pltpu.SemaphoreType.DMA((len(pieces),)),
                ],
            ),
            out_shape=jax.ShapeDtypeStruct((rows, heads_width), bf16),
            compiler_params=params(),
            cost_estimate=cost(2 * rows * depth * 768 * 4, rows * depth * 2),
            name="attention",
        )(lengths, rows_a, prefix_kv, *pieces)

    def convolve(pieces):
        mixes = w_xproj.shape[1]
        return pl.pallas_call(
            functools.partial(conv_kernel, slots, len(pieces)),
            grid=(groups,),
            in_specs=[
                row_block(depth),
                pl.BlockSpec((1,) + conv_state.shape[1:], lambda g: (g, 0, 0)),
                whole(*conv_weight.shape),
                whole(1, channels),
                whole(*w_xproj.shape),
            ]
            + [anywhere] * len(pieces),
            out_specs=[row_block(channels), row_block(mixes)],
            out_shape=[
                jax.ShapeDtypeStruct((rows, channels), bf16),
                jax.ShapeDtypeStruct((rows, mixes), bf16),
            ],
            scratch_shapes=[
                pltpu.VMEM((depth, channels), bf16),
                pltpu.SemaphoreType.DMA((len(pieces),)),
            ],
            compiler_params=params(),
            cost_estimate=cost(2 * rows * depth * channels * 1.5, rows * depth * 4),
            name="convolve",
        )(rows_a, conv_state, conv_weight, conv_bias[None], w_xproj, *pieces)

    def scan(conv_out, mix_own, mix_other):
        rank, states = dt_weight.shape[0], decay_log.shape[0]
        wide = -(-channels // 128) * 128
        mixes = w_xproj.shape[1]
        return pl.pallas_call(
            functools.partial(scan_kernel, slots),
            grid=(groups,),
            in_specs=[
                row_block(channels),
                row_block(mixes),
                row_block(mixes),
                whole(rank, channels),
                whole(1, channels),
                whole(states, channels),
                whole(1, channels),
                pl.BlockSpec((1,) + ssm_state.shape[1:], lambda g: (g, 0, 0)),
            ],
            out_specs=row_block(channels),
            out_shape=jax.ShapeDtypeStruct((rows, channels), f32),
            scratch_shapes=[
                pltpu.VMEM((group_rows, wide), f32),
                pltpu.VMEM((group_rows, wide), f32),
                pltpu.VMEM((group_rows, wide), f32),
                pltpu.VMEM((states, wide), f32),
                pltpu.VMEM((states, wide), f32),
                pltpu.VMEM((states, group_rows, 128), f32),
                pltpu.VMEM((states, group_rows, 128), f32),
            ],
            compiler_params=params(),
            cost_estimate=cost(30e-6 * 1.1e15, rows * channels * 6),
            name="scan_states",
        )(
            conv_out,
            mix_own,
            mix_other,
            dt_weight,
            dt_bias[None],
            decay_log,
            skip_gain[None],
            ssm_state,
        )

    def branches(scanned, heads, gate_pieces, ssm_pieces, attn_pieces):
        return pl.pallas_call(
            functools.partial(
                branch_kernel, len(gate_pieces), len(ssm_pieces), len(attn_pieces)
            ),
            grid_spec=pltpu.PrefetchScalarGridSpec(
                num_scalar_prefetch=1,
                grid=(groups,),
                in_specs=[row_block(depth), row_block(channels), row_block(heads_width)]
                + [anywhere] * (len(gate_pieces) + len(ssm_pieces) + len(attn_pieces)),
                out_specs=[row_block(half)] * 4,
                scratch_shapes=[
                    pltpu.VMEM((depth, channels), bf16),
                    pltpu.VMEM((depth, channels), bf16),
                    pltpu.VMEM((depth, heads_width), bf16),
                    pltpu.SemaphoreType.DMA((len(gate_pieces),)),
                    pltpu.SemaphoreType.DMA((len(ssm_pieces),)),
                    pltpu.SemaphoreType.DMA((len(attn_pieces),)),
                ],
            ),
            out_shape=[jax.ShapeDtypeStruct((rows, half), bf16)] * 4,
            compiler_params=params(),
            cost_estimate=cost(2 * rows * depth * channels * 2.5, rows * depth * 8),
            name="branches",
        )(second.astype(jnp.int32)[None], rows_b, scanned, heads, *gate_pieces, *ssm_pieces, *attn_pieces)

    if by_links:
        def line_first(value):
            return along_z(value, Z_OUTER), along_z(value, Z_INNER)

        def line_second(near, middle):
            return along_z(near, Z_INNER), along_z(middle, Z_ENDS), along_z(near, Z_FAR)

        inner = (row == 1) | (row == 2)

        def line_slots(value, first, last):
            near, middle = first
            crossed, ends, far = last
            return value, near, jnp.where(inner, middle, ends), jnp.where(inner, crossed, far)

        def plane_first(value):
            return swap_x(value), swap_y(value)

        def plane_second(first):
            by_x, by_y = first
            cut = by_x.shape[0] // 16 * 8
            return swap_y(by_x[:cut]), swap_x(by_y[cut:])

        gate_p1 = plane_first(gate_shard)
        qkv_z1 = line_first(qkv_shard)
        conv_z1 = line_first(conv_shard)

        gate_p1 = after(gate_p1, qkv_z1 + conv_z1)
        gate_p2 = plane_second(gate_p1)
        qkv_z2 = line_second(*after(qkv_z1, gate_p1))

        gate_block = jnp.concatenate((gate_shard,) + tuple(gate_p1) + tuple(gate_p2), axis=0)
        qkv_block = jnp.concatenate(line_slots(qkv_shard, qkv_z1, qkv_z2), axis=0)
        qkv_p1 = plane_first(qkv_block)
        conv_z2 = line_second(*after(conv_z1, (qkv_block,)))

        conv_block = jnp.concatenate(line_slots(conv_shard, conv_z1, conv_z2), axis=0)
        qkv_p1 = after(qkv_p1, (conv_block,))
        qkv_p2 = plane_second(qkv_p1)
        out_z1 = line_first(*after((out_shard,), (conv_block,)))

        (conv_block,) = after((conv_block,), qkv_p2 + out_z1)
        conv_p1 = plane_first(conv_block)
        (gate_block,) = after((gate_block,), (conv_block,))
        gate_z1 = line_first(gate_block)
        heads = attention((qkv_block,) + tuple(qkv_p1) + tuple(qkv_p2))

        conv_p1 = after(conv_p1, gate_z1)
        conv_p2 = plane_second(conv_p1)
        out_z2 = line_second(*after(out_z1, gate_z1))

        out_block = jnp.concatenate(line_slots(out_shard, out_z1, out_z2), axis=0)
        (out_block,) = after((out_block,), conv_p2)
        out_p1 = plane_first(out_block)
        gate_z2 = line_second(*after(gate_z1, (out_block,)))
        conv_out, mix_own = convolve((conv_block,) + tuple(conv_p1) + tuple(conv_p2))
        scanned = scan(conv_out, mix_own, other_core(mix_own))
        out_p2 = plane_second(out_p1)
        out_pieces = (out_block,) + tuple(out_p1) + tuple(out_p2)
        gate_pieces = line_slots(gate_block, gate_z1, gate_z2)
        attn_pieces = [piece[:, :heads_width] for piece in out_pieces]
        ssm_pieces = [piece[:, heads_width:] for piece in out_pieces]
    else:
        def gathered(value):
            return lax.all_gather(value, ("rep", "tr"), axis=0, tiled=True)

        heads = attention((gathered(qkv_shard),))
        conv_out, mix_own = convolve((gathered(conv_shard),))
        scanned = scan(conv_out, mix_own, other_core(mix_own))
        out_all = gathered(out_shard)
        gate_pieces = (gathered(gate_shard),)
        attn_pieces = [out_all[:half, :heads_width], out_all[half:, :heads_width]]
        ssm_pieces = [out_all[:half, heads_width:], out_all[half:, heads_width:]]

    keep_ssm, send_ssm, keep_attn, send_attn = branches(
        scanned, heads, gate_pieces, ssm_pieces, attn_pieces
    )
    got_ssm = other_core(send_ssm)
    got_attn = other_core(send_attn)
    squares = pl.pallas_call(
        square_kernel,
        grid=(groups,),
        in_specs=[row_block(half)] * 4,
        out_specs=row_block(2),
        out_shape=jax.ShapeDtypeStruct((rows, 2), f32),
        compiler_params=params(),
        cost_estimate=cost(rows * half * 8, rows * half * 8),
        name="squares",
    )(keep_ssm, got_ssm, keep_attn, got_attn)
    squares = squares + other_core(squares)
    mixed = pl.pallas_call(
        functools.partial(mixed_kernel, slots),
        grid_spec=pltpu.PrefetchScalarGridSpec(
            num_scalar_prefetch=2,
            grid=(groups,),
            in_specs=[row_block(half)] * 5
            + [row_block(2), whole(1, half), whole(1, half), whole(half, width)],
            out_specs=pl.BlockSpec(
                (1, group_rows, width), lambda g, places, sizes: (places[g], 0, 0)
            ),
        ),
        out_shape=jax.ShapeDtypeStruct((groups, group_rows, width), bf16),
        compiler_params=params(),
        cost_estimate=cost(2 * rows * half * width, rows * half * 12),
        name="mixed_rows",
    )(
        places,
        sizes,
        x_keep,
        keep_ssm,
        got_ssm,
        keep_attn,
        got_attn,
        squares,
        attn_gain_here,
        ssm_gain_here,
        features_keep,
    )
    if by_links:
        parts = mixed.reshape(rep_count, pairs, group_rows, width)
        received = jnp.stack(
            [
                parts[0],
                swap_x(parts[1]),
                swap_y(parts[2]),
                lax.ppermute(parts[3], "rep", D_PAIRS),
            ]
        )
        mixed = jnp.take(received, jnp.arange(rep_count, dtype=jnp.int32) ^ rep, axis=0)
    else:
        mixed = lax.all_to_all(mixed, "rep", split_axis=0, concat_axis=0, tiled=True)
    return mixed.reshape(groups, slots, steps, width)


def solution(mesh):
    placed = (
        P(("rep", "tr"), None, None, "tc"),
        P(("rep", "tr"), None, "tc"),
        P(("rep", "tr"), None, "tc"),
        P(("rep", "tr"), None, "tc"),
        P(),
        P(),
        P(),
        P("tc"),
        P(("rep", "tr"), "tc"),
        P(("rep", "tr"), "tc"),
        P(("rep", "tr"), None, "tc"),
        P(None, "tc"),
        P("tc"),
        P("tc", None),
        P(None, "tc"),
        P("tc"),
        P(None, "tc"),
        P("tc"),
        P("tc", ("rep", "tr")),
        P("tc", ("rep", "tr")),
        P(),
        P(),
    )
    return jax.shard_map(
        local,
        mesh=mesh,
        in_specs=placed,
        out_specs=P(("rep", "tr"), None, None, "tc"),
        check_vma=False,
    )
```

time: 651 us -> 383 us (0.59)
  other arithmetic: 182 us -> 28.7 us
  local copies, waits for them, and re-layouts: 203 us -> 51.5 us
  Pallas kernels: 0 us -> 150 us
  blocking collectives: 84.4 us -> 2.46 us
  matrix products: 72.2 us -> 0 us
  starting transfers between devices: 11.7 us -> 51.2 us
  waiting for transfers between devices: 75.1 us -> 96 us
  between operations: 14.2 us -> 0.65 us
    pallas_call x0 -> x7, Pallas kernels: none -> 150 us  [the longest x1 42 us: scan(): pl.pallas_call(functools.partial(scan_kernel, slots), grid=(groups,), in_...]
    reduce_sum x27 -> x3, other arithmetic: 109 us -> 2.87 us  [the longest x1 2.6 us: gain_columns(): return jnp.sum(jnp.where(matches, gain[None, :], 0.0), axis=1)[None, :]]
    ppermute x0 -> x44, waiting for transfers between devices: none -> 96 us  [the longest x20 63.6 us: along_z(): return lax.ppermute(value, 'tr', pairs)]
    dot_general x39 -> x0, matrix products: 72.2 us -> none  [the longest x1 19 us: local(): inner_run = jnp.dot(normed, pieces[2], preferred_element_type=jnp.float32)]
    all_gather x5 -> x0, waiting for transfers between devices: 69.2 us -> none  [the longest x1 46.8 us: local(): lax.all_gather(inner_cols, ('rep', 'tr'), axis=0, tiled=True)]
    dynamic_slice x60 -> x4, local copies, waits for them, and re-layouts: 65 us -> 2.06 us  [the longest x1 0.73 us: local(): served = lax.dynamic_slice_in_dim(serve_replica, first_group, groups, 0)]
    ppermute x0 -> x44, starting transfers between devices: none -> 51.2 us  [the longest x20 30.2 us: along_z(): return lax.ppermute(value, 'tr', pairs)]
    all_gather x1 -> x0, blocking collectives: 51.1 us -> none  [local(): lax.all_gather(w_keyval, ('rep', 'tr'), axis=0, tiled=True)]
  transfers between devices with their start and end apart: 11 -> 44, of which waited for: 4 -> 11; matrix products, arithmetic and copies ran while one was open for 69% -> 15% of each run, Pallas kernels for 0% -> 22%
where the time goes in v1:
time: 383 us; the launch traced here: 381 us
  Pallas kernels  150 us (39%)
  waiting for transfers between devices  96 us (25%)
  local copies, waits for them, and re-layouts  51.5 us (13%)
  starting transfers between devices  51.2 us (13%)
  other arithmetic  28.7 us (7%)
    ppermute x20, waiting for transfers between devices, along_z(): return lax.ppermute(value, 'tr', pairs)  63.6 us
    pallas_call x1, Pallas kernels, scan(): pl.pallas_call(functools.partial(scan_kernel, slots), grid=(groups,), in_...  42 us
    pallas_call x1, Pallas kernels, branches(): pl.pallas_call(functools.partial(branch_kernel, len(gate_pieces), len(ssm...  32.9 us
    ppermute x20, starting transfers between devices, along_z(): return lax.ppermute(value, 'tr', pairs)  30.2 us
    pallas_call x1, Pallas kernels, local(): pl.pallas_call(spread_kernel, grid=(groups,), in_specs=[row_block(width)]...  24.5 us
    ppermute x9, waiting for transfers between devices, swap_y(): return lax.ppermute(value, 'rep', Y_PAIRS)  20.9 us
    pallas_call x1, Pallas kernels, attention(): pl.pallas_call(functools.partial(attention_kernel, slots, kv_here, per_kv...  17.2 us
    pallas_call x1, Pallas kernels, convolve(): pl.pallas_call(functools.partial(conv_kernel, slots, len(pieces)), grid=(...  15.1 us
  transfers between devices with their start and end apart: 44, of which 11 were waited for; matrix products, arithmetic and copies ran while one was open for 15% of the time, Pallas kernels for 22%

profile of v1, /device:TPU:0, one launch (start us, length us, event | category | flops | bytes accessed | tf_op | source)
XLA Modules:
  0.0 380.8 jit_solution(1385812273475979422)
XLA Ops:
  0.0 2.4 fusion.9
  2.6 3.1 collective-permute-start.1
  11.0 3.7 collective-permute-start.3
  15.4 2.5 psum.7
  19.5 5.1 %compare_convert_fusion.2 = (bf16[800,1664]{1,0:T(8,128)(2,1)}, bf16[800,1664]{1,0:T(8,128)(2,1)}, bf16[800,1664]{1,0:T(8,128)(2,1)}, bf16[800,1664]{1,0:T(8,128)(2,1)}) fusion(s32[1664]{0:T(1024)S(1)} %select_n.119, s32[800]{0:T(1024)S(1)} %iota_add_fusion, s32[800]{0:T(1024)S(1)} %iota_add_fusion.1, s32[1664]{0:T(1024)S(1)} %select_n.121), kind=kLoop, calls=%fused_computation.6 | loop fusion | flops 10649600 | bytes 10669312 | tf_op jit(solution)/shard_map/convert_element_type | solution.py:422
  28.1 2.9 copy.58
  41.5 3.7 collective-permute-done.7
  45.2 8.0 %collective-permute-done.9 = bf16[104,768]{1,0:T(8,128)(2,1)S(1)} collective-permute-done((bf16[104,768]{1,0:T(8,128)(2,1)}, bf16[104,768]{1,0:T(8,128)(2,1)S(1)}, u32[]{:S(2)}, u32[]{:S(2)}) %collective-permute-start.9) | collective-permute-done | bytes 159776 | tf_op jit(solution)/shard_map/ppermute | solution.py:53
  58.8 6.7 %collective-permute-done.10 = bf16[104,1600]{1,0:T(8,128)(2,1)S(1)} collective-permute-done((bf16[104,1600]{1,0:T(8,128)(2,1)}, bf16[104,1600]{1,0:T(8,128)(2,1)S(1)}, u32[]{:S(2)}, u32[]{:S(2)}) %collective-permute-start.10) | collective-permute-done | bytes 332832 | tf_op jit(solution)/shard_map/ppermute | solution.py:53
  67.5 10.7 %collective-permute-done.12 = bf16[104,1600]{1,0:T(8,128)(2,1)S(1)} collective-permute-done((bf16[104,1600]{1,0:T(8,128)(2,1)}, bf16[104,1600]{1,0:T(8,128)(2,1)S(1)}, u32[]{:S(2)}, u32[]{:S(2)}) %collective-permute-start.12) | collective-permute-done | bytes 332832 | tf_op jit(solution)/shard_map/ppermute | solution.py:53
  82.0 3.3 collective-permute-start.17
  85.3 7.9 %collective-permute-done.14.rest_2_ = bf16[416,768]{1,0:T(8,128)(2,1)S(1)} collective-permute-done((bf16[416,768]{1,0:T(8,128)(2,1)S(1)}, bf16[416,768]{1,0:T(8,128)(2,1)S(1)}, u32[]{:S(2)}, u32[]{:S(2)}) %collective-permute-start.14) | collective-permute-done | bytes 639008 | tf_op jit(solution)/shard_map/ppermute | solution.py:49
  97.1 4.2 %collective-permute-done.15.rest_3_ = bf16[208,768]{1,0:T(8,128)(2,1)S(1)} collective-permute-done((bf16[208,768]{1,0:T(8,128)(2,1)S(1)}, bf16[208,768]{1,0:T(8,128)(2,1)S(1)}, u32[]{:S(2)}, u32[]{:S(2)}) %collective-permute-start.15) | collective-permute-done | bytes 319520 | tf_op jit(solution)/shard_map/ppermute | solution.py:49
  108.0 3.7 copy.59.other
  111.6 24.5 %spread_rows.1 = (bf16[1024,1664]{1,0:T(8,128)(2,1)}, bf16[1024,1664]{1,0:T(8,128)(2,1)}, bf16[1024,832]{1,0:T(8,128)(2,1)}) custom-call(bf16[1024,800]{1,0:T(8,128)(2,1)} %multiply_convert_fusion.own, bf16[1024,800]{1,0:T(8,128)(2,1)} %copy.59.other, bf16[1024,800]{1,0:T(8,128)(2,1)} %bitcast.21, bf16[800,1664]{1,0:T(8,128)(2,1)} %get-tuple-element.72.a_own, ...), custom_call_target="tpu_custom_call" | custom-call | flops 16357785600 | bytes 16384000 | tf_op jit(solution)/shard_map/spread_rows/pallas_call | solution.py:459
  137.7 17.2 %attention.1.heads = bf16[1024,512]{1,0:T(8,128)(2,1)} custom-call(s32[8]{0:T(128)} %dynamic_slice.15.lengths, bf16[1024,1664]{1,0:T(8,128)(2,1)} %get-tuple-element.34.rows, bf16[8,256,256]{2,1,0:T(8,128)(2,1)} %cache.1, bf16[416,768]{1,0:T(8,128)(2,1)} %copy-done.4, bf16[416,768]{1,0:T(8,128)(2,1)} %copy-done.7, bf16[416,768]{1,0:T(8,128)(2,1)} %copy-done.8, ...), custom_call_target="tpu_custom_call" | custom-call | flops 10468982784 | bytes 3407872 | tf_op jit(solution)/shard_map/attention/pallas_call | solution.py:484
  161.3 14.4 %collective-permute-done.30 = bf16[104,2112]{1,0:T(8,128)(2,1)S(1)} collective-permute-done((bf16[104,2112]{1,0:T(8,128)(2,1)S(1)}, bf16[104,2112]{1,0:T(8,128)(2,1)S(1)}, u32[]{:S(2)}, u32[]{:S(2)}) %collective-permute-start.30) | collective-permute-done | bytes 439328 | tf_op jit(solution)/shard_map/ppermute | solution.py:53
  177.4 15.1 %convolve.1 = (bf16[1024,1600]{1,0:T(8,128)(2,1)}, bf16[1024,132]{1,0:T(8,128)(2,1)}) custom-call(bf16[1024,1664]{1,0:T(8,128)(2,1)} %get-tuple-element.34.rows, f32[8,3,1600]{2,1,0:T(4,128)} %copy.62.history, f32[4,1600]{1,0:T(4,128)} %taps.1, f32[1,1600]{1,0:T(1,128)} %broadcast_in_dim.109.bias, bf16[1600,132]{1,0:T(8,128)(2,1)} %copy.63.mix_weight, ...), custom_call_target="tpu_custom_call" | custom-call | flops 8178892800 | bytes 6815744 | tf_op jit(solution)/shard_map/convolve/pallas_call | solution.py:508
  200.9 42.0 %scan_states.1.scanned = f32[1024,1600]{1,0:T(8,128)} custom-call(bf16[1024,1600]{1,0:T(8,128)(2,1)} %get-tuple-element.48.conv, bf16[1024,132]{1,0:T(8,128)(2,1)} %get-tuple-element.49.mix_own, bf16[1024,132]{1,0:T(8,128)(2,1)} %collective-permute-done.27.mix_other, bf16[100,1600]{1,0:T(8,128)(2,1)} %step_weight.1, f32[1,1600]{1,0:T(1,128)} %broadcast_in_dim.110.step_bias, ...), custom_call_target="tpu_custom_call" | custom-call | flops 32999999488 | bytes 9830400 | tf_op jit(solution)/shard_map/scan_states/pallas_call | solution.py:537
  244.5 20.2 %collective-permute-done.31 = bf16[416,1600]{1,0:T(8,128)(2,1)} collective-permute-done((bf16[416,1600]{1,0:T(8,128)(2,1)}, bf16[416,1600]{1,0:T(8,128)(2,1)}, u32[]{:S(2)}, u32[]{:S(2)}) %collective-permute-start.31) | collective-permute-done | bytes 1331232 | tf_op jit(solution)/shard_map/ppermute | solution.py:53
  264.6 2.6 broadcast_select_fusion.2.rest_2_
  275.8 32.9 %branches.1 = (bf16[1024,832]{1,0:T(8,128)(2,1)}, bf16[1024,832]{1,0:T(8,128)(2,1)}, bf16[1024,832]{1,0:T(8,128)(2,1)}, bf16[1024,832]{1,0:T(8,128)(2,1)}) custom-call(s32[1]{0:T(128)} %bitcast.2.half_start, bf16[1024,1664]{1,0:T(8,128)(2,1)} %get-tuple-element.33.rows, f32[1024,1600]{1,0:T(8,128)} %scan_states.1.scanned, bf16[1024,512]{1,0:T(8,128)(2,1)} %attention.1.heads, ...), custom_call_target="tpu_custom_call" | custom-call | flops 13631488000 | bytes 13631488 | tf_op jit(solution)/shard_map/branches/pallas_call | solution.py:576
  308.8 3.0 copy.64
  311.8 2.5 copy.65
  317.1 2.6 select_reduce_fusion
  319.8 3.8 copy.68.got_ssm
  323.5 2.5 copy.69.got_attn
  326.0 7.2 %squares.1 = f32[1024,2]{1,0:T(8,128)} custom-call(bf16[1024,832]{1,0:T(8,128)(2,1)} %get-tuple-element.55.keep_ssm, bf16[1024,832]{1,0:T(8,128)(2,1)} %copy.68.got_ssm, bf16[1024,832]{1,0:T(8,128)(2,1)} %get-tuple-element.57.keep_attn, bf16[1024,832]{1,0:T(8,128)(2,1)} %copy.69.got_attn), custom_call_target="tpu_custom_call" | custom-call | flops 6815744 | bytes 6815744 | tf_op jit(solution)/shard_map/squares/pallas_call | solution.py:679
  337.6 11.4 %mixed_rows.1 = bf16[8,128,800]{2,1,0:T(8,128)(2,1)} custom-call(s32[8]{0:T(128)} %multiply_add_fusion.places, s32[8]{0:T(128)} %dynamic_slice.13.sizes, bf16[1024,832]{1,0:T(8,128)(2,1)} %get-tuple-element.32.x_rows, bf16[1024,832]{1,0:T(8,128)(2,1)} %get-tuple-element.55.keep_ssm, bf16[1024,832]{1,0:T(8,128)(2,1)} %copy.68.got_ssm, ...), custom_call_target="tpu_custom_call" | custom-call | flops 1363148800 | bytes 10223616 | tf_op jit(solution)/shard_map/mixed_rows/pallas_call | solution.py:690
  354.3 10.6 %collective-permute-done.43 = bf16[2,128,800]{2,1,0:T(8,128)(2,1)S(1)} collective-permute-done((bf16[2,128,800]{2,1,0:T(8,128)(2,1)S(1)}, bf16[2,128,800]{2,1,0:T(8,128)(2,1)S(1)}, u32[]{:S(2)}, u32[]{:S(2)}) %collective-permute-start.43) | collective-permute-done | bytes 409632 | tf_op jit(solution)/shard_map/ppermute | solution.py:725
  364.9 8.8 %collective-permute-done.42 = bf16[2,128,800]{2,1,0:T(8,128)(2,1)S(1)} collective-permute-done((bf16[2,128,800]{2,1,0:T(8,128)(2,1)S(1)}, bf16[2,128,800]{2,1,0:T(8,128)(2,1)S(1)}, u32[]{:S(2)}, u32[]{:S(2)}) %collective-permute-start.42) | collective-permute-done | bytes 409632 | tf_op jit(solution)/shard_map/ppermute | solution.py:49
  377.9 3.0 broadcast_select_fusion
  (203 shorter events, 88.2 us)
Async XLA Ops:
  2.6 34.1 %collective-permute-start.1 = (bf16[104,1600]{1,0:T(8,128)(2,1)S(1)}, bf16[104,1600]{1,0:T(8,128)(2,1)}, u32[]{:S(2)}, u32[]{:S(2)}) collective-permute-start(bf16[104,1600]{1,0:T(8,128)(2,1)S(1)} %pad.15), channel_id=1, source_target_pairs={{0,2},{2,0},{4,6},{6,4},{1,3},{3,1},{5,7},{7,5},{8,10},{10,8},{12,... | collective-permute-start | bytes 998408 | tf_op jit(solution)/shard_map/ppermute | solution.py:53
  5.7 31.1 %collective-permute-start.2 = (bf16[104,1600]{1,0:T(8,128)(2,1)S(1)}, bf16[104,1600]{1,0:T(8,128)(2,1)}, u32[]{:S(2)}, u32[]{:S(2)}) collective-permute-start(bf16[104,1600]{1,0:T(8,128)(2,1)S(1)} %pad.15), channel_id=1, source_target_pairs={{2,4},{4,2},{3,5},{5,3},{10,12},{12,10},{11,13},{13,11},{18,20},{2... | collective-permute-start | bytes 998408 | tf_op jit(solution)/shard_map/ppermute | solution.py:53
  8.0 28.7 %collective-permute-start.5 = (bf16[104,1600]{1,0:T(8,128)(2,1)}, bf16[104,1600]{1,0:T(8,128)(2,1)S(1)}, u32[]{:S(2)}, u32[]{:S(2)}) collective-permute-start(bf16[104,1600]{1,0:T(8,128)(2,1)} %get-tuple-element.68), channel_id=1, source_target_pairs={{0,8},{8,0},{16,24},{24,16},{1,9},{9,1},{17,25},{25,17},{2,10},{10... | collective-permute-start | bytes 998408 | tf_op jit(solution)/shard_map/ppermute | solution.py:45
  9.5 27.2 %collective-permute-start.6 = (bf16[104,1600]{1,0:T(8,128)(2,1)}, bf16[104,1600]{1,0:T(8,128)(2,1)S(1)}, u32[]{:S(2)}, u32[]{:S(2)}) collective-permute-start(bf16[104,1600]{1,0:T(8,128)(2,1)} %get-tuple-element.68), channel_id=1, source_target_pairs={{0,16},{16,0},{8,24},{24,8},{1,17},{17,1},{9,25},{25,9},{2,18},{18... | collective-permute-start | bytes 998408 | tf_op jit(solution)/shard_map/ppermute | solution.py:49
  11.0 13.9 %collective-permute-start.3 = (bf16[104,768]{1,0:T(8,128)(2,1)S(1)}, bf16[104,768]{1,0:T(8,128)(2,1)}, u32[]{:S(2)}, u32[]{:S(2)}) collective-permute-start(bf16[104,768]{1,0:T(8,128)(2,1)S(1)} %fusion.5), channel_id=1, source_target_pairs={{0,2},{2,0},{4,6},{6,4},{1,3},{3,1},{5,7},{7,5},{8,10},{10,8},{12,... | collective-permute-start | bytes 479240 | tf_op jit(solution)/shard_map/ppermute | solution.py:53
  25.0 11.6 %collective-permute-start.4 = (bf16[104,768]{1,0:T(8,128)(2,1)S(1)}, bf16[104,768]{1,0:T(8,128)(2,1)}, u32[]{:S(2)}, u32[]{:S(2)}) collective-permute-start(bf16[104,768]{1,0:T(8,128)(2,1)S(1)} %fusion.5), channel_id=1, source_target_pairs={{2,4},{4,2},{3,5},{5,3},{10,12},{12,10},{11,13},{13,11},{18,20},{2... | collective-permute-start | bytes 479240 | tf_op jit(solution)/shard_map/ppermute | solution.py:53
  36.5 71.4 %collective-permute-start = (bf16[1024,800]{0,1:T(8,128)(2,1)S(1)}, bf16[1024,800]{0,1:T(8,128)(2,1)}, u32[]{:S(2)}, u32[]{:S(2)}) collective-permute-start(bf16[1024,800]{0,1:T(8,128)(2,1)S(1)} %copy.58), channel_id=1, source_target_pairs={{0,1},{1,0},{2,3},{3,2},{4,5},{5,4},{6,7},{7,6},{8,9},{9,8},{10,11... | collective-permute-start | bytes 4915208 | tf_op jit(solution)/shard_map/ppermute | solution.py:57
  40.2 13.0 %collective-permute-start.9 = (bf16[104,768]{1,0:T(8,128)(2,1)}, bf16[104,768]{1,0:T(8,128)(2,1)S(1)}, u32[]{:S(2)}, u32[]{:S(2)}) collective-permute-start(bf16[104,768]{1,0:T(8,128)(2,1)} %collective-permute-done.3), channel_id=1, source_target_pairs={{4,0},{2,6},{5,1},{3,7},{12,8},{10,14},{13,9},{11,15},{20,16},{18,... | collective-permute-start | bytes 479240 | tf_op jit(solution)/shard_map/ppermute | solution.py:53
  56.3 37.6 %collective-permute-start.21 = (bf16[48,1600]{1,0:T(8,128)(2,1)S(1)}, bf16[48,1600]{1,0:T(8,128)(2,1)S(1)}, u32[]{:S(2)}, u32[]{:S(2)}) collective-permute-start(bf16[48,1600]{1,0:T(8,128)(2,1)S(1)} %slice.82), channel_id=1, source_target_pairs={{0,16},{16,0},{8,24},{24,8},{1,17},{17,1},{9,25},{25,9},{2,18},{18... | collective-permute-start | bytes 460808 | tf_op jit(solution)/shard_map/ppermute | solution.py:49
  56.9 37.8 %collective-permute-start.22 = (bf16[56,1600]{1,0:T(8,128)(2,1)S(1)}, bf16[56,1600]{1,0:T(8,128)(2,1)S(1)}, u32[]{:S(2)}, u32[]{:S(2)}) collective-permute-start(bf16[56,1600]{1,0:T(8,128)(2,1)S(1)} %slice.83), channel_id=1, source_target_pairs={{0,8},{8,0},{16,24},{24,16},{1,9},{9,1},{17,25},{25,17},{2,10},{10... | collective-permute-start | bytes 537608 | tf_op jit(solution)/shard_map/ppermute | solution.py:45
  65.5 12.6 %collective-permute-start.12 = (bf16[104,1600]{1,0:T(8,128)(2,1)}, bf16[104,1600]{1,0:T(8,128)(2,1)S(1)}, u32[]{:S(2)}, u32[]{:S(2)}) collective-permute-start(bf16[104,1600]{1,0:T(8,128)(2,1)} %collective-permute-done.1), channel_id=1, source_target_pairs={{4,0},{2,6},{5,1},{3,7},{12,8},{10,14},{13,9},{11,15},{20,16},{18,... | collective-permute-start | bytes 998408 | tf_op jit(solution)/shard_map/ppermute | solution.py:53
  66.9 15.1 %collective-permute-start.13 = (bf16[416,768]{1,0:T(8,128)(2,1)S(1)}, bf16[416,768]{1,0:T(8,128)(2,1)S(1)}, u32[]{:S(2)}, u32[]{:S(2)}) collective-permute-start(bf16[416,768]{1,0:T(8,128)(2,1)S(1)} %pad_maximum_fusion.3.rest_0_), channel_id=1, source_target_pairs={{0,8},{8,0},{16,24},{24,16},{1,9},{9,1},{17,25},{25,17},{2,10},{10... | collective-permute-start | bytes 1916936 | tf_op jit(solution)/shard_map/ppermute | solution.py:45
  78.2 15.0 %collective-permute-start.14 = (bf16[416,768]{1,0:T(8,128)(2,1)S(1)}, bf16[416,768]{1,0:T(8,128)(2,1)S(1)}, u32[]{:S(2)}, u32[]{:S(2)}) collective-permute-start(bf16[416,768]{1,0:T(8,128)(2,1)S(1)} %pad_maximum_fusion.3.rest_0_), channel_id=1, source_target_pairs={{0,16},{16,0},{8,24},{24,8},{1,17},{17,1},{9,25},{25,9},{2,18},{18... | collective-permute-start | bytes 1916936 | tf_op jit(solution)/shard_map/ppermute | solution.py:49
  82.0 15.1 %collective-permute-start.17 = (bf16[104,2112]{1,0:T(8,128)(2,1)S(1)}, bf16[104,2112]{1,0:T(8,128)(2,1)S(1)}, u32[]{:S(2)}, u32[]{:S(2)}) collective-permute-start(bf16[104,2112]{1,0:T(8,128)(2,1)S(1)} %fusion.2), channel_id=1, source_target_pairs={{0,2},{2,0},{4,6},{6,4},{1,3},{3,1},{5,7},{7,5},{8,10},{10,8},{12,... | collective-permute-start | bytes 1317896 | tf_op jit(solution)/shard_map/ppermute | solution.py:53
  102.2 54.7 %collective-permute-start.19 = (bf16[416,1600]{1,0:T(8,128)(2,1)}, bf16[416,1600]{1,0:T(8,128)(2,1)}, u32[]{:S(2)}, u32[]{:S(2)}) collective-permute-start(bf16[416,1600]{1,0:T(8,128)(2,1)} %pad_maximum_fusion.2.rest_0_), channel_id=1, source_target_pairs={{0,8},{8,0},{16,24},{24,16},{1,9},{9,1},{17,25},{25,17},{2,10},{10... | collective-permute-start | bytes 3993608 | tf_op jit(solution)/shard_map/ppermute | solution.py:45
  104.2 52.7 %collective-permute-start.20 = (bf16[416,1600]{1,0:T(8,128)(2,1)}, bf16[416,1600]{1,0:T(8,128)(2,1)}, u32[]{:S(2)}, u32[]{:S(2)}) collective-permute-start(bf16[416,1600]{1,0:T(8,128)(2,1)} %pad_maximum_fusion.2.rest_0_), channel_id=1, source_target_pairs={{0,16},{16,0},{8,24},{24,8},{1,17},{17,1},{9,25},{25,9},{2,18},{18... | collective-permute-start | bytes 3993608 | tf_op jit(solution)/shard_map/ppermute | solution.py:49
  104.5 31.6 %collective-permute-start.23 = (bf16[416,1600]{1,0:T(8,128)(2,1)}, bf16[416,1600]{1,0:T(8,128)(2,1)}, u32[]{:S(2)}, u32[]{:S(2)}) collective-permute-start(bf16[416,1600]{1,0:T(8,128)(2,1)} %constant_dynamic-update-slice_fusion.rest_0_), channel_id=1, source_target_pairs={{0,2},{2,0},{4,6},{6,4},{1,3},{3,1},{5,7},{7,5},{8,10},{10,8},{12,... | collective-permute-start | bytes 3993608 | tf_op jit(solution)/shard_map/ppermute | solution.py:53
  106.2 30.0 %collective-permute-start.24 = (bf16[416,1600]{1,0:T(8,128)(2,1)}, bf16[416,1600]{1,0:T(8,128)(2,1)}, u32[]{:S(2)}, u32[]{:S(2)}) collective-permute-start(bf16[416,1600]{1,0:T(8,128)(2,1)} %constant_dynamic-update-slice_fusion.rest_0_), channel_id=1, source_target_pairs={{2,4},{4,2},{3,5},{5,3},{10,12},{12,10},{11,13},{13,11},{18,20},{2... | collective-permute-start | bytes 3993608 | tf_op jit(solution)/shard_map/ppermute | solution.py:53
  136.2 25.0 %collective-permute-start.28 = (bf16[104,2112]{1,0:T(8,128)(2,1)S(1)}, bf16[104,2112]{1,0:T(8,128)(2,1)S(1)}, u32[]{:S(2)}, u32[]{:S(2)}) collective-permute-start(bf16[104,2112]{1,0:T(8,128)(2,1)S(1)} %collective-permute-done.18), channel_id=1, source_target_pairs={{2,0},{4,6},{3,1},{5,7},{10,8},{12,14},{11,9},{13,15},{18,16},{20,... | collective-permute-start | bytes 1317896 | tf_op jit(solution)/shard_map/ppermute | solution.py:53
  155.6 20.1 %collective-permute-start.30 = (bf16[104,2112]{1,0:T(8,128)(2,1)S(1)}, bf16[104,2112]{1,0:T(8,128)(2,1)S(1)}, u32[]{:S(2)}, u32[]{:S(2)}) collective-permute-start(bf16[104,2112]{1,0:T(8,128)(2,1)S(1)} %collective-permute-done.17), channel_id=1, source_target_pairs={{4,0},{2,6},{5,1},{3,7},{12,8},{10,14},{13,9},{11,15},{20,16},{18,... | collective-permute-start | bytes 1317896 | tf_op jit(solution)/shard_map/ppermute | solution.py:53
  158.0 17.7 %collective-permute-start.25 = (bf16[208,1600]{1,0:T(8,128)(2,1)S(1)}, bf16[208,1600]{1,0:T(8,128)(2,1)S(1)}, u32[]{:S(2)}, u32[]{:S(2)}) collective-permute-start(bf16[208,1600]{1,0:T(8,128)(2,1)S(1)} %slice.84), channel_id=1, source_target_pairs={{0,16},{16,0},{8,24},{24,8},{1,17},{17,1},{9,25},{25,9},{2,18},{18... | collective-permute-start | bytes 1996808 | tf_op jit(solution)/shard_map/ppermute | solution.py:49
  159.6 16.1 %collective-permute-start.26 = (bf16[208,1600]{1,0:T(8,128)(2,1)S(1)}, bf16[208,1600]{1,0:T(8,128)(2,1)S(1)}, u32[]{:S(2)}, u32[]{:S(2)}) collective-permute-start(bf16[208,1600]{1,0:T(8,128)(2,1)S(1)} %slice.85), channel_id=1, source_target_pairs={{0,8},{8,0},{16,24},{24,16},{1,9},{9,1},{17,25},{25,17},{2,10},{10... | collective-permute-start | bytes 1996808 | tf_op jit(solution)/shard_map/ppermute | solution.py:45
  192.8 74.5 %collective-permute-start.32 = (bf16[416,1600]{1,0:T(8,128)(2,1)}, bf16[416,1600]{1,0:T(8,128)(2,1)S(1)}, u32[]{:S(2)}, u32[]{:S(2)}) collective-permute-start(bf16[416,1600]{1,0:T(8,128)(2,1)} %collective-permute-done.23.rest_1_), channel_id=1, source_target_pairs={{2,4},{4,2},{3,5},{5,3},{10,12},{12,10},{11,13},{13,11},{18,20},{2... | collective-permute-start | bytes 3993608 | tf_op jit(solution)/shard_map/ppermute | solution.py:53
  193.5 73.7 %collective-permute-start.33 = (bf16[416,1600]{1,0:T(8,128)(2,1)}, bf16[416,1600]{1,0:T(8,128)(2,1)S(1)}, u32[]{:S(2)}, u32[]{:S(2)}) collective-permute-start(bf16[416,1600]{1,0:T(8,128)(2,1)} %collective-permute-done.23.rest_1_), channel_id=1, source_target_pairs={{4,0},{2,6},{5,1},{3,7},{12,8},{10,14},{13,9},{11,15},{20,16},{18,... | collective-permute-start | bytes 3993608 | tf_op jit(solution)/shard_map/ppermute | solution.py:53
  196.0 46.9 %collective-permute-start.34 = (bf16[416,2112]{1,0:T(8,128)(2,1)S(1)}, bf16[416,2112]{1,0:T(8,128)(2,1)S(1)}, u32[]{:S(2)}, u32[]{:S(2)}) collective-permute-start(bf16[416,2112]{1,0:T(8,128)(2,1)S(1)} %pad_maximum_fusion.1), channel_id=1, source_target_pairs={{0,8},{8,0},{16,24},{24,16},{1,9},{9,1},{17,25},{25,17},{2,10},{10... | collective-permute-start | bytes 5271560 | tf_op jit(solution)/shard_map/ppermute | solution.py:45
  197.2 46.3 %collective-permute-start.35 = (bf16[416,2112]{1,0:T(8,128)(2,1)S(1)}, bf16[416,2112]{1,0:T(8,128)(2,1)S(1)}, u32[]{:S(2)}, u32[]{:S(2)}) collective-permute-start(bf16[416,2112]{1,0:T(8,128)(2,1)S(1)} %pad_maximum_fusion.1), channel_id=1, source_target_pairs={{0,16},{16,0},{8,24},{24,8},{1,17},{17,1},{9,25},{25,9},{2,18},{18... | collective-permute-start | bytes 5271560 | tf_op jit(solution)/shard_map/ppermute | solution.py:49
  199.7 65.0 %collective-permute-start.31 = (bf16[416,1600]{1,0:T(8,128)(2,1)}, bf16[416,1600]{1,0:T(8,128)(2,1)}, u32[]{:S(2)}, u32[]{:S(2)}) collective-permute-start(bf16[416,1600]{1,0:T(8,128)(2,1)} %collective-permute-done.24), channel_id=1, source_target_pairs={{2,0},{4,6},{3,1},{5,7},{10,8},{12,14},{11,9},{13,15},{18,16},{20,... | collective-permute-start | bytes 3993608 | tf_op jit(solution)/shard_map/ppermute | solution.py:53
  243.0 29.5 %collective-permute-start.36 = (bf16[208,2112]{1,0:T(8,128)(2,1)S(1)}, bf16[208,2112]{1,0:T(8,128)(2,1)S(1)}, u32[]{:S(2)}, u32[]{:S(2)}) collective-permute-start(bf16[208,2112]{1,0:T(8,128)(2,1)S(1)} %slice.107), channel_id=1, source_target_pairs={{0,16},{16,0},{8,24},{24,8},{1,17},{17,1},{9,25},{25,9},{2,18},{18... | collective-permute-start | bytes 2635784 | tf_op jit(solution)/shard_map/ppermute | solution.py:49
  243.5 30.6 %collective-permute-start.37 = (bf16[208,2112]{1,0:T(8,128)(2,1)S(1)}, bf16[208,2112]{1,0:T(8,128)(2,1)S(1)}, u32[]{:S(2)}, u32[]{:S(2)}) collective-permute-start(bf16[208,2112]{1,0:T(8,128)(2,1)S(1)} %slice.109), channel_id=1, source_target_pairs={{0,8},{8,0},{16,24},{24,16},{1,9},{9,1},{17,25},{25,17},{2,10},{10... | collective-permute-start | bytes 2635784 | tf_op jit(solution)/shard_map/ppermute | solution.py:45
  350.6 14.3 %collective-permute-start.43 = (bf16[2,128,800]{2,1,0:T(8,128)(2,1)S(1)}, bf16[2,128,800]{2,1,0:T(8,128)(2,1)S(1)}, u32[]{:S(2)}, u32[]{:S(2)}) collective-permute-start(bf16[2,128,800]{2,1,0:T(8,128)(2,1)S(1)} %get-tuple-element.62), channel_id=1, source_target_pairs={{0,24},{24,0},{8,16},{16,8},{1,25},{25,1},{9,17},{17,9},{2,26},{26... | collective-permute-start | bytes 1228808 | tf_op jit(solution)/shard_map/ppermute | solution.py:725
  351.3 22.4 %collective-permute-start.42 = (bf16[2,128,800]{2,1,0:T(8,128)(2,1)S(1)}, bf16[2,128,800]{2,1,0:T(8,128)(2,1)S(1)}, u32[]{:S(2)}, u32[]{:S(2)}) collective-permute-start(bf16[2,128,800]{2,1,0:T(8,128)(2,1)S(1)} %get-tuple-element.63), channel_id=1, source_target_pairs={{0,16},{16,0},{8,24},{24,8},{1,17},{17,1},{9,25},{25,9},{2,18},{18... | collective-permute-start | bytes 1228808 | tf_op jit(solution)/shard_map/ppermute | solution.py:49
  352.5 21.3 %collective-permute-start.41 = (bf16[2,128,800]{2,1,0:T(8,128)(2,1)S(1)}, bf16[2,128,800]{2,1,0:T(8,128)(2,1)S(1)}, u32[]{:S(2)}, u32[]{:S(2)}) collective-permute-start(bf16[2,128,800]{2,1,0:T(8,128)(2,1)S(1)} %get-tuple-element.64), channel_id=1, source_target_pairs={{0,8},{8,0},{16,24},{24,16},{1,9},{9,1},{17,25},{25,17},{2,10},{10... | collective-permute-start | bytes 1228808 | tf_op jit(solution)/shard_map/ppermute | solution.py:45
  (36 other events, 284.9 us)

commit v2 on v0

v2 whole, which is shorter than its diff:
```python
import functools

import jax
import jax.numpy as jnp
from jax import lax
from jax.experimental import pallas as pl
from jax.experimental.pallas import tpu as pltpu
from jax.sharding import PartitionSpec as P

D = 1600
HD = 64
QH = 16
KVH = 4

EPSILON = 1e-06
LOG2_E = 1.4426950408889634

X_PAIRS = ((0, 1), (1, 0), (2, 3), (3, 2))
Y_PAIRS = ((0, 2), (2, 0), (1, 3), (3, 1))
D_PAIRS = ((0, 3), (3, 0), (1, 2), (2, 1))
Z_OUTER = ((0, 1), (1, 0), (2, 3), (3, 2))
Z_INNER = ((1, 2), (2, 1))
Z_ENDS = ((1, 0), (2, 3))
Z_FAR = ((2, 0), (1, 3))
Z_SLOTS = ((0, 1, 2, 3), (1, 0, 2, 3), (2, 3, 1, 0), (3, 2, 1, 0))

VMEM_LIMIT = 56 * 1024 * 1024


def params():
    return pltpu.CompilerParams(vmem_limit_bytes=VMEM_LIMIT)


def cost(flops, size):
    return pl.CostEstimate(flops=int(flops), bytes_accessed=int(size), transcendentals=0)


def tie(*values):
    return lax.optimization_barrier(values)


def swap_x(value):
    return lax.ppermute(value, "rep", X_PAIRS)


def swap_y(value):
    return lax.ppermute(value, "rep", Y_PAIRS)


def along_z(value, pairs):
    return lax.ppermute(value, "tr", pairs)


def other_core(value):
    return lax.ppermute(value, "tc", ((0, 1), (1, 0)))


def load_halves(pieces, target, sems, second, half, wide, column=0):
    width = target.shape[1]
    if wide > half:
        gap = jnp.zeros((wide - half, width), target.dtype)
        target[half:wide, :] = gap
        target[wide + half :, :] = gap
    copies = []
    start = 0
    for piece in pieces:
        count = piece.shape[0]
        for low in range(0, count, half):
            size = min(half, count)
            at_first = start < half
            place = (second if at_first else 1 - second) * wide + start % half
            copies.append(
                pltpu.make_async_copy(
                    piece.at[pl.ds(low, size), pl.ds(column, width)],
                    target.at[pl.ds(pl.multiple_of(place, 16), size), :],
                    sems.at[len(copies)],
                )
            )
            start += size
    for copy in copies:
        copy.start()
    for copy in copies:
        copy.wait()


def silu(value):
    scaled = 0.5 * value
    return scaled + scaled * jnp.tanh(scaled)


def row_mover(slots, steps, inward):
    count = slots * steps
    to_row = lax.broadcasted_iota(jnp.int32, (count, count), 0)
    from_row = lax.broadcasted_iota(jnp.int32, (count, count), 1)
    if inward:
        source = (to_row % slots) * steps + to_row // slots
    else:
        source = (to_row % steps) * slots + to_row // steps
    return jnp.where(from_row == source, 1.0, 0.0).astype(jnp.bfloat16)


def both_halves(rows_own, rows_other, weight):
    rows = jnp.concatenate([rows_own[...], rows_other[...]], axis=1)
    return jnp.dot(rows, weight[...], preferred_element_type=jnp.float32)


def exact_dot(left, right):
    return jnp.dot(left, right, preferred_element_type=jnp.float32).astype(jnp.bfloat16)


def spread_kernel(slots, proc, x, inv_rms, gain, pick, out):
    normed = (x[0].astype(jnp.float32) * inv_rms[0] * gain[...]).astype(jnp.bfloat16)
    mover = row_mover(slots, x.shape[1] // slots, True)
    out[...] = exact_dot(exact_dot(mover, normed), pick[...])


def place_kernel(slots, proc, x, pick, out):
    mover = row_mover(slots, x.shape[1] // slots, True)
    out[...] = exact_dot(exact_dot(mover, x[0]), pick[...])


def attention_kernel(
    slots,
    group_rows,
    kv_here,
    per_kv,
    count,
    half,
    first_column,
    proc,
    lengths,
    second,
    rows_own,
    rows_other,
    cache,
    *rest,
):
    pieces, (out, weight, sems) = rest[:count], rest[count:]
    tile = pl.program_id(0)

    @pl.when(tile == 0)
    def _():
        load_halves(pieces, weight, sems, second[0], half, weight.shape[0] // 2, first_column)

    made = both_halves(rows_own, rows_other, weight).astype(jnp.bfloat16)
    here = made.shape[0] // group_rows
    query_width = kv_here * per_kv * HD
    positions = cache.shape[1]
    stacked = per_kv * group_rows
    row_id = lax.broadcasted_iota(jnp.int32, (stacked, group_rows), 0) % group_rows
    column_id = lax.broadcasted_iota(jnp.int32, (stacked, group_rows), 1)
    own_mask = (row_id % slots == column_id % slots) & (column_id // slots <= row_id // slots)
    column = lax.broadcasted_iota(jnp.int32, (stacked, positions), 1)
    contract = (((1,), (1,)), ((), ()))
    scale = HD ** (-0.5)
    for index in range(here):
        group = proc[tile * here + index]
        prefix_mask = column < lengths[group]
        block = made[index * group_rows : (index + 1) * group_rows]
        past = cache[group]
        results = []
        for head in range(kv_here):
            query = jnp.concatenate(
                [
                    block[:, (head * per_kv + j) * HD : (head * per_kv + j + 1) * HD]
                    for j in range(per_kv)
                ],
                axis=0,
            )
            base = query_width + head * 2 * HD
            key_new = block[:, base : base + HD]
            value_new = block[:, base + HD : base + 2 * HD]
            key_old = past[:, head * 2 * HD : head * 2 * HD + HD]
            value_old = past[:, head * 2 * HD + HD : (head + 1) * 2 * HD]
            old = lax.dot_general(query, key_old, contract, preferred_element_type=jnp.float32)
            new = lax.dot_general(query, key_new, contract, preferred_element_type=jnp.float32)
            old = jnp.where(prefix_mask, old * scale, -jnp.inf)
            new = jnp.where(own_mask, new * scale, -jnp.inf)
            top = jnp.maximum(
                jnp.max(old, axis=1, keepdims=True), jnp.max(new, axis=1, keepdims=True)
            )
            old = jnp.exp(old - top)
            new = jnp.exp(new - top)
            total = jnp.sum(old, axis=1, keepdims=True) + jnp.sum(new, axis=1, keepdims=True)
            value = jnp.dot(
                old.astype(jnp.bfloat16), value_old, preferred_element_type=jnp.float32
            ) + jnp.dot(new.astype(jnp.bfloat16), value_new, preferred_element_type=jnp.float32)
            value = (value / total).astype(jnp.bfloat16)
            for j in range(per_kv):
                results.append(value[j * group_rows : (j + 1) * group_rows])
        out[index * group_rows : (index + 1) * group_rows, :] = jnp.concatenate(results, axis=1)


def conv_kernel(
    slots,
    group_rows,
    count,
    half,
    first_column,
    proc,
    second,
    rows_own,
    rows_other,
    history,
    taps,
    bias,
    mix_weight,
    *rest,
):
    pieces, (out, out_mix, weight, sems) = rest[:count], rest[count:]
    tile = pl.program_id(0)

    @pl.when(tile == 0)
    def _():
        load_halves(pieces, weight, sems, second[0], half, weight.shape[0] // 2, first_column)

    made = both_halves(rows_own, rows_other, weight)
    here = made.shape[0] // group_rows
    steps = group_rows // slots
    tap_count = taps.shape[0]
    past = history.shape[1]
    for index in range(here):
        start = index * group_rows
        state = history[proc[tile * here + index]]
        sequence = [
            jnp.broadcast_to(state[k : k + 1, :], (slots, made.shape[1])) for k in range(past)
        ] + [made[start + step * slots : start + (step + 1) * slots] for step in range(steps)]
        for step in range(steps):
            value = bias[...]
            for tap in range(tap_count):
                value = value + taps[tap : tap + 1, :] * sequence[step + tap]
            out[start + step * slots : start + (step + 1) * slots, :] = silu(value).astype(
                jnp.bfloat16
            )
    out_mix[...] = jnp.dot(
        out[...], mix_weight[...], preferred_element_type=jnp.float32
    ).astype(jnp.bfloat16)


def softplus(value):
    small = jnp.exp(-jnp.abs(value))
    series = small * (1.0 - small * (0.5 - small * (1.0 / 3.0)))
    return jnp.maximum(value, 0.0) + jnp.where(small < 0.01, series, jnp.log(1.0 + small))


def scan_kernel(
    slots, proc, conv, mix_own, mix_other, step_weight, step_bias, decay_log, skip, state, *rest
):
    out, *scratch = rest[-8:]
    step_scratch, drive_scratch, out_scratch, rate_scratch, state_scratch, in_mix, out_mix = scratch
    lanes = 128
    kind = jnp.bfloat16
    rank = step_weight.shape[0]
    states, channels = decay_log.shape
    total_rows = conv.shape[0]
    mix = mix_own[...].astype(jnp.float32) + mix_other[...].astype(jnp.float32)
    raw = (
        jnp.dot(mix[:, :rank].astype(kind), step_weight[...], preferred_element_type=jnp.float32)
        + step_bias[...]
    )
    step = softplus(raw)
    value = conv[...].astype(jnp.float32)
    step_scratch[:, :channels] = step
    drive_scratch[:, :channels] = step * value
    rate_scratch[:, :channels] = -jnp.exp(decay_log[...]) * LOG2_E
    state_scratch[:, :channels] = state[0]
    for n in range(states):
        in_mix[n] = jnp.broadcast_to(mix[:, 128 + n : 129 + n], (total_rows, lanes)).astype(kind)
        out_mix[n] = jnp.broadcast_to(
            mix[:, 128 + states + n : 129 + states + n], (total_rows, lanes)
        ).astype(kind)

    def one(chunk, carry):
        columns = pl.ds(pl.multiple_of(chunk * lanes, lanes), lanes)

        def spread(source, n):
            return jnp.broadcast_to(source[n : n + 1, columns], (slots, lanes)).astype(kind)

        held = [spread(state_scratch, n) for n in range(states)]
        for start in range(0, total_rows, slots):
            here = pl.ds(start, slots)
            size = step_scratch[here, columns].astype(kind)
            drive = drive_scratch[here, columns].astype(kind)
            total = None
            for first in range(0, states, 4):
                part = None
                for n in range(first, first + 4):
                    held[n] = jnp.exp2(size * spread(rate_scratch, n)) * held[n] + drive * in_mix[n, here, :]
                    term = held[n] * out_mix[n, here, :]
                    part = term if part is None else part + term
                part = part.astype(jnp.float32)
                total = part if total is None else total + part
            out_scratch[here, columns] = total
        return carry

    lax.fori_loop(0, step_scratch.shape[1] // lanes, one, 0)
    out[...] = out_scratch[:, :channels] + skip[...] * value


def gate_kernel(count, half, first_column, second, rows_own, rows_other, scanned, *rest):
    pieces, (out, weight, sems) = rest[:count], rest[count:]

    @pl.when(pl.program_id(0) == 0)
    def _():
        load_halves(pieces, weight, sems, second[0], half, weight.shape[0] // 2, first_column)

    gate = both_halves(rows_own, rows_other, weight)
    out[...] = (scanned[...] * silu(gate)).astype(jnp.bfloat16)


def transposed_dot(left, right):
    return lax.dot_general(
        left, right, (((1,), (1,)), ((), ())), preferred_element_type=jnp.float32
    ).astype(jnp.bfloat16)


def attn_out_kernel(count, half, first_column, blocks, second, heads, *rest):
    pieces, (keep, send, raw, weight, sems) = rest[:count], rest[count:]
    wide = raw.shape[0] // 2
    columns = weight.shape[0] // 2

    @pl.when(pl.program_id(0) == 0)
    def _():
        load_halves(pieces, raw, sems, second[0], half, wide, first_column)
        loaded = raw[...].astype(jnp.float32)
        for index in range(2):
            parts = [
                jnp.zeros((size, loaded.shape[1]), jnp.float32)
                if at is None
                else loaded[index * wide + at : index * wide + at + size]
                for at, size in blocks
            ]
            weight[index * columns : (index + 1) * columns, :] = jnp.concatenate(
                parts, axis=0
            ).astype(weight.dtype)

    attended = heads[...]
    keep[...] = transposed_dot(attended, weight[:columns, :])
    send[...] = transposed_dot(attended, weight[columns:, :])


def ssm_out_kernel(slot_choices, part, summed, scalars, gated, *rest):
    ready, rest = rest[:summed], rest[summed:]
    count = sum(slot_choices)
    pieces, (keep, send, *sums, weight, sems) = rest[:count], rest[count:]
    wide = weight.shape[0] // 2
    filled = part * len(slot_choices)
    second = scalars[0]

    @pl.when(pl.program_id(0) == 0)
    def _():
        if wide > filled:
            gap = jnp.zeros((wide - filled, weight.shape[1]), weight.dtype)
            weight[filled:wide, :] = gap
            weight[wide + filled :, :] = gap

        def copies(source, slot):
            for index, base in ((0, second), (1, 1 - second)):
                yield pltpu.make_async_copy(
                    source.at[pl.ds(pl.multiple_of(base * part, 16), part), :],
                    weight.at[pl.ds(index * wide + slot * part, part), :],
                    sems.at[slot, index],
                )

        at = 0
        firsts = []
        for slot, choices in enumerate(slot_choices):
            firsts.append(pieces[at])
            if choices == 1:
                for copy in copies(pieces[at], slot):
                    copy.start()
            else:
                for choice in range(2):

                    @pl.when(scalars[1] == 1 - choice)
                    def _(piece=pieces[at + choice], slot=slot):
                        for copy in copies(piece, slot):
                            copy.start()

            at += choices
        for slot, piece in enumerate(firsts):
            for copy in copies(piece, slot):
                copy.wait()

    value = gated[...]
    send[...] = transposed_dot(value, weight[wide:, :])
    keep[...] = transposed_dot(value, weight[:wide, :])
    if ready:
        sums[0][:, 0:1] = square_sum(ready[0], ready[1])
        sums[0][:, 1:2] = square_sum(ready[2], ready[3])


def square_sum(keep, got):
    value = keep[...].astype(jnp.float32) + got[...].astype(jnp.float32)
    return jnp.sum(value * value, axis=1, keepdims=True)


def square_kernel(*refs):
    *refs, out = refs
    if len(refs) == 4:
        out[:, 0:1] = square_sum(refs[0], refs[1])
        out[:, 1:2] = square_sum(refs[2], refs[3])
    else:
        out[:, 0:1] = refs[0][:, 0:1]
        out[:, 1:2] = refs[0][:, 1:2] + square_sum(refs[1], refs[2])


def mixed_kernel(slots, first, sections, here, proc, sizes, x_keep, keep_attn, got_attn, *rest):
    ssm_refs = rest[: 2 * sections]
    own_squares, other_squares, gains, features = rest[2 * sections : 2 * sections + 4]
    outs = rest[2 * sections + 4 : 2 * sections + 4 + here]
    made, sems = rest[2 * sections + 4 + here :]
    step = pl.program_id(0)
    ssm = jnp.concatenate(
        [
            keep[...].astype(jnp.float32) + got[...].astype(jnp.float32)
            for keep, got in zip(ssm_refs[::2], ssm_refs[1::2])
        ],
        axis=1,
    )
    attn = keep_attn[...].astype(jnp.float32) + got_attn[...].astype(jnp.float32)
    scales = lax.rsqrt((own_squares[...] + other_squares[...]) / D + EPSILON)
    branch = 0.5 * (
        gains[0:1, :] * attn * scales[:, 0:1] + gains[1:2, :] * ssm * scales[:, 1:2]
    )
    mixed = (x_keep[...].astype(jnp.float32) + branch).astype(jnp.bfloat16)
    placed = exact_dot(mixed, features[...])
    size = made.shape[1]
    in_step = mixed.shape[0] // size
    outward = row_mover(slots, size // slots, False)
    slot = lax.broadcasted_iota(jnp.int32, (size, 1), 0) // (size // slots)

    def copy(number):
        return pltpu.make_async_copy(made.at[number], outs[number], sems.at[number])

    for index in range(in_step):
        number = step * in_step + index
        rows = exact_dot(outward, placed[index * size : (index + 1) * size])
        live = slot < sizes[proc[first + number]]
        made[number] = jnp.where(live, rows, jnp.zeros_like(rows))
    for number in range(here):

        @pl.when(step == number // in_step)
        def _(number=number):
            copy(number).start()

    @pl.when(step == here // in_step - 1)
    def _():
        for number in range(here):
            copy(number).wait()


def local(
    tokens,
    prefix_kv,
    ssm_state,
    conv_state,
    prefix_len,
    group_size,
    serve_replica,
    in_gain,
    w_query,
    w_keyval,
    w_inner,
    conv_weight,
    conv_bias,
    w_xproj,
    dt_weight,
    dt_bias,
    decay_log,
    skip_gain,
    w_attn_out,
    w_ssm_out,
    attn_gain,
    ssm_gain,
):
    rep_count = lax.axis_size("rep")
    row_axis = lax.axis_size("tr")
    tensor_count = lax.axis_size("tc")
    rep = lax.axis_index("rep")
    row = lax.axis_index("tr")
    core = lax.axis_index("tc")
    groups, slots, steps, width = tokens.shape
    pairs = groups // rep_count
    kv_here = KVH // tensor_count
    per_kv = QH // KVH
    heads_width = QH // tensor_count * HD
    group_rows = slots * steps
    rows = groups * group_rows
    tile = groups // 4 * group_rows
    channels = w_inner.shape[2]
    shards = rep_count * row_axis
    shard = w_query.shape[0]
    pad = -(-shard // 8) * 8
    depth = shards * pad
    half = depth // 2
    wide = -(-half // 128) * 128
    by_links = rep_count == 4 and row_axis == 4
    sections = 2 if by_links else 1
    section = half // sections
    section_wide = -(-section // 128) * 128
    columns = sections * section_wide
    bf16 = jnp.bfloat16
    f32 = jnp.float32
    i32 = jnp.int32

    def padded(value):
        return jnp.pad(value, ((0, pad - shard), (0, 0)))

    ssm_shard = padded(w_ssm_out.T)
    conv_shard = padded(w_inner[:, 0])
    gate_shard = padded(w_inner[:, 1])
    attn_shard = padded(jnp.concatenate([w_query, w_keyval, w_attn_out.T], axis=1))
    qkv_width = w_query.shape[1] + w_keyval.shape[1]
    rank, states = dt_weight.shape[0], decay_log.shape[0]
    mixes = 256

    def feature_at(column, lines_outside, rep, row):
        inside = column < half
        if lines_outside:
            inside = column % section_wide < section
            column = column // section_wide * section + column % section_wide
        block, offset = column // pad, column % pad
        if by_links:
            if lines_outside:
                slot, plane = block // 2, block % 2
            else:
                slot, plane = block % row_axis, block // row_axis
            low = row < 2
            line = jnp.where(
                slot == 0,
                row,
                jnp.where(
                    slot == 1,
                    row ^ 1,
                    jnp.where(slot == 2, jnp.where(low, 2, 1), jnp.where(low, 3, 0)),
                ),
            )
            block = ((rep % 2) ^ plane) * row_axis + line
        return jnp.where((offset < shard) & inside, block * shard + offset, -1)

    def picker(shape, column_dim, lines_outside, rep, row):
        column = lax.broadcasted_iota(i32, shape, column_dim)
        feature = lax.broadcasted_iota(i32, shape, 1 - column_dim)
        return feature == feature_at(column, lines_outside, rep, row)

    def column_picks(rep, row):
        keep_pick = picker((width, columns), 1, True, rep, row)
        gains = jnp.stack([attn_gain, ssm_gain])
        gains = lax.dynamic_slice_in_dim(gains, core * width, width, 1)
        gains = jnp.sum(jnp.where(keep_pick[None], gains[:, :, None], 0.0), axis=1)
        features_back = picker((columns, width), 0, True, rep, row).astype(bf16)
        return keep_pick.astype(bf16), gains, features_back

    second = ((rep // 2) ^ core if by_links else core).astype(i32)[None]

    def group_order(serve_replica):
        served = lax.dynamic_slice_in_dim(serve_replica, first_group, groups, 0)
        target = served ^ rep if by_links else served
        ids = jnp.arange(groups, dtype=i32)
        same = (served[:, None] == served[None, :]) & (ids[None, :] < ids[:, None])
        places = jnp.sum(same.astype(i32), axis=1) * rep_count + target
        return jnp.sum(
            jnp.where(places[None, :] == ids[:, None], ids[None, :], 0), axis=1
        ).astype(i32)

    def inverse_rms(tokens):
        wide_rows = tokens.reshape(groups, group_rows, width).astype(f32)
        square_sums = lax.psum(jnp.sum(wide_rows * wide_rows, axis=2), "tc")
        return lax.rsqrt(square_sums / D + EPSILON)[:, :, None]

    first_group = (rep * row_axis + row) * groups
    def row_block(columns, size=tile, first=0):
        return pl.BlockSpec((size, columns), lambda g, *_: (g + first, 0))

    def whole(*shape):
        return pl.BlockSpec(shape, lambda g, *_: (0,) * len(shape))

    def group_block(*shape, first=0):
        return pl.BlockSpec(
            (1,) + shape, lambda g, proc, *_: (proc[g + first],) + (0,) * len(shape)
        )

    anywhere = pl.BlockSpec(memory_space=pl.ANY)

    def rows_of(columns, kind=bf16, count=rows):
        return jax.ShapeDtypeStruct((count, columns), kind)

    def call(kernel, scalars, grid, in_specs, out_specs, out_shape, scratch, spend, name, alias=None):
        return pl.pallas_call(
            kernel,
            grid_spec=pltpu.PrefetchScalarGridSpec(
                num_scalar_prefetch=scalars,
                grid=(grid,),
                in_specs=in_specs,
                out_specs=out_specs,
                scratch_shapes=scratch,
            ),
            out_shape=out_shape,
            input_output_aliases=alias or {},
            compiler_params=params(),
            cost_estimate=cost(spend * 1.0e7, rows * 4),
            name=name,
        )

    def piece_copies(pieces):
        return pltpu.SemaphoreType.DMA((max(len(pieces), 2),))

    def spread(inv, rep, row):
        spread_pick = picker((width, wide), 1, False, rep, row).astype(bf16)
        return call(
            functools.partial(spread_kernel, slots),
            1,
            groups,
            [
                group_block(group_rows, width),
                group_block(group_rows, 1),
                whole(1, width),
                whole(width, wide),
            ],
            row_block(wide, group_rows),
            rows_of(wide),
            [],
            8,
            "spread_rows",
        )(proc, tokens.reshape(groups, group_rows, width), inv, in_gain[None], spread_pick)

    def place(keep_pick):
        return call(
            functools.partial(place_kernel, slots),
            1,
            groups,
            [group_block(group_rows, width), whole(width, columns)],
            row_block(columns, group_rows),
            rows_of(columns),
            [],
            8,
            "place_rows",
        )(proc, tokens.reshape(groups, group_rows, width), keep_pick)

    def attention(rows_own, rows_other, pieces, lengths):
        return call(
            functools.partial(
                attention_kernel, slots, group_rows, kv_here, per_kv, len(pieces), half, 0
            ),
            3,
            rows // tile,
            [row_block(wide)] * 2 + [whole(*prefix_kv.shape)] + [anywhere] * len(pieces),
            row_block(heads_width),
            rows_of(heads_width),
            [pltpu.VMEM((2 * wide, qkv_width), bf16), piece_copies(pieces)],
            15,
            "attention",
        )(proc, lengths, second, rows_own, rows_other, prefix_kv, *pieces)

    def small_operands(w_xproj, conv_state, conv_bias, dt_bias, skip_gain, prefix_len, group_size):
        mix_weight = jnp.concatenate(
            [
                jnp.pad(w_xproj[:, :rank], ((0, 0), (0, 128 - rank))),
                jnp.pad(w_xproj[:, rank:], ((0, 0), (0, mixes - 128 - 2 * states))),
            ],
            axis=1,
        )
        return (
            mix_weight,
            conv_state,
            conv_bias[None],
            dt_bias[None],
            skip_gain[None],
            lax.dynamic_slice_in_dim(prefix_len, first_group, groups, 0),
            lax.dynamic_slice_in_dim(group_size, first_group, groups, 0),
        )

    plain = (w_xproj, conv_state, conv_bias, dt_bias, skip_gain, prefix_len, group_size)

    def convolve(rows_own, rows_other, pieces, small):
        return call(
            functools.partial(conv_kernel, slots, group_rows, len(pieces), half, 0),
            2,
            rows // tile,
            [
                row_block(wide),
                row_block(wide),
                whole(*conv_state.shape),
                whole(*conv_weight.shape),
                whole(1, channels),
                whole(channels, mixes),
            ]
            + [anywhere] * len(pieces),
            [row_block(channels), row_block(mixes)],
            [rows_of(channels), rows_of(mixes)],
            [pltpu.VMEM((2 * wide, channels), bf16), piece_copies(pieces)],
            14,
            "convolve",
        )(
            proc,
            second,
            rows_own,
            rows_other,
            small[1],
            conv_weight,
            small[2],
            small[0],
            *pieces,
        )

    def scan(first, count, conv_out, mix_own, mix_other, small, earlier=()):
        across = -(-channels // 128) * 128
        blocks = functools.partial(row_block, size=group_rows, first=first)
        return call(
            functools.partial(scan_kernel, slots),
            1,
            count,
            [
                blocks(channels),
                blocks(mixes),
                blocks(mixes),
                whole(rank, channels),
                whole(1, channels),
                whole(states, channels),
                whole(1, channels),
                group_block(*ssm_state.shape[1:], first=first),
            ]
            + [anywhere] * len(earlier),
            blocks(channels),
            rows_of(channels, f32),
            [pltpu.VMEM((group_rows, across), f32)] * 3
            + [pltpu.VMEM((states, across), f32)] * 2
            + [pltpu.VMEM((states, group_rows, 128), bf16)] * 2,
            4 * count,
            "scan_states",
            {9: 0} if earlier else None,
        )(
            proc,
            conv_out,
            mix_own,
            mix_other,
            dt_weight,
            small[3],
            decay_log,
            small[4],
            ssm_state,
            *earlier,
        )

    def gate(rows_own, rows_other, scanned, pieces):
        return call(
            functools.partial(gate_kernel, len(pieces), half, 0),
            1,
            rows // tile,
            [row_block(wide)] * 2 + [row_block(channels)] + [anywhere] * len(pieces),
            row_block(channels),
            rows_of(channels),
            [pltpu.VMEM((2 * wide, channels), bf16), piece_copies(pieces)],
            13,
            "gate",
        )(second, rows_own, rows_other, scanned, *pieces)

    def attn_out(heads, pieces):
        blocks = []
        for number in range(sections):
            if by_links:
                blocks += [
                    ((plane * row_axis + slot) * pad, pad)
                    for slot in (2 * number, 2 * number + 1)
                    for plane in range(2)
                ]
            else:
                blocks.append((0, half))
            if section_wide > section:
                blocks.append((None, section_wide - section))
        return call(
            functools.partial(attn_out_kernel, len(pieces), half, qkv_width, tuple(blocks)),
            1,
            rows // tile,
            [row_block(heads_width)] + [anywhere] * len(pieces),
            [row_block(columns)] * 2,
            [rows_of(columns)] * 2,
            [
                pltpu.VMEM((2 * wide, heads_width), bf16),
                pltpu.VMEM((2 * columns, heads_width), bf16),
                piece_copies(pieces),
            ],
            6,
            "attn_out",
        )(second, heads, *pieces)

    def ssm_out(gated, choices, pieces, ready=()):
        scalars = jnp.stack([second[0], inner.astype(i32) if by_links else second[0]])
        sums = 1 if ready else 0
        return call(
            functools.partial(ssm_out_kernel, choices, section // len(choices), len(ready)),
            1,
            rows // tile,
            [row_block(channels)]
            + [row_block(value.shape[1]) for value in ready]
            + [anywhere] * len(pieces),
            [row_block(section_wide)] * 2 + [row_block(2)] * sums,
            [rows_of(section_wide)] * 2 + [rows_of(2, f32)] * sums,
            [
                pltpu.VMEM((2 * section_wide, channels), bf16),
                pltpu.SemaphoreType.DMA((len(choices), 2)),
            ],
            8,
            "ssm_out",
        )(scalars, gated, *ready, *pieces)

    def squares(attn, ssm, earlier=None):
        if earlier is not None:
            operands, specs = [earlier], [row_block(2)]
        else:
            operands, specs = list(attn), [row_block(columns)] * 2
        return call(
            square_kernel,
            0,
            rows // tile,
            specs + [row_block(section_wide)] * 2,
            row_block(2),
            rows_of(2, f32),
            [],
            2,
            "squares",
        )(*operands, *ssm)

    def mix(part, x_keep, attn, ssm, own_squares, other_squares, gains, features_back, sizes):
        here = groups // pairs
        size = 2 * group_rows
        block = functools.partial(row_block, size=size, first=part * here // 2)
        return call(
            functools.partial(mixed_kernel, slots, part * here, sections, here),
            2,
            here // 2,
            [block(columns)] * 3
            + [block(section_wide)] * (2 * sections)
            + [block(2)] * 2
            + [whole(2, columns), whole(columns, width)],
            [anywhere] * here,
            [rows_of(width, count=group_rows)] * here,
            [pltpu.VMEM((here, group_rows, width), bf16), pltpu.SemaphoreType.DMA((here,))],
            4,
            "mixed_rows",
        )(
            proc,
            sizes,
            x_keep,
            *attn,
            *ssm,
            own_squares,
            other_squares,
            gains,
            features_back,
        )

    if by_links:

        def line_first(value):
            return along_z(value, Z_OUTER), along_z(value, Z_INNER)

        def line_second(first):
            near, middle = first
            return along_z(near, Z_INNER), along_z(middle, Z_ENDS), along_z(near, Z_FAR)

        inner = (row == 1) | (row == 2)

        def line_block(value, first, last):
            near, middle = first
            crossed, ends, far = last
            return jnp.concatenate(
                [value, near, jnp.where(inner, middle, ends), jnp.where(inner, crossed, far)],
                axis=0,
            )

        def plane_first(value):
            return swap_x(value), swap_y(value)

        def plane_second(first):
            by_x, by_y = first
            cut = by_x.shape[0] // 16 * 8
            return swap_y(by_x[:cut]), swap_x(by_y[cut:])

        ssm_p1 = plane_first(ssm_shard)
        conv_z1 = line_first(conv_shard)

        ssm_p1, conv_z1, tokens_late, serve_late, rep_late, row_late = tie(
            ssm_p1, conv_z1, tokens, serve_replica, rep, row
        )
        ssm_p2 = plane_second(ssm_p1)
        conv_z2 = line_second(conv_z1)
        proc = group_order(serve_late)
        rows_own = spread(inverse_rms(tokens_late), rep_late, row_late)

        conv_block = line_block(conv_shard, conv_z1, conv_z2)
        conv_block, ssm_p2, gate_shard, rows_own = tie(conv_block, ssm_p2, gate_shard, rows_own)
        conv_p1 = plane_first(conv_block)
        gate_z1 = line_first(gate_shard)
        gate_z1, plain = tie(gate_z1, plain)
        gate_z2 = line_second(gate_z1)
        small = small_operands(*plain)

        ssm_block = jnp.concatenate((ssm_shard,) + tuple(ssm_p1) + tuple(ssm_p2), axis=0)
        gate_block = line_block(gate_shard, gate_z1, gate_z2)
        conv_p1, gate_block, ssm_block, rows_own, rep_late, row_late, small = tie(
            conv_p1, gate_block, ssm_block, rows_own, rep, row, small
        )
        conv_p2 = plane_second(conv_p1)
        ssm_near, ssm_middle = line_first(ssm_block)
        rows_other = other_core(rows_own)
        keep_pick, gains, features_back = column_picks(rep_late, row_late)
        x_keep = place(keep_pick)

        conv_p2, gate_block, rows_other, attn_shard, x_keep, gains, features_back = tie(
            conv_p2, gate_block, rows_other, attn_shard, x_keep, gains, features_back
        )
        gate_p1 = plane_first(gate_block)
        conv_out, mix_own = convolve(
            rows_own, rows_other, (conv_block,) + tuple(conv_p1) + tuple(conv_p2), small
        )
        conv_out, mix_own, ssm_near, ssm_middle, attn_shard = tie(
            conv_out, mix_own, ssm_near, ssm_middle, attn_shard
        )
        mix_other = other_core(mix_own)
        attn_z1 = line_first(attn_shard)
        count = groups // 2
        scanned = scan(0, count, conv_out, mix_own, mix_other, small)

        gate_p1, attn_z1, scanned = tie(gate_p1, attn_z1, scanned)
        gate_p2 = plane_second(gate_p1)
        attn_z2 = line_second(attn_z1)
        scanned = scan(
            count, groups - count, conv_out, mix_own, mix_other, small, (scanned,)
        )
        attn_block = line_block(attn_shard, attn_z1, attn_z2)

        gate_p2, attn_block, ssm_near, ssm_middle, scanned = tie(
            gate_p2, attn_block, ssm_near, ssm_middle, scanned
        )
        attn_p1 = plane_first(attn_block)
        crossed = along_z(ssm_near, Z_INNER)
        ends = along_z(ssm_middle, Z_ENDS)
        gated = gate(rows_own, rows_other, scanned, (gate_block,) + tuple(gate_p1) + tuple(gate_p2))

        attn_p1, gated = tie(attn_p1, gated)
        attn_p2 = plane_second(attn_p1)
        keep_early, send_early = ssm_out(gated, (1, 1), (ssm_block, ssm_near))
        crossed, ends, ssm_near, keep_early, attn_p2, attn_block = tie(
            crossed, ends, ssm_near, keep_early, attn_p2, attn_block
        )
        far = along_z(ssm_near, Z_FAR)
        got_early = other_core(send_early)
        attn_pieces = (attn_block,) + tuple(attn_p1) + tuple(attn_p2)
        heads = attention(rows_own, rows_other, attn_pieces, small[5])
        keep_attn, send_attn = attn_out(heads, attn_pieces)
        send_attn, far = tie(send_attn, far)
        got_attn = other_core(send_attn)
        attn = [keep_attn, got_attn]

        late_pieces = (ssm_middle, ends, crossed, far)
        keep_late, send_late, sums = ssm_out(
            gated, (2, 2), late_pieces, attn + [keep_early, got_early]
        )
        got_late = other_core(send_late)
        sums = squares(attn, [keep_late, got_late], sums)
        other_sums = other_core(sums)
        ssm = [keep_early, got_early, keep_late, got_late]
        received = []
        for part in range(pairs):
            mixed = mix(part, x_keep, attn, ssm, sums, other_sums, gains, features_back, small[6])
            received.append(
                (
                    mixed[0],
                    swap_x(mixed[1]),
                    swap_y(mixed[2]),
                    lax.ppermute(mixed[3], "rep", D_PAIRS),
                )
            )
        by_source = [jnp.stack([part[index] for part in received]) for index in range(rep_count)]
        for bit in (1, 2):
            swapped = (rep & bit) != 0
            by_source = [
                jnp.where(swapped, by_source[index ^ bit], by_source[index])
                for index in range(rep_count)
            ]
        mixed = jnp.concatenate(by_source, axis=0)
    else:

        def gathered(value):
            return lax.all_gather(value, ("rep", "tr"), axis=0, tiled=True)

        proc = group_order(serve_replica)
        small = small_operands(*plain)
        rows_own = spread(inverse_rms(tokens), rep, row)
        rows_other = other_core(rows_own)
        keep_pick, gains, features_back = column_picks(rep, row)
        x_keep = place(keep_pick)
        attn_pieces = (gathered(attn_shard),)
        heads = attention(rows_own, rows_other, attn_pieces, small[5])
        conv_out, mix_own = convolve(rows_own, rows_other, (gathered(conv_shard),), small)
        scanned = scan(0, groups, conv_out, mix_own, other_core(mix_own), small)
        gated = gate(rows_own, rows_other, scanned, (gathered(gate_shard),))
        keep_attn, send_attn = attn_out(heads, attn_pieces)
        attn = [keep_attn, other_core(send_attn)]
        kept, sent = ssm_out(gated, (1,), (gathered(ssm_shard),))
        ssm = [kept, other_core(sent)]
        sums = squares(attn, ssm)
        other_sums = other_core(sums)
        received = [
            jnp.stack(
                mix(part, x_keep, attn, ssm, sums, other_sums, gains, features_back, small[6])
            )
            for part in range(pairs)
        ]
        mixed = jnp.stack(received, axis=1).reshape(groups, group_rows, width)
        mixed = lax.all_to_all(mixed, "rep", split_axis=0, concat_axis=0, tiled=True)
    return mixed.reshape(groups, slots, steps, width)


def solution(mesh):
    placed = (
        P(("rep", "tr"), None, None, "tc"),
        P(("rep", "tr"), None, "tc"),
        P(("rep", "tr"), None, "tc"),
        P(("rep", "tr"), None, "tc"),
        P(),
        P(),
        P(),
        P("tc"),
        P(("rep", "tr"), "tc"),
        P(("rep", "tr"), "tc"),
        P(("rep", "tr"), None, "tc"),
        P(None, "tc"),
        P("tc"),
        P("tc", None),
        P(None, "tc"),
        P("tc"),
        P(None, "tc"),
        P("tc"),
        P("tc", ("rep", "tr")),
        P("tc", ("rep", "tr")),
        P(),
        P(),
    )
    return jax.shard_map(
        local,
        mesh=mesh,
        in_specs=placed,
        out_specs=P(("rep", "tr"), None, None, "tc"),
        check_vma=False,
    )
```

time: 651 us -> 319 us (0.49)
  local copies, waits for them, and re-layouts: 203 us -> 27.1 us
  other arithmetic: 182 us -> 25.9 us
  Pallas kernels: 0 us -> 141 us
  blocking collectives: 84.4 us -> 2.47 us
  matrix products: 72.2 us -> 0 us
  starting transfers between devices: 11.7 us -> 58.1 us
  waiting for transfers between devices: 75.1 us -> 61.2 us
  between operations: 14.2 us -> 0.89 us
    pallas_call x0 -> x13, Pallas kernels: none -> 141 us  [the longest x2 32.9 us: scan(): call(functools.partial(scan_kernel, slots), 1, count, [blocks(channels),...]
    reduce_sum x28 -> x4, other arithmetic: 110 us -> 2.57 us  [the longest x1 1.31 us: column_picks(): gains = jnp.sum(jnp.where(keep_pick[None], gains[:, :, None], 0.0), axis=1)]
    dot_general x39 -> x0, matrix products: 72.2 us -> none  [the longest x1 19 us: local(): inner_run = jnp.dot(normed, pieces[2], preferred_element_type=jnp.float32)]
    all_gather x5 -> x0, waiting for transfers between devices: 69.2 us -> none  [the longest x1 46.8 us: local(): lax.all_gather(inner_cols, ('rep', 'tr'), axis=0, tiled=True)]
    dynamic_slice x60 -> x3, local copies, waits for them, and re-layouts: 65 us -> 1.88 us  [the longest x1 0.73 us: group_order(): served = lax.dynamic_slice_in_dim(serve_replica, first_group, groups, 0)]
    ppermute x0 -> x48, waiting for transfers between devices: none -> 61.2 us  [the longest x20 30.4 us: along_z(): return lax.ppermute(value, 'tr', pairs)]
    ppermute x0 -> x48, starting transfers between devices: none -> 58.1 us  [the longest x20 31.8 us: along_z(): return lax.ppermute(value, 'tr', pairs)]
    all_gather x1 -> x0, blocking collectives: 51.1 us -> none  [local(): lax.all_gather(w_keyval, ('rep', 'tr'), axis=0, tiled=True)]
  transfers between devices with their start and end apart: 11 -> 48, of which waited for: 4 -> 17; matrix products, arithmetic and copies ran while one was open for 69% -> 14% of each run, Pallas kernels for 0% -> 38%
where the time goes in v2:
time: 319 us; the launch traced here: 316 us
  Pallas kernels  141 us (44%)
  waiting for transfers between devices  61.2 us (19%)
  starting transfers between devices  58.1 us (18%)
  local copies, waits for them, and re-layouts  27.1 us (8%)
  other arithmetic  25.9 us (8%)
    pallas_call x2, Pallas kernels, scan(): call(functools.partial(scan_kernel, slots), 1, count, [blocks(channels),...  32.9 us
    ppermute x20, starting transfers between devices, along_z(): return lax.ppermute(value, 'tr', pairs)  31.8 us
    ppermute x20, waiting for transfers between devices, along_z(): return lax.ppermute(value, 'tr', pairs)  30.4 us
    pallas_call x2, Pallas kernels, ssm_out(): call(functools.partial(ssm_out_kernel, choices, section // len(choices),...  19.8 us
    pallas_call x1, Pallas kernels, attention(): call(functools.partial(attention_kernel, slots, group_rows, kv_here, per_...  17.4 us
    pallas_call x1, Pallas kernels, convolve(): call(functools.partial(conv_kernel, slots, group_rows, len(pieces), half,...  15 us
    pallas_call x2, Pallas kernels, mix(): call(functools.partial(mixed_kernel, slots, part * here, sections, here),...  13.3 us
    pallas_call x1, Pallas kernels, gate(): call(functools.partial(gate_kernel, len(pieces), half, 0), 1, rows // til...  13.1 us
  transfers between devices with their start and end apart: 48, of which 17 were waited for; matrix products, arithmetic and copies ran while one was open for 14% of the time, Pallas kernels for 38%

profile of v2, /device:TPU:0, one launch (start us, length us, event | category | flops | bytes accessed | tf_op | source)
XLA Modules:
  0.0 316.5 jit_solution(3475882598467045800)
XLA Ops:
  0.0 2.5 fusion.65
  2.6 3.1 collective-permute-start.2
  15.9 2.0 collective-permute-done
  23.9 2.5 psum.7
  35.6 9.4 %spread_rows.1.rows_own = bf16[1024,896]{1,0:T(8,128)(2,1)} custom-call(s32[8]{0:T(128)} %select_reduce_fusion.1.proc, bf16[8,128,800]{2,1,0:T(8,128)(2,1)} %bitcast.21, f32[8,128,1]{2,1,0:T(8,128)} %copy.37.inv_rms, f32[1,800]{1,0:T(1,128)} %broadcast_in_dim.113.gain, bf16[800,896]{1,0:T(8,128)(2,1)} %fusion.42.pick), custom_call_target="tpu_custom_call" | custom-call | flops 80000000 | bytes 4096 | tf_op jit(solution)/shard_map/spread_rows/pallas_call | solution.py:611
  48.0 2.2 pad_maximum_fusion.1.rest_0_
  50.2 4.9 %collective-permute-start.11 = (bf16[104,1600]{1,0:T(8,128)(2,1)S(1)}, bf16[104,1600]{1,0:T(8,128)(2,1)}, u32[]{:S(2)}, u32[]{:S(2)}) collective-permute-start(bf16[104,1600]{1,0:T(8,128)(2,1)S(1)} %pad.24), channel_id=1, source_target_pairs={{0,2},{2,0},{4,6},{6,4},{1,3},{3,1},{5,7},{7,5},{8,10},{10,8},{12,... | collective-permute-start | bytes 998408 | tf_op jit(solution)/shard_map/ppermute | solution.py:51
  59.9 3.2 %collective-permute-done.11 = bf16[104,1600]{1,0:T(8,128)(2,1)} collective-permute-done((bf16[104,1600]{1,0:T(8,128)(2,1)S(1)}, bf16[104,1600]{1,0:T(8,128)(2,1)}, u32[]{:S(2)}, u32[]{:S(2)}) %collective-permute-start.11) | collective-permute-done | bytes 332832 | tf_op jit(solution)/shard_map/ppermute | solution.py:51
  71.7 16.9 %collective-permute-done.13 = bf16[104,1600]{1,0:T(8,128)(2,1)S(1)} collective-permute-done((bf16[104,1600]{1,0:T(8,128)(2,1)}, bf16[104,1600]{1,0:T(8,128)(2,1)S(1)}, u32[]{:S(2)}, u32[]{:S(2)}) %collective-permute-start.13) | collective-permute-done | bytes 332832 | tf_op jit(solution)/shard_map/ppermute | solution.py:51
  93.3 2.0 slice.43
  96.4 2.0 slice.44
  99.9 4.5 %fusion.15.rest_7_ = bf16[1024,800]{1,0:T(8,128)(2,1)} fusion(s32[]{:T(128)S(6)} %select_n.394, s32[]{:T(128)S(6)} %select_n.393, s32[]{:T(128)S(6)} %xor.45, s32[]{:T(128)S(6)} %axis_index.36, s32[]{:T(128)S(6)} %select_n.389, s32[1024]{0:T(1024)S(1)} %get-tuple-element.200, s32[1024]{0:T(1024)S(1)} %get-tuple-element.201, s32[1024]{0:T(1024)S(1)} %get-tuple-element.199, ...), kind=kLoop, calls=%fused_computation.47 | loop fusion | flops 42598400 | bytes 1656852 | tf_op jit(solution)/shard_map/convert_element_type | solution.py:552
  104.4 2.4 fusion.22
  106.8 9.1 %place_rows.1.x_keep = bf16[1024,1024]{1,0:T(8,128)(2,1)} custom-call(s32[8]{0:T(128)} %select_reduce_fusion.1.proc, bf16[8,128,800]{2,1,0:T(8,128)(2,1)} %bitcast.22, bf16[800,1024]{1,0:T(8,128)(2,1)} %get-tuple-element.192.pick), custom_call_target="tpu_custom_call" | custom-call | flops 80000000 | bytes 4096 | tf_op jit(solution)/shard_map/place_rows/pallas_call | solution.py:629
  120.5 15.0 %convolve.1 = (bf16[1024,1600]{1,0:T(8,128)(2,1)}, bf16[1024,256]{1,0:T(8,128)(2,1)}) custom-call(s32[8]{0:T(128)} %select_reduce_fusion.1.proc, s32[1]{0:T(128)} %bitcast.6.second, bf16[1024,896]{1,0:T(8,128)(2,1)} %spread_rows.1.rows_own, bf16[1024,896]{1,0:T(8,128)(2,1)} %collective-permute-done.18.rows_other, f32[8,3,1600]{2,1,0:T(4,128)} %copy.40.history, ...), custom_call_target="tpu_custom_call" | custom-call | flops 140000000 | bytes 4096 | tf_op jit(solution)/shard_map/convolve/pallas_call | solution.py:677
  139.3 16.4 %scan_states.2.rest_0_ = f32[1024,1600]{1,0:T(8,128)} custom-call(s32[8]{0:T(128)} %select_reduce_fusion.1.proc, bf16[1024,1600]{1,0:T(8,128)(2,1)} %get-tuple-element.137.conv, bf16[1024,256]{1,0:T(8,128)(2,1)} %get-tuple-element.138.mix_own, bf16[1024,256]{1,0:T(8,128)(2,1)} %copy-done.13, bf16[100,1600]{1,0:T(8,128)(2,1)} %step_weight.3, ...), custom_call_target="tpu_custom_call" | custom-call | flops 160000000 | bytes 4096 | tf_op jit(solution)/shard_map/scan_states/pallas_call | solution.py:710
  162.6 16.5 %scan_states.3.scanned = f32[1024,1600]{1,0:T(8,128)} custom-call(s32[8]{0:T(128)} %select_reduce_fusion.1.proc, bf16[1024,1600]{1,0:T(8,128)(2,1)} %get-tuple-element.137.conv, bf16[1024,256]{1,0:T(8,128)(2,1)} %get-tuple-element.138.mix_own, bf16[1024,256]{1,0:T(8,128)(2,1)} %copy-done.13, ...), custom_call_target="tpu_custom_call", output_to_operand_aliasing={{}: (9, {})} | custom-call | flops 160000000 | bytes 4096 | tf_op jit(solution)/shard_map/scan_states/pallas_call | solution.py:710
  184.3 13.1 %gate.1.gated = bf16[1024,1600]{1,0:T(8,128)(2,1)} custom-call(s32[1]{0:T(128)} %bitcast.6.second, bf16[1024,896]{1,0:T(8,128)(2,1)} %spread_rows.1.rows_own, bf16[1024,896]{1,0:T(8,128)(2,1)} %collective-permute-done.18.rows_other, f32[1024,1600]{1,0:T(8,128)} %scan_states.3.scanned, bf16[416,1600]{1,0:T(8,128)(2,1)} %copy-done.8, ...), custom_call_target="tpu_custom_call" | custom-call | flops 130000000 | bytes 4096 | tf_op jit(solution)/shard_map/gate/pallas_call | solution.py:747
  197.4 7.0 %collective-permute-done.33.rest_1_ = bf16[416,1280]{1,0:T(8,128)(2,1)S(1)} collective-permute-done((bf16[416,1280]{1,0:T(8,128)(2,1)S(1)}, bf16[416,1280]{1,0:T(8,128)(2,1)S(1)}, u32[]{:S(2)}, u32[]{:S(2)}) %collective-permute-start.33) | collective-permute-done | bytes 1064992 | tf_op jit(solution)/shard_map/ppermute | solution.py:43
  209.8 9.1 %ssm_out.2 = (bf16[1024,512]{1,0:T(8,128)(2,1)}, bf16[1024,512]{1,0:T(8,128)(2,1)}) custom-call(s32[2]{0:T(128)} %pad_add_fusion.scalars, bf16[1024,1600]{1,0:T(8,128)(2,1)} %gate.1.gated, bf16[416,1600]{1,0:T(8,128)(2,1)} %constant_dynamic-update-slice_fusion.rest_0_, bf16[416,1600]{1,0:T(8,128)(2,1)} %collective-permute-done.21.rest_1_), custom_call_target="tpu_custom_call" | custom-call | flops 80000000 | bytes 4096 | tf_op jit(solution)/shard_map/ssm_out/pallas_call | solution.py:791
  221.7 17.4 %attention.1.heads = bf16[1024,512]{1,0:T(8,128)(2,1)} custom-call(s32[8]{0:T(128)} %select_reduce_fusion.1.proc, s32[8]{0:T(128)} %dynamic_slice.13.lengths, s32[1]{0:T(128)} %bitcast.6.second, bf16[1024,896]{1,0:T(8,128)(2,1)} %spread_rows.1.rows_own, bf16[1024,896]{1,0:T(8,128)(2,1)} %collective-permute-done.18.rows_other, bf16[8,256,256]{2,1,0:T(8,128)(2,1)} %cache.1, ...), custom_call_target="tpu_custom_call" | custom-call | flops 150000000 | bytes 4096 | tf_op jit(solution)/shard_map/attention/pallas_call | solution.py:642
  239.2 6.9 %attn_out.1 = (bf16[1024,1024]{1,0:T(8,128)(2,1)}, bf16[1024,1024]{1,0:T(8,128)(2,1)}) custom-call(s32[1]{0:T(128)} %bitcast.6.second, bf16[1024,512]{1,0:T(8,128)(2,1)} %attention.1.heads, bf16[416,1280]{1,0:T(8,128)(2,1)} %copy-done.3, bf16[416,1280]{1,0:T(8,128)(2,1)} %copy-done.6, bf16[416,1280]{1,0:T(8,128)(2,1)} %copy-done.7, ...), custom_call_target="tpu_custom_call" | custom-call | flops 60000000 | bytes 4096 | tf_op jit(solution)/shard_map/attn_out/pallas_call | solution.py:772
  246.1 8.2 %collective-permute-done.37.rest_7_ = bf16[416,1600]{1,0:T(8,128)(2,1)S(1)} collective-permute-done((bf16[416,1600]{1,0:T(8,128)(2,1)}, bf16[416,1600]{1,0:T(8,128)(2,1)S(1)}, u32[]{:S(2)}, u32[]{:S(2)}) %collective-permute-start.37) | collective-permute-done | bytes 1331232 | tf_op jit(solution)/shard_map/ppermute | solution.py:51
  254.8 4.8 %collective-permute-done.39.rest_3_.rest_1_ = bf16[1024,512]{1,0:T(8,128)(2,1)S(1)} collective-permute-done((bf16[1024,512]{1,0:T(8,128)(2,1)S(1)}, bf16[1024,512]{1,0:T(8,128)(2,1)S(1)}, u32[]{:S(2)}, u32[]{:S(2)}) %collective-permute-start.39) | collective-permute-done | bytes 1048608 | tf_op jit(solution)/shard_map/ppermute | solution.py:55
  261.5 10.7 %ssm_out.3 = (bf16[1024,512]{1,0:T(8,128)(2,1)}, bf16[1024,512]{1,0:T(8,128)(2,1)}, f32[1024,2]{1,0:T(8,128)}) custom-call(s32[2]{0:T(128)} %pad_add_fusion.scalars, bf16[1024,1600]{1,0:T(8,128)(2,1)} %gate.1.gated, bf16[1024,1024]{1,0:T(8,128)(2,1)} %get-tuple-element.161.rest_0_.keep_attn, bf16[1024,1024]{1,0:T(8,128)(2,1)} %copy-done.1, ...), custom_call_target="tpu_custom_call" | custom-call | flops 80000000 | bytes 4096 | tf_op jit(solution)/shard_map/ssm_out/pallas_call | solution.py:791
  272.4 2.7 collective-permute-done.40.refs_2_.rest_3_
  276.1 3.8 %squares.1.rest_4_ = f32[1024,2]{1,0:T(8,128)} custom-call(f32[1024,2]{1,0:T(8,128)} %get-tuple-element.172.refs_0_, bf16[1024,512]{1,0:T(8,128)(2,1)} %get-tuple-element.170.refs_1_.rest_2_, bf16[1024,512]{1,0:T(8,128)(2,1)} %copy-done.5), custom_call_target="tpu_custom_call" | custom-call | flops 20000000 | bytes 4096 | tf_op jit(solution)/shard_map/squares/pallas_call | solution.py:813
  280.1 2.0 collective-permute-done.41.rest_5_
  282.9 6.7 %mixed_rows.2 = (bf16[128,800]{1,0:T(8,128)(2,1)}, bf16[128,800]{1,0:T(8,128)(2,1)}, bf16[128,800]{1,0:T(8,128)(2,1)}, bf16[128,800]{1,0:T(8,128)(2,1)}) custom-call(s32[8]{0:T(128)} %select_reduce_fusion.1.proc, s32[8]{0:T(128)} %dynamic_slice.14.sizes, bf16[1024,1024]{1,0:T(8,128)(2,1)} %place_rows.1.x_keep, ...), custom_call_target="tpu_custom_call" | custom-call | flops 40000000 | bytes 4096 | tf_op jit(solution)/shard_map/mixed_rows/pallas_call | solution.py:829
  293.1 6.7 %mixed_rows.3 = (bf16[128,800]{1,0:T(8,128)(2,1)}, bf16[128,800]{1,0:T(8,128)(2,1)}, bf16[128,800]{1,0:T(8,128)(2,1)}, bf16[128,800]{1,0:T(8,128)(2,1)}) custom-call(s32[8]{0:T(128)} %select_reduce_fusion.1.proc, s32[8]{0:T(128)} %dynamic_slice.14.sizes, bf16[1024,1024]{1,0:T(8,128)(2,1)} %place_rows.1.x_keep, ...), custom_call_target="tpu_custom_call" | custom-call | flops 40000000 | bytes 4096 | tf_op jit(solution)/shard_map/mixed_rows/pallas_call | solution.py:829
  303.9 6.2 %collective-permute-done.45 = bf16[128,800]{1,0:T(8,128)(2,1)S(1)} collective-permute-done((bf16[128,800]{1,0:T(8,128)(2,1)}, bf16[128,800]{1,0:T(8,128)(2,1)S(1)}, u32[]{:S(2)}, u32[]{:S(2)}) %collective-permute-start.45) | collective-permute-done | bytes 204832 | tf_op jit(solution)/shard_map/ppermute | solution.py:47
  310.1 3.3 %collective-permute-done.43 = bf16[128,800]{1,0:T(8,128)(2,1)S(1)} collective-permute-done((bf16[128,800]{1,0:T(8,128)(2,1)}, bf16[128,800]{1,0:T(8,128)(2,1)S(1)}, u32[]{:S(2)}, u32[]{:S(2)}) %collective-permute-start.43) | collective-permute-done | bytes 204832 | tf_op jit(solution)/shard_map/ppermute | solution.py:973
  (227 shorter events, 92.4 us)
Async XLA Ops:
  2.6 13.2 %collective-permute-start.2 = (bf16[104,1600]{1,0:T(8,128)(2,1)S(1)}, bf16[104,1600]{1,0:T(8,128)(2,1)}, u32[]{:S(2)}, u32[]{:S(2)}) collective-permute-start(bf16[104,1600]{1,0:T(8,128)(2,1)S(1)} %pad.23), channel_id=1, source_target_pairs={{0,2},{2,0},{4,6},{6,4},{1,3},{3,1},{5,7},{7,5},{8,10},{10,8},{12,... | collective-permute-start | bytes 998408 | tf_op jit(solution)/shard_map/ppermute | solution.py:51
  19.0 27.9 %collective-permute-start.5 = (bf16[104,1600]{1,0:T(8,128)(2,1)}, bf16[104,1600]{1,0:T(8,128)(2,1)}, u32[]{:S(2)}, u32[]{:S(2)}) collective-permute-start(bf16[104,1600]{1,0:T(8,128)(2,1)} %collective-permute-done.2), channel_id=1, source_target_pairs={{2,4},{4,2},{3,5},{5,3},{10,12},{12,10},{11,13},{13,11},{18,20},{2... | collective-permute-start | bytes 998408 | tf_op jit(solution)/shard_map/ppermute | solution.py:51
  20.4 26.5 %collective-permute-start.6 = (bf16[104,1600]{1,0:T(8,128)(2,1)}, bf16[104,1600]{1,0:T(8,128)(2,1)}, u32[]{:S(2)}, u32[]{:S(2)}) collective-permute-start(bf16[104,1600]{1,0:T(8,128)(2,1)} %collective-permute-done.2), channel_id=1, source_target_pairs={{4,0},{2,6},{5,1},{3,7},{12,8},{10,14},{13,9},{11,15},{20,16},{18,... | collective-permute-start | bytes 998408 | tf_op jit(solution)/shard_map/ppermute | solution.py:51
  27.4 19.5 %collective-permute-start.4 = (bf16[104,1600]{1,0:T(8,128)(2,1)}, bf16[104,1600]{1,0:T(8,128)(2,1)S(1)}, u32[]{:S(2)}, u32[]{:S(2)}) collective-permute-start(bf16[104,1600]{1,0:T(8,128)(2,1)} %collective-permute-done.3), channel_id=1, source_target_pairs={{2,0},{4,6},{3,1},{5,7},{10,8},{12,14},{11,9},{13,15},{18,16},{20,... | collective-permute-start | bytes 998408 | tf_op jit(solution)/shard_map/ppermute | solution.py:51
  28.8 21.5 %collective-permute-start.8 = (bf16[56,1600]{1,0:T(8,128)(2,1)S(1)}, bf16[56,1600]{1,0:T(8,128)(2,1)S(1)}, u32[]{:S(2)}, u32[]{:S(2)}) collective-permute-start(bf16[56,1600]{1,0:T(8,128)(2,1)S(1)} %slice.39), channel_id=1, source_target_pairs={{0,8},{8,0},{16,24},{24,16},{1,9},{9,1},{17,25},{25,17},{2,10},{10... | collective-permute-start | bytes 537608 | tf_op jit(solution)/shard_map/ppermute | solution.py:43
  30.3 19.9 %collective-permute-start.7 = (bf16[48,1600]{1,0:T(8,128)(2,1)S(1)}, bf16[48,1600]{1,0:T(8,128)(2,1)S(1)}, u32[]{:S(2)}, u32[]{:S(2)}) collective-permute-start(bf16[48,1600]{1,0:T(8,128)(2,1)S(1)} %slice.38), channel_id=1, source_target_pairs={{0,16},{16,0},{8,24},{24,8},{1,17},{17,1},{9,25},{25,9},{2,18},{18... | collective-permute-start | bytes 460808 | tf_op jit(solution)/shard_map/ppermute | solution.py:47
  56.6 34.2 %collective-permute-start.10 = (bf16[416,1600]{1,0:T(8,128)(2,1)}, bf16[416,1600]{1,0:T(8,128)(2,1)}, u32[]{:S(2)}, u32[]{:S(2)}) collective-permute-start(bf16[416,1600]{1,0:T(8,128)(2,1)} %pad_maximum_fusion.1.rest_0_), channel_id=1, source_target_pairs={{0,16},{16,0},{8,24},{24,8},{1,17},{17,1},{9,25},{25,9},{2,18},{18... | collective-permute-start | bytes 3993608 | tf_op jit(solution)/shard_map/ppermute | solution.py:47
  57.1 33.7 %collective-permute-start.9 = (bf16[416,1600]{1,0:T(8,128)(2,1)}, bf16[416,1600]{1,0:T(8,128)(2,1)}, u32[]{:S(2)}, u32[]{:S(2)}) collective-permute-start(bf16[416,1600]{1,0:T(8,128)(2,1)} %pad_maximum_fusion.1.rest_0_), channel_id=1, source_target_pairs={{0,8},{8,0},{16,24},{24,16},{1,9},{9,1},{17,25},{25,17},{2,10},{10... | collective-permute-start | bytes 3993608 | tf_op jit(solution)/shard_map/ppermute | solution.py:43
  63.2 25.5 %collective-permute-start.14 = (bf16[104,1600]{1,0:T(8,128)(2,1)}, bf16[104,1600]{1,0:T(8,128)(2,1)}, u32[]{:S(2)}, u32[]{:S(2)}) collective-permute-start(bf16[104,1600]{1,0:T(8,128)(2,1)} %collective-permute-done.11), channel_id=1, source_target_pairs={{2,4},{4,2},{3,5},{5,3},{10,12},{12,10},{11,13},{13,11},{18,20},{2... | collective-permute-start | bytes 998408 | tf_op jit(solution)/shard_map/ppermute | solution.py:51
  64.6 24.1 %collective-permute-start.15 = (bf16[104,1600]{1,0:T(8,128)(2,1)}, bf16[104,1600]{1,0:T(8,128)(2,1)}, u32[]{:S(2)}, u32[]{:S(2)}) collective-permute-start(bf16[104,1600]{1,0:T(8,128)(2,1)} %collective-permute-done.11), channel_id=1, source_target_pairs={{4,0},{2,6},{5,1},{3,7},{12,8},{10,14},{13,9},{11,15},{20,16},{18,... | collective-permute-start | bytes 998408 | tf_op jit(solution)/shard_map/ppermute | solution.py:51
  66.4 22.2 %collective-permute-start.13 = (bf16[104,1600]{1,0:T(8,128)(2,1)}, bf16[104,1600]{1,0:T(8,128)(2,1)S(1)}, u32[]{:S(2)}, u32[]{:S(2)}) collective-permute-start(bf16[104,1600]{1,0:T(8,128)(2,1)} %collective-permute-done.12), channel_id=1, source_target_pairs={{2,0},{4,6},{3,1},{5,7},{10,8},{12,14},{11,9},{13,15},{18,16},{20,... | collective-permute-start | bytes 998408 | tf_op jit(solution)/shard_map/ppermute | solution.py:51
  90.9 44.7 %collective-permute-start.21 = (bf16[416,1600]{1,0:T(8,128)(2,1)}, bf16[416,1600]{1,0:T(8,128)(2,1)}, u32[]{:S(2)}, u32[]{:S(2)}) collective-permute-start(bf16[416,1600]{1,0:T(8,128)(2,1)} %constant_dynamic-update-slice_fusion.rest_0_), channel_id=1, source_target_pairs={{0,2},{2,0},{4,6},{6,4},{1,3},{3,1},{5,7},{7,5},{8,10},{10,8},{12,... | collective-permute-start | bytes 3993608 | tf_op jit(solution)/shard_map/ppermute | solution.py:51
  91.5 44.0 %collective-permute-start.22 = (bf16[416,1600]{1,0:T(8,128)(2,1)}, bf16[416,1600]{1,0:T(8,128)(2,1)}, u32[]{:S(2)}, u32[]{:S(2)}) collective-permute-start(bf16[416,1600]{1,0:T(8,128)(2,1)} %constant_dynamic-update-slice_fusion.rest_0_), channel_id=1, source_target_pairs={{2,4},{4,2},{3,5},{5,3},{10,12},{12,10},{11,13},{13,11},{18,20},{2... | collective-permute-start | bytes 3993608 | tf_op jit(solution)/shard_map/ppermute | solution.py:51
  93.3 23.9 %collective-permute-start.18 = (bf16[1024,896]{1,0:T(8,128)(2,1)S(1)}, bf16[1024,896]{1,0:T(8,128)(2,1)}, u32[]{:S(2)}, u32[]{:S(2)}) collective-permute-start(bf16[1024,896]{1,0:T(8,128)(2,1)S(1)} %copy-done), channel_id=1, source_target_pairs={{0,1},{1,0},{2,3},{3,2},{4,5},{5,4},{6,7},{7,6},{8,9},{9,8},{10,11... | collective-permute-start | bytes 5505032 | tf_op jit(solution)/shard_map/ppermute | solution.py:55
  95.4 21.9 %collective-permute-start.16 = (bf16[208,1600]{1,0:T(8,128)(2,1)}, bf16[208,1600]{1,0:T(8,128)(2,1)}, u32[]{:S(2)}, u32[]{:S(2)}) collective-permute-start(bf16[208,1600]{1,0:T(8,128)(2,1)} %slice.43), channel_id=1, source_target_pairs={{0,16},{16,0},{8,24},{24,8},{1,17},{17,1},{9,25},{25,9},{2,18},{18... | collective-permute-start | bytes 1996808 | tf_op jit(solution)/shard_map/ppermute | solution.py:47
  98.4 18.8 %collective-permute-start.17 = (bf16[208,1600]{1,0:T(8,128)(2,1)}, bf16[208,1600]{1,0:T(8,128)(2,1)}, u32[]{:S(2)}, u32[]{:S(2)}) collective-permute-start(bf16[208,1600]{1,0:T(8,128)(2,1)} %slice.44), channel_id=1, source_target_pairs={{0,8},{8,0},{16,24},{24,16},{1,9},{9,1},{17,25},{25,17},{2,10},{10... | collective-permute-start | bytes 1996808 | tf_op jit(solution)/shard_map/ppermute | solution.py:43
  117.2 38.5 %collective-permute-start.19 = (bf16[416,1600]{1,0:T(8,128)(2,1)S(1)}, bf16[416,1600]{1,0:T(8,128)(2,1)S(1)}, u32[]{:S(2)}, u32[]{:S(2)}) collective-permute-start(bf16[416,1600]{1,0:T(8,128)(2,1)S(1)} %pad_maximum_fusion.2.rest_0_), channel_id=1, source_target_pairs={{0,8},{8,0},{16,24},{24,16},{1,9},{9,1},{17,25},{25,17},{2,10},{10... | collective-permute-start | bytes 3993608 | tf_op jit(solution)/shard_map/ppermute | solution.py:43
  117.9 37.9 %collective-permute-start.20 = (bf16[416,1600]{1,0:T(8,128)(2,1)S(1)}, bf16[416,1600]{1,0:T(8,128)(2,1)}, u32[]{:S(2)}, u32[]{:S(2)}) collective-permute-start(bf16[416,1600]{1,0:T(8,128)(2,1)S(1)} %pad_maximum_fusion.2.rest_0_), channel_id=1, source_target_pairs={{0,16},{16,0},{8,24},{24,8},{1,17},{17,1},{9,25},{25,9},{2,18},{18... | collective-permute-start | bytes 3993608 | tf_op jit(solution)/shard_map/ppermute | solution.py:47
  135.6 20.1 %collective-permute-start.23 = (bf16[104,1280]{1,0:T(8,128)(2,1)S(1)}, bf16[104,1280]{1,0:T(8,128)(2,1)S(1)}, u32[]{:S(2)}, u32[]{:S(2)}) collective-permute-start(bf16[104,1280]{1,0:T(8,128)(2,1)S(1)} %fusion.49), channel_id=1, source_target_pairs={{0,2},{2,0},{4,6},{6,4},{1,3},{3,1},{5,7},{7,5},{8,10},{10,8},{12,... | collective-permute-start | bytes 798728 | tf_op jit(solution)/shard_map/ppermute | solution.py:51
  137.6 18.1 %collective-permute-start.24 = (bf16[104,1280]{1,0:T(8,128)(2,1)S(1)}, bf16[104,1280]{1,0:T(8,128)(2,1)S(1)}, u32[]{:S(2)}, u32[]{:S(2)}) collective-permute-start(bf16[104,1280]{1,0:T(8,128)(2,1)S(1)} %fusion.49), channel_id=1, source_target_pairs={{2,4},{4,2},{3,5},{5,3},{10,12},{12,10},{11,13},{13,11},{18,20},{2... | collective-permute-start | bytes 798728 | tf_op jit(solution)/shard_map/ppermute | solution.py:51
  155.8 23.3 %collective-permute-start.28 = (bf16[104,1280]{1,0:T(8,128)(2,1)S(1)}, bf16[104,1280]{1,0:T(8,128)(2,1)S(1)}, u32[]{:S(2)}, u32[]{:S(2)}) collective-permute-start(bf16[104,1280]{1,0:T(8,128)(2,1)S(1)} %collective-permute-done.24), channel_id=1, source_target_pairs={{2,0},{4,6},{3,1},{5,7},{10,8},{12,14},{11,9},{13,15},{18,16},{20,... | collective-permute-start | bytes 798728 | tf_op jit(solution)/shard_map/ppermute | solution.py:51
  157.1 22.1 %collective-permute-start.29 = (bf16[104,1280]{1,0:T(8,128)(2,1)S(1)}, bf16[104,1280]{1,0:T(8,128)(2,1)S(1)}, u32[]{:S(2)}, u32[]{:S(2)}) collective-permute-start(bf16[104,1280]{1,0:T(8,128)(2,1)S(1)} %collective-permute-done.23), channel_id=1, source_target_pairs={{2,4},{4,2},{3,5},{5,3},{10,12},{12,10},{11,13},{13,11},{18,20},{2... | collective-permute-start | bytes 798728 | tf_op jit(solution)/shard_map/ppermute | solution.py:51
  157.7 21.4 %collective-permute-start.30 = (bf16[104,1280]{1,0:T(8,128)(2,1)S(1)}, bf16[104,1280]{1,0:T(8,128)(2,1)S(1)}, u32[]{:S(2)}, u32[]{:S(2)}) collective-permute-start(bf16[104,1280]{1,0:T(8,128)(2,1)S(1)} %collective-permute-done.23), channel_id=1, source_target_pairs={{4,0},{2,6},{5,1},{3,7},{12,8},{10,14},{13,9},{11,15},{20,16},{18,... | collective-permute-start | bytes 798728 | tf_op jit(solution)/shard_map/ppermute | solution.py:51
  159.1 20.2 %collective-permute-start.26 = (bf16[208,1600]{1,0:T(8,128)(2,1)S(1)}, bf16[208,1600]{1,0:T(8,128)(2,1)S(1)}, u32[]{:S(2)}, u32[]{:S(2)}) collective-permute-start(bf16[208,1600]{1,0:T(8,128)(2,1)S(1)} %slice.45), channel_id=1, source_target_pairs={{0,16},{16,0},{8,24},{24,8},{1,17},{17,1},{9,25},{25,9},{2,18},{18... | collective-permute-start | bytes 1996808 | tf_op jit(solution)/shard_map/ppermute | solution.py:47
  161.1 18.2 %collective-permute-start.27 = (bf16[208,1600]{1,0:T(8,128)(2,1)S(1)}, bf16[208,1600]{1,0:T(8,128)(2,1)S(1)}, u32[]{:S(2)}, u32[]{:S(2)}) collective-permute-start(bf16[208,1600]{1,0:T(8,128)(2,1)S(1)} %slice.46), channel_id=1, source_target_pairs={{0,8},{8,0},{16,24},{24,16},{1,9},{9,1},{17,25},{25,17},{2,10},{10... | collective-permute-start | bytes 1996808 | tf_op jit(solution)/shard_map/ppermute | solution.py:43
  179.3 25.1 %collective-permute-start.33 = (bf16[416,1280]{1,0:T(8,128)(2,1)S(1)}, bf16[416,1280]{1,0:T(8,128)(2,1)S(1)}, u32[]{:S(2)}, u32[]{:S(2)}) collective-permute-start(bf16[416,1280]{1,0:T(8,128)(2,1)S(1)} %pad_maximum_fusion.3.rest_0_), channel_id=1, source_target_pairs={{0,8},{8,0},{16,24},{24,16},{1,9},{9,1},{17,25},{25,17},{2,10},{10... | collective-permute-start | bytes 3194888 | tf_op jit(solution)/shard_map/ppermute | solution.py:43
  179.9 24.7 %collective-permute-start.34 = (bf16[416,1280]{1,0:T(8,128)(2,1)S(1)}, bf16[416,1280]{1,0:T(8,128)(2,1)S(1)}, u32[]{:S(2)}, u32[]{:S(2)}) collective-permute-start(bf16[416,1280]{1,0:T(8,128)(2,1)S(1)} %pad_maximum_fusion.3.rest_0_), channel_id=1, source_target_pairs={{0,16},{16,0},{8,24},{24,8},{1,17},{17,1},{9,25},{25,9},{2,18},{18... | collective-permute-start | bytes 3194888 | tf_op jit(solution)/shard_map/ppermute | solution.py:47
  181.2 37.8 %collective-permute-start.31 = (bf16[416,1600]{1,0:T(8,128)(2,1)}, bf16[416,1600]{1,0:T(8,128)(2,1)}, u32[]{:S(2)}, u32[]{:S(2)}) collective-permute-start(bf16[416,1600]{1,0:T(8,128)(2,1)} %collective-permute-done.21.rest_1_), channel_id=1, source_target_pairs={{2,4},{4,2},{3,5},{5,3},{10,12},{12,10},{11,13},{13,11},{18,20},{2... | collective-permute-start | bytes 3993608 | tf_op jit(solution)/shard_map/ppermute | solution.py:51
  183.0 37.0 %collective-permute-start.32 = (bf16[416,1600]{1,0:T(8,128)(2,1)}, bf16[416,1600]{1,0:T(8,128)(2,1)}, u32[]{:S(2)}, u32[]{:S(2)}) collective-permute-start(bf16[416,1600]{1,0:T(8,128)(2,1)} %collective-permute-done.22.rest_4_), channel_id=1, source_target_pairs={{2,0},{4,6},{3,1},{5,7},{10,8},{12,14},{11,9},{13,15},{18,16},{20,... | collective-permute-start | bytes 3993608 | tf_op jit(solution)/shard_map/ppermute | solution.py:51
  205.6 14.3 %collective-permute-start.35 = (bf16[208,1280]{1,0:T(8,128)(2,1)}, bf16[208,1280]{1,0:T(8,128)(2,1)S(1)}, u32[]{:S(2)}, u32[]{:S(2)}) collective-permute-start(bf16[208,1280]{1,0:T(8,128)(2,1)} %slice.47), channel_id=1, source_target_pairs={{0,16},{16,0},{8,24},{24,8},{1,17},{17,1},{9,25},{25,9},{2,18},{18... | collective-permute-start | bytes 1597448 | tf_op jit(solution)/shard_map/ppermute | solution.py:47
  220.2 34.1 %collective-permute-start.37 = (bf16[416,1600]{1,0:T(8,128)(2,1)}, bf16[416,1600]{1,0:T(8,128)(2,1)S(1)}, u32[]{:S(2)}, u32[]{:S(2)}) collective-permute-start(bf16[416,1600]{1,0:T(8,128)(2,1)} %collective-permute-done.21.rest_1_), channel_id=1, source_target_pairs={{4,0},{2,6},{5,1},{3,7},{12,8},{10,14},{13,9},{11,15},{20,16},{18,... | collective-permute-start | bytes 3993608 | tf_op jit(solution)/shard_map/ppermute | solution.py:51
  290.1 13.3 %collective-permute-start.46 = (bf16[128,800]{1,0:T(8,128)(2,1)}, bf16[128,800]{1,0:T(8,128)(2,1)S(1)}, u32[]{:S(2)}, u32[]{:S(2)}) collective-permute-start(bf16[128,800]{1,0:T(8,128)(2,1)} %get-tuple-element.179), channel_id=1, source_target_pairs={{0,8},{8,0},{16,24},{24,16},{1,9},{9,1},{17,25},{25,17},{2,10},{10... | collective-permute-start | bytes 614408 | tf_op jit(solution)/shard_map/ppermute | solution.py:43
  (58 other events, 743.3 us)

commit v3 on v2

--- a/solution.py
+++ b/solution.py
@@ -285,7 +285,10 @@
             for first in range(0, states, 4):
                 part = None
                 for n in range(first, first + 4):
-                    held[n] = jnp.exp2(size * spread(rate_scratch, n)) * held[n] + drive * in_mix[n, here, :]
+                    held[n] = (
+                        jnp.exp2(size * spread(rate_scratch, n)) * held[n]
+                        + drive * in_mix[n, here, :]
+                    )
                     term = held[n] * out_mix[n, here, :]
                     part = term if part is None else part + term
                 part = part.astype(jnp.float32)
@@ -339,10 +342,9 @@
     send[...] = transposed_dot(attended, weight[columns:, :])
 
 
-def ssm_out_kernel(slot_choices, part, summed, scalars, gated, *rest):
-    ready, rest = rest[:summed], rest[summed:]
+def ssm_out_kernel(slot_choices, part, scalars, gated, *rest):
     count = sum(slot_choices)
-    pieces, (keep, send, *sums, weight, sems) = rest[:count], rest[count:]
+    pieces, (keep, send, weight, sems) = rest[:count], rest[count:]
     wide = weight.shape[0] // 2
     filled = part * len(slot_choices)
     second = scalars[0]
@@ -385,9 +387,6 @@
     value = gated[...]
     send[...] = transposed_dot(value, weight[wide:, :])
     keep[...] = transposed_dot(value, weight[:wide, :])
-    if ready:
-        sums[0][:, 0:1] = square_sum(ready[0], ready[1])
-        sums[0][:, 1:2] = square_sum(ready[2], ready[3])
 
 
 def square_sum(keep, got):
@@ -397,12 +396,11 @@
 
 def square_kernel(*refs):
     *refs, out = refs
-    if len(refs) == 4:
-        out[:, 0:1] = square_sum(refs[0], refs[1])
-        out[:, 1:2] = square_sum(refs[2], refs[3])
-    else:
-        out[:, 0:1] = refs[0][:, 0:1]
-        out[:, 1:2] = refs[0][:, 1:2] + square_sum(refs[1], refs[2])
+    out[:, 0:1] = square_sum(refs[0], refs[1])
+    total = square_sum(refs[2], refs[3])
+    for index in range(4, len(refs), 2):
+        total += square_sum(refs[index], refs[index + 1])
+    out[:, 1:2] = total
 
 
 def mixed_kernel(slots, first, sections, here, proc, sizes, x_keep, keep_attn, got_attn, *rest):
@@ -509,9 +507,11 @@
 
     ssm_shard = padded(w_ssm_out.T)
     conv_shard = padded(w_inner[:, 0])
-    gate_shard = padded(w_inner[:, 1])
-    attn_shard = padded(jnp.concatenate([w_query, w_keyval, w_attn_out.T], axis=1))
+    def shard_behind(w_query, w_keyval, w_attn_out, w_gate):
+        return padded(jnp.concatenate([w_query, w_keyval, w_attn_out.T, w_gate], axis=1))
+
     qkv_width = w_query.shape[1] + w_keyval.shape[1]
+    attn_width = qkv_width + heads_width
     rank, states = dt_weight.shape[0], decay_log.shape[0]
     mixes = 256
 
@@ -540,9 +540,10 @@
         return jnp.where((offset < shard) & inside, block * shard + offset, -1)
 
     def picker(shape, column_dim, lines_outside, rep, row):
-        column = lax.broadcasted_iota(i32, shape, column_dim)
-        feature = lax.broadcasted_iota(i32, shape, 1 - column_dim)
-        return feature == feature_at(column, lines_outside, rep, row)
+        line = tuple(size if dim == column_dim else 1 for dim, size in enumerate(shape))
+        column = lax.broadcasted_iota(i32, line, column_dim)
+        (source,) = tie(feature_at(column, lines_outside, rep, row))
+        return lax.broadcasted_iota(i32, shape, 1 - column_dim) == source
 
     def column_picks(rep, row):
         keep_pick = picker((width, columns), 1, True, rep, row)
@@ -743,9 +744,9 @@
             *earlier,
         )
 
-    def gate(rows_own, rows_other, scanned, pieces):
+    def gate(rows_own, rows_other, scanned, pieces, first_column):
         return call(
-            functools.partial(gate_kernel, len(pieces), half, 0),
+            functools.partial(gate_kernel, len(pieces), half, first_column),
             1,
             rows // tile,
             [row_block(wide)] * 2 + [row_block(channels)] + [anywhere] * len(pieces),
@@ -785,42 +786,35 @@
             "attn_out",
         )(second, heads, *pieces)
 
-    def ssm_out(gated, choices, pieces, ready=()):
+    def ssm_out(gated, choices, pieces):
         scalars = jnp.stack([second[0], inner.astype(i32) if by_links else second[0]])
-        sums = 1 if ready else 0
         return call(
-            functools.partial(ssm_out_kernel, choices, section // len(choices), len(ready)),
+            functools.partial(ssm_out_kernel, choices, section // len(choices)),
             1,
             rows // tile,
-            [row_block(channels)]
-            + [row_block(value.shape[1]) for value in ready]
-            + [anywhere] * len(pieces),
-            [row_block(section_wide)] * 2 + [row_block(2)] * sums,
-            [rows_of(section_wide)] * 2 + [rows_of(2, f32)] * sums,
+            [row_block(channels)] + [anywhere] * len(pieces),
+            [row_block(section_wide)] * 2,
+            [rows_of(section_wide)] * 2,
             [
                 pltpu.VMEM((2 * section_wide, channels), bf16),
                 pltpu.SemaphoreType.DMA((len(choices), 2)),
             ],
             8,
             "ssm_out",
-        )(scalars, gated, *ready, *pieces)
-
-    def squares(attn, ssm, earlier=None):
-        if earlier is not None:
-            operands, specs = [earlier], [row_block(2)]
-        else:
-            operands, specs = list(attn), [row_block(columns)] * 2
+        )(scalars, gated, *pieces)
+
+    def squares(attn, ssm):
         return call(
             square_kernel,
             0,
             rows // tile,
-            specs + [row_block(section_wide)] * 2,
+            [row_block(columns)] * 2 + [row_block(section_wide)] * len(ssm),
             row_block(2),
             rows_of(2, f32),
             [],
             2,
             "squares",
-        )(*operands, *ssm)
+        )(*attn, *ssm)
 
     def mix(part, x_keep, attn, ssm, own_squares, other_squares, gains, features_back, sizes):
         here = groups // pairs
@@ -878,73 +872,113 @@
             cut = by_x.shape[0] // 16 * 8
             return swap_y(by_x[:cut]), swap_x(by_y[cut:])
 
-        ssm_p1 = plane_first(ssm_shard)
+        def upper(value, first):
+            return jnp.concatenate([value, first[0]], axis=0)
+
+        def lower(first, last):
+            crossed, ends, far = last
+            return jnp.concatenate(
+                [jnp.where(inner, first[1], ends), jnp.where(inner, crossed, far)], axis=0
+            )
+
+        def left(values):
+            return tuple(value[:, :attn_width] for value in values)
+
+        def right(values):
+            return tuple(value[:, attn_width:] for value in values)
+
+        ssm_plane = plane_first(ssm_shard) + (lax.ppermute(ssm_shard, "rep", D_PAIRS),)
         conv_z1 = line_first(conv_shard)
-
-        ssm_p1, conv_z1, tokens_late, serve_late, rep_late, row_late = tie(
-            ssm_p1, conv_z1, tokens, serve_replica, rep, row
-        )
-        ssm_p2 = plane_second(ssm_p1)
+        inv_rms = inverse_rms(tokens)
+
+        ssm_x, ssm_y, ssm_corner = ssm_plane
+        (
+            conv_z1,
+            conv_shard,
+            ssm_x,
+            ssm_y,
+            inv_rms,
+            serve_late,
+            rep_late,
+            row_late,
+            late_weights,
+        ) = tie(
+            conv_z1,
+            conv_shard,
+            ssm_x,
+            ssm_y,
+            inv_rms,
+            serve_replica,
+            rep,
+            row,
+            (w_query, w_keyval, w_attn_out, w_inner[:, 1]),
+        )
         conv_z2 = line_second(conv_z1)
+        conv_top_own = upper(conv_shard, conv_z1)
+        conv_top = plane_first(conv_top_own)
         proc = group_order(serve_late)
-        rows_own = spread(inverse_rms(tokens_late), rep_late, row_late)
-
-        conv_block = line_block(conv_shard, conv_z1, conv_z2)
-        conv_block, ssm_p2, gate_shard, rows_own = tie(conv_block, ssm_p2, gate_shard, rows_own)
-        conv_p1 = plane_first(conv_block)
-        gate_z1 = line_first(gate_shard)
-        gate_z1, plain = tie(gate_z1, plain)
-        gate_z2 = line_second(gate_z1)
+        rows_own = spread(inv_rms, rep_late, row_late)
+        back_shard = shard_behind(*late_weights)
+
+        conv_bottom_own = lower(conv_z1, conv_z2)
+        conv_top, conv_bottom_own, back_shard, rows_own, plain, rep_late, row_late, ssm_corner = tie(
+            conv_top, conv_bottom_own, back_shard, rows_own, plain, rep, row, ssm_corner
+        )
+        ssm_plane = (ssm_x, ssm_y, ssm_corner)
+        conv_bottom = plane_first(conv_bottom_own)
+        back_z1 = line_first(back_shard)
+        rows_other = other_core(rows_own)
         small = small_operands(*plain)
-
-        ssm_block = jnp.concatenate((ssm_shard,) + tuple(ssm_p1) + tuple(ssm_p2), axis=0)
-        gate_block = line_block(gate_shard, gate_z1, gate_z2)
-        conv_p1, gate_block, ssm_block, rows_own, rep_late, row_late, small = tie(
-            conv_p1, gate_block, ssm_block, rows_own, rep, row, small
-        )
-        conv_p2 = plane_second(conv_p1)
+        picks = column_picks(rep_late, row_late)
+
+        conv_top, conv_bottom, back_z1, small, rows_other, ssm_plane, picks = tie(
+            conv_top, conv_bottom, back_z1, small, rows_other, ssm_plane, picks
+        )
+        keep_pick, gains, features_back = picks
+        conv_corner = (swap_y(conv_top[0]), swap_x(conv_bottom[1]))
+        back_z2 = line_second(back_z1)
+        ssm_block = jnp.concatenate((ssm_shard,) + ssm_plane, axis=0)
+        x_keep = place(keep_pick)
+
+        conv_corner, ssm_block, x_keep, gains, features_back = tie(
+            conv_corner, ssm_block, x_keep, gains, features_back
+        )
+        conv_out, mix_own = convolve(
+            rows_own,
+            rows_other,
+            (conv_top_own, conv_bottom_own, conv_top[0], conv_bottom[0], conv_top[1], conv_bottom[1])
+            + conv_corner,
+            small,
+        )
+
+        conv_out, mix_own, back_z2, ssm_block = tie(conv_out, mix_own, back_z2, ssm_block)
+        gate_block = line_block(right((back_shard,))[0], right(back_z1), right(back_z2))
+        gate_p1 = plane_first(gate_block)
         ssm_near, ssm_middle = line_first(ssm_block)
-        rows_other = other_core(rows_own)
-        keep_pick, gains, features_back = column_picks(rep_late, row_late)
-        x_keep = place(keep_pick)
-
-        conv_p2, gate_block, rows_other, attn_shard, x_keep, gains, features_back = tie(
-            conv_p2, gate_block, rows_other, attn_shard, x_keep, gains, features_back
-        )
-        gate_p1 = plane_first(gate_block)
-        conv_out, mix_own = convolve(
-            rows_own, rows_other, (conv_block,) + tuple(conv_p1) + tuple(conv_p2), small
-        )
-        conv_out, mix_own, ssm_near, ssm_middle, attn_shard = tie(
-            conv_out, mix_own, ssm_near, ssm_middle, attn_shard
-        )
         mix_other = other_core(mix_own)
-        attn_z1 = line_first(attn_shard)
         count = groups // 2
         scanned = scan(0, count, conv_out, mix_own, mix_other, small)
 
-        gate_p1, attn_z1, scanned = tie(gate_p1, attn_z1, scanned)
+        gate_p1, scanned, ssm_near, ssm_middle = tie(gate_p1, scanned, ssm_near, ssm_middle)
         gate_p2 = plane_second(gate_p1)
-        attn_z2 = line_second(attn_z1)
+        crossed = along_z(ssm_near, Z_INNER)
+        ends = along_z(ssm_middle, Z_ENDS)
         scanned = scan(
             count, groups - count, conv_out, mix_own, mix_other, small, (scanned,)
         )
-        attn_block = line_block(attn_shard, attn_z1, attn_z2)
-
-        gate_p2, attn_block, ssm_near, ssm_middle, scanned = tie(
-            gate_p2, attn_block, ssm_near, ssm_middle, scanned
-        )
+        attn_block = line_block(left((back_shard,))[0], left(back_z1), left(back_z2))
+
+        gate_p2, attn_block, scanned = tie(gate_p2, attn_block, scanned)
         attn_p1 = plane_first(attn_block)
-        crossed = along_z(ssm_near, Z_INNER)
-        ends = along_z(ssm_middle, Z_ENDS)
-        gated = gate(rows_own, rows_other, scanned, (gate_block,) + tuple(gate_p1) + tuple(gate_p2))
-
-        attn_p1, gated = tie(attn_p1, gated)
+        gated = gate(
+            rows_own, rows_other, scanned, (gate_block,) + tuple(gate_p1) + tuple(gate_p2), 0
+        )
+        keep_early, send_early = ssm_out(gated, (1, 1), (ssm_block, ssm_near))
+
+        attn_p1, keep_early, crossed, ends, ssm_near = tie(
+            attn_p1, keep_early, crossed, ends, ssm_near
+        )
         attn_p2 = plane_second(attn_p1)
-        keep_early, send_early = ssm_out(gated, (1, 1), (ssm_block, ssm_near))
-        crossed, ends, ssm_near, keep_early, attn_p2, attn_block = tie(
-            crossed, ends, ssm_near, keep_early, attn_p2, attn_block
-        )
         far = along_z(ssm_near, Z_FAR)
         got_early = other_core(send_early)
         attn_pieces = (attn_block,) + tuple(attn_p1) + tuple(attn_p2)
@@ -955,13 +989,11 @@
         attn = [keep_attn, got_attn]
 
         late_pieces = (ssm_middle, ends, crossed, far)
-        keep_late, send_late, sums = ssm_out(
-            gated, (2, 2), late_pieces, attn + [keep_early, got_early]
-        )
+        keep_late, send_late = ssm_out(gated, (2, 2), late_pieces)
         got_late = other_core(send_late)
-        sums = squares(attn, [keep_late, got_late], sums)
+        ssm = [keep_early, got_early, keep_late, got_late]
+        sums = squares(attn, ssm)
         other_sums = other_core(sums)
-        ssm = [keep_early, got_early, keep_late, got_late]
         received = []
         for part in range(pairs):
             mixed = mix(part, x_keep, attn, ssm, sums, other_sums, gains, features_back, small[6])
@@ -992,11 +1024,11 @@
         rows_other = other_core(rows_own)
         keep_pick, gains, features_back = column_picks(rep, row)
         x_keep = place(keep_pick)
-        attn_pieces = (gathered(attn_shard),)
+        attn_pieces = (gathered(shard_behind(w_query, w_keyval, w_attn_out, w_inner[:, 1])),)
         heads = attention(rows_own, rows_other, attn_pieces, small[5])
         conv_out, mix_own = convolve(rows_own, rows_other, (gathered(conv_shard),), small)
         scanned = scan(0, groups, conv_out, mix_own, other_core(mix_own), small)
-        gated = gate(rows_own, rows_other, scanned, (gathered(gate_shard),))
+        gated = gate(rows_own, rows_other, scanned, attn_pieces, attn_width)
         keep_attn, send_attn = attn_out(heads, attn_pieces)
         attn = [keep_attn, other_core(send_attn)]
         kept, sent = ssm_out(gated, (1,), (gathered(ssm_shard),))

time: 319 us -> 307 us (0.962)
  waiting for transfers between devices: 61.2 us -> 51.9 us
  other arithmetic: 25.9 us -> 19.9 us
  starting transfers between devices: 58.1 us -> 63.9 us
  local copies, waits for them, and re-layouts: 27.1 us -> 23.1 us
    ppermute x20 -> x15, waiting for transfers between devices: 30.4 us -> 7.47 us  [along_z(): return lax.ppermute(value, 'tr', pairs)]
    ppermute x10, waiting for transfers between devices: 9.3 us -> 22.2 us  [swap_x(): return lax.ppermute(value, 'rep', X_PAIRS)]
    slice x8 -> x4, local copies, waits for them, and re-layouts: 8 us -> 0.18 us  [plane_second(): return (swap_y(by_x[:cut]), swap_x(by_y[cut:]))]
    ppermute x6, waiting for transfers between devices: 10.1 us -> 4.83 us  [other_core(): return lax.ppermute(value, 'tc', ((0, 1), (1, 0)))]
    ppermute x20 -> x15, starting transfers between devices: 31.8 us -> 36 us  [along_z(): return lax.ppermute(value, 'tr', pairs)]
    ppermute x10, waiting for transfers between devices: 7.58 us -> 11.6 us  [swap_y(): return lax.ppermute(value, 'rep', Y_PAIRS)]
    slice x1 -> x5, local copies, waits for them, and re-layouts: 2.48 us -> 6.42 us  [the longest x1 2.47 us: local(): w_inner[:, 1]]
    ppermute x0 -> x1, starting transfers between devices: none -> 3.89 us  [local(): lax.ppermute(ssm_shard, 'rep', D_PAIRS)]
  transfers between devices with their start and end apart: 48 -> 44, of which waited for: 17 -> 17; matrix products, arithmetic and copies ran while one was open for 14% -> 10% of each run, Pallas kernels for 38% -> 43%
where the time goes in v3:
time: 307 us; the launch traced here: 303 us
  Pallas kernels  141 us (46%)
  starting transfers between devices  63.9 us (21%)
  waiting for transfers between devices  51.9 us (17%)
  local copies, waits for them, and re-layouts  23.1 us (8%)
  other arithmetic  19.9 us (6%)
    ppermute x15, starting transfers between devices, along_z(): return lax.ppermute(value, 'tr', pairs)  36 us
    pallas_call x2, Pallas kernels, scan(): call(functools.partial(scan_kernel, slots), 1, count, [blocks(channels),...  32.9 us
    ppermute x10, waiting for transfers between devices, swap_x(): return lax.ppermute(value, 'rep', X_PAIRS)  22.2 us
    pallas_call x2, Pallas kernels, ssm_out(): call(functools.partial(ssm_out_kernel, choices, section // len(choices)),...  18.3 us
    pallas_call x1, Pallas kernels, attention(): call(functools.partial(attention_kernel, slots, group_rows, kv_here, per_...  17.4 us
    pallas_call x1, Pallas kernels, convolve(): call(functools.partial(conv_kernel, slots, group_rows, len(pieces), half,...  15 us
    pallas_call x2, Pallas kernels, mix(): call(functools.partial(mixed_kernel, slots, part * here, sections, here),...  13.3 us
    pallas_call x1, Pallas kernels, gate(): call(functools.partial(gate_kernel, len(pieces), half, first_column), 1,...  13.1 us
  transfers between devices with their start and end apart: 44, of which 17 were waited for; matrix products, arithmetic and copies ran while one was open for 10% of the time, Pallas kernels for 43%

profile of v3, /device:TPU:0, one launch (start us, length us, event | category | flops | bytes accessed | tf_op | source)
XLA Modules:
  0.0 303.1 jit_solution(2772685409878927214)
XLA Ops:
  0.0 1.7 pad.20
  1.8 3.9 %collective-permute-start.9 = (bf16[104,1600]{1,0:T(8,128)(2,1)}, bf16[104,1600]{1,0:T(8,128)(2,1)}, u32[]{:S(2)}, u32[]{:S(2)}) collective-permute-start(bf16[104,1600]{1,0:T(8,128)(2,1)} %pad.20), channel_id=1, source_target_pairs={{0,24},{24,0},{8,16},{16,8},{1,25},{25,1},{9,17},{17,9},{2,26},{26... | collective-permute-start | bytes 998408 | tf_op jit(solution)/shard_map/ppermute | solution.py:890
  6.2 2.5 fusion.25
  9.5 4.9 %collective-permute-start = (bf16[104,1600]{1,0:T(8,128)(2,1)S(1)}, bf16[104,1600]{1,0:T(8,128)(2,1)S(1)}, u32[]{:S(2)}, u32[]{:S(2)}) collective-permute-start(bf16[104,1600]{1,0:T(8,128)(2,1)S(1)} %pad.19), channel_id=1, source_target_pairs={{0,2},{2,0},{4,6},{6,4},{1,3},{3,1},{5,7},{7,5},{8,10},{10,8},{12,... | collective-permute-start | bytes 998408 | tf_op jit(solution)/shard_map/ppermute | solution.py:51
  15.7 2.5 psum.7
  18.2 3.2 %collective-permute-done.3 = bf16[104,1600]{1,0:T(8,128)(2,1)S(1)} collective-permute-done((bf16[104,1600]{1,0:T(8,128)(2,1)}, bf16[104,1600]{1,0:T(8,128)(2,1)S(1)}, u32[]{:S(2)}, u32[]{:S(2)}) %collective-permute-start.3) | collective-permute-done | bytes 332832 | tf_op jit(solution)/shard_map/ppermute | solution.py:47
  31.0 9.6 %spread_rows.1.rows_own = bf16[1024,896]{1,0:T(8,128)(2,1)} custom-call(s32[8]{0:T(128)} %select_reduce_fusion.1.proc, bf16[8,128,800]{2,1,0:T(8,128)(2,1)} %bitcast.23, f32[8,128,1]{2,1,0:T(8,128)} %copy.37.inv_rms, f32[1,800]{1,0:T(1,128)} %broadcast_in_dim.113.gain, bf16[800,896]{1,0:T(8,128)(2,1)} %fusion.1.pick), custom_call_target="tpu_custom_call" | custom-call | flops 80000000 | bytes 4096 | tf_op jit(solution)/shard_map/spread_rows/pallas_call | solution.py:612
  45.7 13.3 %collective-permute-done.4.rest_2_ = bf16[208,1600]{1,0:T(8,128)(2,1)S(1)} collective-permute-done((bf16[208,1600]{1,0:T(8,128)(2,1)S(1)}, bf16[208,1600]{1,0:T(8,128)(2,1)S(1)}, u32[]{:S(2)}, u32[]{:S(2)}) %collective-permute-start.4) | collective-permute-done | bytes 665632 | tf_op jit(solution)/shard_map/ppermute | solution.py:43
  61.5 8.3 %collective-permute-start.12 = (bf16[104,2880]{1,0:T(8,128)(2,1)}, bf16[104,2880]{1,0:T(8,128)(2,1)}, u32[]{:S(2)}, u32[]{:S(2)}) collective-permute-start(bf16[104,2880]{1,0:T(8,128)(2,1)} %fusion.10), channel_id=1, source_target_pairs={{0,2},{2,0},{4,6},{6,4},{1,3},{3,1},{5,7},{7,5},{8,10},{10,8},{12,... | collective-permute-start | bytes 1797128 | tf_op jit(solution)/shard_map/ppermute | solution.py:51
  79.4 2.0 iota_compare_fusion.1
  83.5 3.0 collective-permute-done.11.rest_5_
  95.4 9.1 %place_rows.1.x_keep = bf16[1024,1024]{1,0:T(8,128)(2,1)} custom-call(s32[8]{0:T(128)} %select_reduce_fusion.1.proc, bf16[8,128,800]{2,1,0:T(8,128)(2,1)} %bitcast.24, bf16[800,1024]{1,0:T(8,128)(2,1)} %get-tuple-element.132.pick), custom_call_target="tpu_custom_call" | custom-call | flops 80000000 | bytes 4096 | tf_op jit(solution)/shard_map/place_rows/pallas_call | solution.py:630
  106.9 15.0 %convolve.1 = (bf16[1024,1600]{1,0:T(8,128)(2,1)}, bf16[1024,256]{1,0:T(8,128)(2,1)}) custom-call(s32[8]{0:T(128)} %select_reduce_fusion.1.proc, s32[1]{0:T(128)} %bitcast.8.second, bf16[1024,896]{1,0:T(8,128)(2,1)} %spread_rows.1.rows_own, bf16[1024,896]{1,0:T(8,128)(2,1)} %collective-permute-done.14.rows_other, f32[8,3,1600]{2,1,0:T(4,128)} %copy.40.history, ...), custom_call_target="tpu_custom_call" | custom-call | flops 140000000 | bytes 4096 | tf_op jit(solution)/shard_map/convolve/pallas_call | solution.py:678
  125.7 1.8 collective-permute-start.24
  127.4 6.3 %collective-permute-start.23 = (bf16[416,1600]{1,0:T(8,128)(2,1)S(1)}, bf16[416,1600]{1,0:T(8,128)(2,1)}, u32[]{:S(2)}, u32[]{:S(2)}) collective-permute-start(bf16[416,1600]{1,0:T(8,128)(2,1)S(1)} %pad_maximum_fusion.1.rest_0_), channel_id=1, source_target_pairs={{0,2},{2,0},{4,6},{6,4},{1,3},{3,1},{5,7},{7,5},{8,10},{10,8},{12,... | collective-permute-start | bytes 3993608 | tf_op jit(solution)/shard_map/ppermute | solution.py:51
  136.6 16.4 %scan_states.2.rest_0_ = f32[1024,1600]{1,0:T(8,128)} custom-call(s32[8]{0:T(128)} %select_reduce_fusion.1.proc, bf16[1024,1600]{1,0:T(8,128)(2,1)} %get-tuple-element.153.conv, bf16[1024,256]{1,0:T(8,128)(2,1)} %get-tuple-element.154.mix_own, bf16[1024,256]{1,0:T(8,128)(2,1)} %copy-done.17, bf16[100,1600]{1,0:T(8,128)(2,1)} %step_weight.3, ...), custom_call_target="tpu_custom_call" | custom-call | flops 160000000 | bytes 4096 | tf_op jit(solution)/shard_map/scan_states/pallas_call | solution.py:711
  154.4 6.0 %collective-permute-done.23.rest_1_ = bf16[416,1600]{1,0:T(8,128)(2,1)} collective-permute-done((bf16[416,1600]{1,0:T(8,128)(2,1)S(1)}, bf16[416,1600]{1,0:T(8,128)(2,1)}, u32[]{:S(2)}, u32[]{:S(2)}) %collective-permute-start.23) | collective-permute-done | bytes 1331232 | tf_op jit(solution)/shard_map/ppermute | solution.py:51
  165.2 1.8 collective-permute-start.29
  167.0 16.5 %scan_states.3.scanned = f32[1024,1600]{1,0:T(8,128)} custom-call(s32[8]{0:T(128)} %select_reduce_fusion.1.proc, bf16[1024,1600]{1,0:T(8,128)(2,1)} %get-tuple-element.153.conv, bf16[1024,256]{1,0:T(8,128)(2,1)} %get-tuple-element.154.mix_own, bf16[1024,256]{1,0:T(8,128)(2,1)} %copy-done.17, ...), custom_call_target="tpu_custom_call", output_to_operand_aliasing={{}: (9, {})} | custom-call | flops 160000000 | bytes 4096 | tf_op jit(solution)/shard_map/scan_states/pallas_call | solution.py:711
  187.3 13.1 %gate.1.gated = bf16[1024,1600]{1,0:T(8,128)(2,1)} custom-call(s32[1]{0:T(128)} %bitcast.8.second, bf16[1024,896]{1,0:T(8,128)(2,1)} %spread_rows.1.rows_own, bf16[1024,896]{1,0:T(8,128)(2,1)} %collective-permute-done.14.rows_other, f32[1024,1600]{1,0:T(8,128)} %scan_states.3.scanned, bf16[416,1600]{1,0:T(8,128)(2,1)} %copy-done.9, ...), custom_call_target="tpu_custom_call" | custom-call | flops 130000000 | bytes 4096 | tf_op jit(solution)/shard_map/gate/pallas_call | solution.py:748
  200.4 9.1 %ssm_out.2 = (bf16[1024,512]{1,0:T(8,128)(2,1)}, bf16[1024,512]{1,0:T(8,128)(2,1)}) custom-call(s32[2]{0:T(128)} %pad_add_fusion.scalars, bf16[1024,1600]{1,0:T(8,128)(2,1)} %gate.1.gated, bf16[416,1600]{1,0:T(8,128)(2,1)} %copy-done.8, bf16[416,1600]{1,0:T(8,128)(2,1)} %collective-permute-done.23.rest_1_), custom_call_target="tpu_custom_call" | custom-call | flops 80000000 | bytes 4096 | tf_op jit(solution)/shard_map/ssm_out/pallas_call | solution.py:791
  213.1 7.3 %collective-permute-done.32.rest_4_ = bf16[208,1280]{1,0:T(8,128)(2,1)S(1)} collective-permute-done((bf16[208,1280]{1,0:T(8,128)(2,1)S(1)}, bf16[208,1280]{1,0:T(8,128)(2,1)S(1)}, u32[]{:S(2)}, u32[]{:S(2)}) %collective-permute-start.32) | collective-permute-done | bytes 532512 | tf_op jit(solution)/shard_map/ppermute | solution.py:43
  222.3 17.4 %attention.1.heads = bf16[1024,512]{1,0:T(8,128)(2,1)} custom-call(s32[8]{0:T(128)} %select_reduce_fusion.1.proc, s32[8]{0:T(128)} %dynamic_slice.13.lengths, s32[1]{0:T(128)} %bitcast.8.second, bf16[1024,896]{1,0:T(8,128)(2,1)} %spread_rows.1.rows_own, bf16[1024,896]{1,0:T(8,128)(2,1)} %collective-permute-done.14.rows_other, bf16[8,256,256]{2,1,0:T(8,128)(2,1)} %cache.1, ...), custom_call_target="tpu_custom_call" | custom-call | flops 150000000 | bytes 4096 | tf_op jit(solution)/shard_map/attention/pallas_call | solution.py:643
  239.7 6.9 %attn_out.1 = (bf16[1024,1024]{1,0:T(8,128)(2,1)}, bf16[1024,1024]{1,0:T(8,128)(2,1)}) custom-call(s32[1]{0:T(128)} %bitcast.8.second, bf16[1024,512]{1,0:T(8,128)(2,1)} %attention.1.heads, bf16[416,1280]{1,0:T(8,128)(2,1)} %copy-done.3, bf16[416,1280]{1,0:T(8,128)(2,1)} %copy-done.7, bf16[416,1280]{1,0:T(8,128)(2,1)} %copy-done.6, ...), custom_call_target="tpu_custom_call" | custom-call | flops 60000000 | bytes 4096 | tf_op jit(solution)/shard_map/attn_out/pallas_call | solution.py:773
  247.7 9.1 %ssm_out.3 = (bf16[1024,512]{1,0:T(8,128)(2,1)}, bf16[1024,512]{1,0:T(8,128)(2,1)}) custom-call(s32[2]{0:T(128)} %pad_add_fusion.scalars, bf16[1024,1600]{1,0:T(8,128)(2,1)} %gate.1.gated, bf16[416,1600]{1,0:T(8,128)(2,1)} %collective-permute-done.24.rest_0_, bf16[416,1600]{1,0:T(8,128)(2,1)} %collective-permute-done.30.rest_1_, ...), custom_call_target="tpu_custom_call" | custom-call | flops 80000000 | bytes 4096 | tf_op jit(solution)/shard_map/ssm_out/pallas_call | solution.py:791
  257.0 2.8 collective-permute-done.36.refs_5_.rest_3_
  261.5 5.3 %squares.1.rest_4_ = f32[1024,2]{1,0:T(8,128)} custom-call(bf16[1024,1024]{1,0:T(8,128)(2,1)} %get-tuple-element.170.refs_0_.keep_attn, bf16[1024,1024]{1,0:T(8,128)(2,1)} %copy-done.1, bf16[1024,512]{1,0:T(8,128)(2,1)} %get-tuple-element.174.refs_2_.rest_0_, bf16[1024,512]{1,0:T(8,128)(2,1)} %copy-done.4, ...), custom_call_target="tpu_custom_call" | custom-call | flops 20000000 | bytes 4096 | tf_op jit(solution)/shard_map/squares/pallas_call | solution.py:807
  267.0 2.0 collective-permute-done.37.rest_5_
  269.8 6.7 %mixed_rows.3 = (bf16[128,800]{1,0:T(8,128)(2,1)}, bf16[128,800]{1,0:T(8,128)(2,1)}, bf16[128,800]{1,0:T(8,128)(2,1)}, bf16[128,800]{1,0:T(8,128)(2,1)}) custom-call(s32[8]{0:T(128)} %select_reduce_fusion.1.proc, s32[8]{0:T(128)} %dynamic_slice.14.sizes, bf16[1024,1024]{1,0:T(8,128)(2,1)} %place_rows.1.x_keep, ...), custom_call_target="tpu_custom_call" | custom-call | flops 40000000 | bytes 4096 | tf_op jit(solution)/shard_map/mixed_rows/pallas_call | solution.py:823
  280.0 6.7 %mixed_rows.2 = (bf16[128,800]{1,0:T(8,128)(2,1)}, bf16[128,800]{1,0:T(8,128)(2,1)}, bf16[128,800]{1,0:T(8,128)(2,1)}, bf16[128,800]{1,0:T(8,128)(2,1)}) custom-call(s32[8]{0:T(128)} %select_reduce_fusion.1.proc, s32[8]{0:T(128)} %dynamic_slice.14.sizes, bf16[1024,1024]{1,0:T(8,128)(2,1)} %place_rows.1.x_keep, ...), custom_call_target="tpu_custom_call" | custom-call | flops 40000000 | bytes 4096 | tf_op jit(solution)/shard_map/mixed_rows/pallas_call | solution.py:823
  290.7 5.7 %collective-permute-done.38 = bf16[128,800]{1,0:T(8,128)(2,1)S(1)} collective-permute-done((bf16[128,800]{1,0:T(8,128)(2,1)}, bf16[128,800]{1,0:T(8,128)(2,1)S(1)}, u32[]{:S(2)}, u32[]{:S(2)}) %collective-permute-start.38) | collective-permute-done | bytes 204832 | tf_op jit(solution)/shard_map/ppermute | solution.py:1005
  296.5 3.6 %collective-permute-done.40 = bf16[128,800]{1,0:T(8,128)(2,1)S(1)} collective-permute-done((bf16[128,800]{1,0:T(8,128)(2,1)}, bf16[128,800]{1,0:T(8,128)(2,1)S(1)}, u32[]{:S(2)}, u32[]{:S(2)}) %collective-permute-start.40) | collective-permute-done | bytes 204832 | tf_op jit(solution)/shard_map/ppermute | solution.py:47
  (224 shorter events, 78.6 us)
Async XLA Ops:
  1.8 43.9 %collective-permute-start.9 = (bf16[104,1600]{1,0:T(8,128)(2,1)}, bf16[104,1600]{1,0:T(8,128)(2,1)}, u32[]{:S(2)}, u32[]{:S(2)}) collective-permute-start(bf16[104,1600]{1,0:T(8,128)(2,1)} %pad.20), channel_id=1, source_target_pairs={{0,24},{24,0},{8,16},{16,8},{1,25},{25,1},{9,17},{17,9},{2,26},{26... | collective-permute-start | bytes 998408 | tf_op jit(solution)/shard_map/ppermute | solution.py:890
  5.6 15.7 %collective-permute-start.3 = (bf16[104,1600]{1,0:T(8,128)(2,1)}, bf16[104,1600]{1,0:T(8,128)(2,1)S(1)}, u32[]{:S(2)}, u32[]{:S(2)}) collective-permute-start(bf16[104,1600]{1,0:T(8,128)(2,1)} %pad.20), channel_id=1, source_target_pairs={{0,16},{16,0},{8,24},{24,8},{1,17},{17,1},{9,25},{25,9},{2,18},{18... | collective-permute-start | bytes 998408 | tf_op jit(solution)/shard_map/ppermute | solution.py:47
  6.2 15.5 %collective-permute-start.2 = (bf16[104,1600]{1,0:T(8,128)(2,1)}, bf16[104,1600]{1,0:T(8,128)(2,1)S(1)}, u32[]{:S(2)}, u32[]{:S(2)}) collective-permute-start(bf16[104,1600]{1,0:T(8,128)(2,1)} %pad.20), channel_id=1, source_target_pairs={{0,8},{8,0},{16,24},{24,16},{1,9},{9,1},{17,25},{25,17},{2,10},{10... | collective-permute-start | bytes 998408 | tf_op jit(solution)/shard_map/ppermute | solution.py:43
  8.8 12.9 %collective-permute-start.1 = (bf16[104,1600]{1,0:T(8,128)(2,1)S(1)}, bf16[104,1600]{1,0:T(8,128)(2,1)S(1)}, u32[]{:S(2)}, u32[]{:S(2)}) collective-permute-start(bf16[104,1600]{1,0:T(8,128)(2,1)S(1)} %pad.19), channel_id=1, source_target_pairs={{2,4},{4,2},{3,5},{5,3},{10,12},{12,10},{11,13},{13,11},{18,20},{2... | collective-permute-start | bytes 998408 | tf_op jit(solution)/shard_map/ppermute | solution.py:51
  21.7 22.8 %collective-permute-start.8 = (bf16[104,1600]{1,0:T(8,128)(2,1)S(1)}, bf16[104,1600]{1,0:T(8,128)(2,1)}, u32[]{:S(2)}, u32[]{:S(2)}) collective-permute-start(bf16[104,1600]{1,0:T(8,128)(2,1)S(1)} %collective-permute-done), channel_id=1, source_target_pairs={{4,0},{2,6},{5,1},{3,7},{12,8},{10,14},{13,9},{11,15},{20,16},{18,... | collective-permute-start | bytes 998408 | tf_op jit(solution)/shard_map/ppermute | solution.py:51
  23.0 21.5 %collective-permute-start.7 = (bf16[104,1600]{1,0:T(8,128)(2,1)S(1)}, bf16[104,1600]{1,0:T(8,128)(2,1)}, u32[]{:S(2)}, u32[]{:S(2)}) collective-permute-start(bf16[104,1600]{1,0:T(8,128)(2,1)S(1)} %collective-permute-done), channel_id=1, source_target_pairs={{2,4},{4,2},{3,5},{5,3},{10,12},{12,10},{11,13},{13,11},{18,20},{2... | collective-permute-start | bytes 998408 | tf_op jit(solution)/shard_map/ppermute | solution.py:51
  25.6 16.4 %collective-permute-start.6 = (bf16[104,1600]{1,0:T(8,128)(2,1)S(1)}, bf16[104,1600]{1,0:T(8,128)(2,1)}, u32[]{:S(2)}, u32[]{:S(2)}) collective-permute-start(bf16[104,1600]{1,0:T(8,128)(2,1)S(1)} %collective-permute-done.1), channel_id=1, source_target_pairs={{2,0},{4,6},{3,1},{5,7},{10,8},{12,14},{11,9},{13,15},{18,16},{20,... | collective-permute-start | bytes 998408 | tf_op jit(solution)/shard_map/ppermute | solution.py:51
  27.9 17.7 %collective-permute-start.5 = (bf16[208,1600]{1,0:T(8,128)(2,1)S(1)}, bf16[208,1600]{1,0:T(8,128)(2,1)S(1)}, u32[]{:S(2)}, u32[]{:S(2)}) collective-permute-start(bf16[208,1600]{1,0:T(8,128)(2,1)S(1)} %constant_dynamic-update-slice_fusion.rest_0_), channel_id=1, source_target_pairs={{0,16},{16,0},{8,24},{24,8},{1,17},{17,1},{9,25},{25,9},{2,18},{18... | collective-permute-start | bytes 1996808 | tf_op jit(solution)/shard_map/ppermute | solution.py:47
  42.0 17.0 %collective-permute-start.4 = (bf16[208,1600]{1,0:T(8,128)(2,1)S(1)}, bf16[208,1600]{1,0:T(8,128)(2,1)S(1)}, u32[]{:S(2)}, u32[]{:S(2)}) collective-permute-start(bf16[208,1600]{1,0:T(8,128)(2,1)S(1)} %constant_dynamic-update-slice_fusion.rest_0_), channel_id=1, source_target_pairs={{0,8},{8,0},{16,24},{24,16},{1,9},{9,1},{17,25},{25,17},{2,10},{10... | collective-permute-start | bytes 1996808 | tf_op jit(solution)/shard_map/ppermute | solution.py:43
  59.0 27.7 %collective-permute-start.14 = (bf16[1024,896]{1,0:T(8,128)(2,1)S(1)}, bf16[1024,896]{1,0:T(8,128)(2,1)}, u32[]{:S(2)}, u32[]{:S(2)}) collective-permute-start(bf16[1024,896]{1,0:T(8,128)(2,1)S(1)} %copy-done), channel_id=1, source_target_pairs={{0,1},{1,0},{2,3},{3,2},{4,5},{5,4},{6,7},{7,6},{8,9},{9,8},{10,11... | collective-permute-start | bytes 5505032 | tf_op jit(solution)/shard_map/ppermute | solution.py:55
  60.0 22.7 %collective-permute-start.13 = (bf16[104,2880]{1,0:T(8,128)(2,1)}, bf16[104,2880]{1,0:T(8,128)(2,1)}, u32[]{:S(2)}, u32[]{:S(2)}) collective-permute-start(bf16[104,2880]{1,0:T(8,128)(2,1)} %fusion.10), channel_id=1, source_target_pairs={{2,4},{4,2},{3,5},{5,3},{10,12},{12,10},{11,13},{13,11},{18,20},{2... | collective-permute-start | bytes 1797128 | tf_op jit(solution)/shard_map/ppermute | solution.py:51
  61.5 22.0 %collective-permute-start.12 = (bf16[104,2880]{1,0:T(8,128)(2,1)}, bf16[104,2880]{1,0:T(8,128)(2,1)}, u32[]{:S(2)}, u32[]{:S(2)}) collective-permute-start(bf16[104,2880]{1,0:T(8,128)(2,1)} %fusion.10), channel_id=1, source_target_pairs={{0,2},{2,0},{4,6},{6,4},{1,3},{3,1},{5,7},{7,5},{8,10},{10,8},{12,... | collective-permute-start | bytes 1797128 | tf_op jit(solution)/shard_map/ppermute | solution.py:51
  69.8 16.6 %collective-permute-start.11 = (bf16[208,1600]{1,0:T(8,128)(2,1)S(1)}, bf16[208,1600]{1,0:T(8,128)(2,1)}, u32[]{:S(2)}, u32[]{:S(2)}) collective-permute-start(bf16[208,1600]{1,0:T(8,128)(2,1)S(1)} %pad_maximum_fusion.4.rest_1_), channel_id=1, source_target_pairs={{0,16},{16,0},{8,24},{24,8},{1,17},{17,1},{9,25},{25,9},{2,18},{18... | collective-permute-start | bytes 1996808 | tf_op jit(solution)/shard_map/ppermute | solution.py:47
  70.3 16.4 %collective-permute-start.10 = (bf16[208,1600]{1,0:T(8,128)(2,1)S(1)}, bf16[208,1600]{1,0:T(8,128)(2,1)}, u32[]{:S(2)}, u32[]{:S(2)}) collective-permute-start(bf16[208,1600]{1,0:T(8,128)(2,1)S(1)} %pad_maximum_fusion.4.rest_1_), channel_id=1, source_target_pairs={{0,8},{8,0},{16,24},{24,16},{1,9},{9,1},{17,25},{25,17},{2,10},{10... | collective-permute-start | bytes 1996808 | tf_op jit(solution)/shard_map/ppermute | solution.py:43
  86.7 19.0 %collective-permute-start.15 = (bf16[208,1600]{1,0:T(8,128)(2,1)S(1)}, bf16[208,1600]{1,0:T(8,128)(2,1)S(1)}, u32[]{:S(2)}, u32[]{:S(2)}) collective-permute-start(bf16[208,1600]{1,0:T(8,128)(2,1)S(1)} %copy-done.24), channel_id=1, source_target_pairs={{0,16},{16,0},{8,24},{24,8},{1,17},{17,1},{9,25},{25,9},{2,18},{18... | collective-permute-start | bytes 1996808 | tf_op jit(solution)/shard_map/ppermute | solution.py:47
  88.2 17.5 %collective-permute-start.16 = (bf16[208,1600]{1,0:T(8,128)(2,1)}, bf16[208,1600]{1,0:T(8,128)(2,1)S(1)}, u32[]{:S(2)}, u32[]{:S(2)}) collective-permute-start(bf16[208,1600]{1,0:T(8,128)(2,1)} %collective-permute-done.11.rest_5_), channel_id=1, source_target_pairs={{0,8},{8,0},{16,24},{24,16},{1,9},{9,1},{17,25},{25,17},{2,10},{10... | collective-permute-start | bytes 1996808 | tf_op jit(solution)/shard_map/ppermute | solution.py:43
  88.5 33.4 %collective-permute-start.18 = (bf16[104,2880]{1,0:T(8,128)(2,1)}, bf16[104,2880]{1,0:T(8,128)(2,1)S(1)}, u32[]{:S(2)}, u32[]{:S(2)}) collective-permute-start(bf16[104,2880]{1,0:T(8,128)(2,1)} %collective-permute-done.13), channel_id=1, source_target_pairs={{2,0},{4,6},{3,1},{5,7},{10,8},{12,14},{11,9},{13,15},{18,16},{20,... | collective-permute-start | bytes 1797128 | tf_op jit(solution)/shard_map/ppermute | solution.py:51
  89.8 32.1 %collective-permute-start.19 = (bf16[104,2880]{1,0:T(8,128)(2,1)}, bf16[104,2880]{1,0:T(8,128)(2,1)}, u32[]{:S(2)}, u32[]{:S(2)}) collective-permute-start(bf16[104,2880]{1,0:T(8,128)(2,1)} %collective-permute-done.12), channel_id=1, source_target_pairs={{4,0},{2,6},{5,1},{3,7},{12,8},{10,14},{13,9},{11,15},{20,16},{18,... | collective-permute-start | bytes 1797128 | tf_op jit(solution)/shard_map/ppermute | solution.py:51
  91.1 30.8 %collective-permute-start.17 = (bf16[104,2880]{1,0:T(8,128)(2,1)}, bf16[104,2880]{1,0:T(8,128)(2,1)}, u32[]{:S(2)}, u32[]{:S(2)}) collective-permute-start(bf16[104,2880]{1,0:T(8,128)(2,1)} %collective-permute-done.12), channel_id=1, source_target_pairs={{2,4},{4,2},{3,5},{5,3},{10,12},{12,10},{11,13},{13,11},{18,20},{2... | collective-permute-start | bytes 1797128 | tf_op jit(solution)/shard_map/ppermute | solution.py:51
  123.4 29.9 %collective-permute-start.21 = (bf16[416,1600]{1,0:T(8,128)(2,1)S(1)}, bf16[416,1600]{1,0:T(8,128)(2,1)S(1)}, u32[]{:S(2)}, u32[]{:S(2)}) collective-permute-start(bf16[416,1600]{1,0:T(8,128)(2,1)S(1)} %pad_maximum_fusion.2.rest_0_), channel_id=1, source_target_pairs={{0,16},{16,0},{8,24},{24,8},{1,17},{17,1},{9,25},{25,9},{2,18},{18... | collective-permute-start | bytes 3993608 | tf_op jit(solution)/shard_map/ppermute | solution.py:47
  125.1 29.3 %collective-permute-start.20 = (bf16[416,1600]{1,0:T(8,128)(2,1)S(1)}, bf16[416,1600]{1,0:T(8,128)(2,1)S(1)}, u32[]{:S(2)}, u32[]{:S(2)}) collective-permute-start(bf16[416,1600]{1,0:T(8,128)(2,1)S(1)} %pad_maximum_fusion.2.rest_0_), channel_id=1, source_target_pairs={{0,8},{8,0},{16,24},{24,16},{1,9},{9,1},{17,25},{25,17},{2,10},{10... | collective-permute-start | bytes 3993608 | tf_op jit(solution)/shard_map/ppermute | solution.py:43
  125.7 28.8 %collective-permute-start.24 = (bf16[416,1600]{1,0:T(8,128)(2,1)S(1)}, bf16[416,1600]{1,0:T(8,128)(2,1)}, u32[]{:S(2)}, u32[]{:S(2)}) collective-permute-start(bf16[416,1600]{1,0:T(8,128)(2,1)S(1)} %pad_maximum_fusion.1.rest_0_), channel_id=1, source_target_pairs={{2,4},{4,2},{3,5},{5,3},{10,12},{12,10},{11,13},{13,11},{18,20},{2... | collective-permute-start | bytes 3993608 | tf_op jit(solution)/shard_map/ppermute | solution.py:51
  127.4 33.0 %collective-permute-start.23 = (bf16[416,1600]{1,0:T(8,128)(2,1)S(1)}, bf16[416,1600]{1,0:T(8,128)(2,1)}, u32[]{:S(2)}, u32[]{:S(2)}) collective-permute-start(bf16[416,1600]{1,0:T(8,128)(2,1)S(1)} %pad_maximum_fusion.1.rest_0_), channel_id=1, source_target_pairs={{0,2},{2,0},{4,6},{6,4},{1,3},{3,1},{5,7},{7,5},{8,10},{10,8},{12,... | collective-permute-start | bytes 3993608 | tf_op jit(solution)/shard_map/ppermute | solution.py:51
  160.6 22.9 %collective-permute-start.26 = (bf16[208,1600]{1,0:T(8,128)(2,1)S(1)}, bf16[208,1600]{1,0:T(8,128)(2,1)S(1)}, u32[]{:S(2)}, u32[]{:S(2)}) collective-permute-start(bf16[208,1600]{1,0:T(8,128)(2,1)S(1)} %slice.72), channel_id=1, source_target_pairs={{0,8},{8,0},{16,24},{24,16},{1,9},{9,1},{17,25},{25,17},{2,10},{10... | collective-permute-start | bytes 1996808 | tf_op jit(solution)/shard_map/ppermute | solution.py:43
  162.0 21.5 %collective-permute-start.25 = (bf16[208,1600]{1,0:T(8,128)(2,1)S(1)}, bf16[208,1600]{1,0:T(8,128)(2,1)S(1)}, u32[]{:S(2)}, u32[]{:S(2)}) collective-permute-start(bf16[208,1600]{1,0:T(8,128)(2,1)S(1)} %slice.71), channel_id=1, source_target_pairs={{0,16},{16,0},{8,24},{24,8},{1,17},{17,1},{9,25},{25,9},{2,18},{18... | collective-permute-start | bytes 1996808 | tf_op jit(solution)/shard_map/ppermute | solution.py:47
  163.9 45.7 %collective-permute-start.30 = (bf16[416,1600]{1,0:T(8,128)(2,1)}, bf16[416,1600]{1,0:T(8,128)(2,1)}, u32[]{:S(2)}, u32[]{:S(2)}) collective-permute-start(bf16[416,1600]{1,0:T(8,128)(2,1)} %collective-permute-done.24.rest_0_), channel_id=1, source_target_pairs={{2,0},{4,6},{3,1},{5,7},{10,8},{12,14},{11,9},{13,15},{18,16},{20,... | collective-permute-start | bytes 3993608 | tf_op jit(solution)/shard_map/ppermute | solution.py:51
  165.2 44.4 %collective-permute-start.29 = (bf16[416,1600]{1,0:T(8,128)(2,1)}, bf16[416,1600]{1,0:T(8,128)(2,1)}, u32[]{:S(2)}, u32[]{:S(2)}) collective-permute-start(bf16[416,1600]{1,0:T(8,128)(2,1)} %collective-permute-done.23.rest_1_), channel_id=1, source_target_pairs={{2,4},{4,2},{3,5},{5,3},{10,12},{12,10},{11,13},{13,11},{18,20},{2... | collective-permute-start | bytes 3993608 | tf_op jit(solution)/shard_map/ppermute | solution.py:51
  184.3 25.2 %collective-permute-start.28 = (bf16[416,1280]{1,0:T(8,128)(2,1)S(1)}, bf16[416,1280]{1,0:T(8,128)(2,1)S(1)}, u32[]{:S(2)}, u32[]{:S(2)}) collective-permute-start(bf16[416,1280]{1,0:T(8,128)(2,1)S(1)} %pad_maximum_fusion.3.rest_0_), channel_id=1, source_target_pairs={{0,16},{16,0},{8,24},{24,8},{1,17},{17,1},{9,25},{25,9},{2,18},{18... | collective-permute-start | bytes 3194888 | tf_op jit(solution)/shard_map/ppermute | solution.py:47
  185.7 23.9 %collective-permute-start.27 = (bf16[416,1280]{1,0:T(8,128)(2,1)S(1)}, bf16[416,1280]{1,0:T(8,128)(2,1)S(1)}, u32[]{:S(2)}, u32[]{:S(2)}) collective-permute-start(bf16[416,1280]{1,0:T(8,128)(2,1)S(1)} %pad_maximum_fusion.3.rest_0_), channel_id=1, source_target_pairs={{0,8},{8,0},{16,24},{24,16},{1,9},{9,1},{17,25},{25,17},{2,10},{10... | collective-permute-start | bytes 3194888 | tf_op jit(solution)/shard_map/ppermute | solution.py:43
  209.6 37.0 %collective-permute-start.33 = (bf16[416,1600]{1,0:T(8,128)(2,1)}, bf16[416,1600]{1,0:T(8,128)(2,1)S(1)}, u32[]{:S(2)}, u32[]{:S(2)}) collective-permute-start(bf16[416,1600]{1,0:T(8,128)(2,1)} %collective-permute-done.23.rest_1_), channel_id=1, source_target_pairs={{4,0},{2,6},{5,1},{3,7},{12,8},{10,14},{13,9},{11,15},{20,16},{18,... | collective-permute-start | bytes 3993608 | tf_op jit(solution)/shard_map/ppermute | solution.py:51
  246.7 13.2 %collective-permute-start.34 = (bf16[1024,1024]{1,0:T(8,128)(2,1)}, bf16[1024,1024]{1,0:T(8,128)(2,1)S(1)}, u32[]{:S(2)}, u32[]{:S(2)}) collective-permute-start(bf16[1024,1024]{1,0:T(8,128)(2,1)} %get-tuple-element.173), channel_id=1, source_target_pairs={{0,1},{1,0},{2,3},{3,2},{4,5},{5,4},{6,7},{7,6},{8,9},{9,8},{10,11... | collective-permute-start | bytes 6291464 | tf_op jit(solution)/shard_map/ppermute | solution.py:55
  278.0 12.7 %collective-permute-start.41 = (bf16[128,800]{1,0:T(8,128)(2,1)}, bf16[128,800]{1,0:T(8,128)(2,1)S(1)}, u32[]{:S(2)}, u32[]{:S(2)}) collective-permute-start(bf16[128,800]{1,0:T(8,128)(2,1)} %get-tuple-element.186), channel_id=1, source_target_pairs={{0,16},{16,0},{8,24},{24,8},{1,17},{17,1},{9,25},{25,9},{2,18},{18... | collective-permute-start | bytes 614408 | tf_op jit(solution)/shard_map/ppermute | solution.py:47
  (60 other events, 555.4 us)

commit v4 on v3

--- a/solution.py
+++ b/solution.py
@@ -887,16 +887,16 @@
         def right(values):
             return tuple(value[:, attn_width:] for value in values)
 
-        ssm_plane = plane_first(ssm_shard) + (lax.ppermute(ssm_shard, "rep", D_PAIRS),)
+        ssm_corner = lax.ppermute(ssm_shard, "rep", D_PAIRS)
+        ssm_late, conv_shard = tie(ssm_shard, conv_shard)
+        ssm_plane = plane_first(ssm_late) + (ssm_corner,)
         conv_z1 = line_first(conv_shard)
         inv_rms = inverse_rms(tokens)
 
-        ssm_x, ssm_y, ssm_corner = ssm_plane
         (
             conv_z1,
             conv_shard,
-            ssm_x,
-            ssm_y,
+            ssm_plane,
             inv_rms,
             serve_late,
             rep_late,
@@ -905,8 +905,7 @@
         ) = tie(
             conv_z1,
             conv_shard,
-            ssm_x,
-            ssm_y,
+            ssm_plane,
             inv_rms,
             serve_replica,
             rep,
@@ -921,10 +920,9 @@
         back_shard = shard_behind(*late_weights)
 
         conv_bottom_own = lower(conv_z1, conv_z2)
-        conv_top, conv_bottom_own, back_shard, rows_own, plain, rep_late, row_late, ssm_corner = tie(
-            conv_top, conv_bottom_own, back_shard, rows_own, plain, rep, row, ssm_corner
-        )
-        ssm_plane = (ssm_x, ssm_y, ssm_corner)
+        conv_top, conv_bottom_own, back_shard, rows_own, plain, rep_late, row_late = tie(
+            conv_top, conv_bottom_own, back_shard, rows_own, plain, rep, row
+        )
         conv_bottom = plane_first(conv_bottom_own)
         back_z1 = line_first(back_shard)
         rows_other = other_core(rows_own)
@@ -959,12 +957,15 @@
         count = groups // 2
         scanned = scan(0, count, conv_out, mix_own, mix_other, small)
 
-        gate_p1, scanned, ssm_near, ssm_middle = tie(gate_p1, scanned, ssm_near, ssm_middle)
+        gate_p1, scanned = tie(gate_p1, scanned)
         gate_p2 = plane_second(gate_p1)
+        quarter = groups // 4
+        scanned = scan(count, quarter, conv_out, mix_own, mix_other, small, (scanned,))
+        scanned, ssm_near, ssm_middle = tie(scanned, ssm_near, ssm_middle)
         crossed = along_z(ssm_near, Z_INNER)
         ends = along_z(ssm_middle, Z_ENDS)
         scanned = scan(
-            count, groups - count, conv_out, mix_own, mix_other, small, (scanned,)
+            count + quarter, quarter, conv_out, mix_own, mix_other, small, (scanned,)
         )
         attn_block = line_block(left((back_shard,))[0], left(back_z1), left(back_z2))
 

time: 307 us -> 291 us (0.948)
  waiting for transfers between devices: 51.9 us -> 35.1 us
    ppermute x10, waiting for transfers between devices: 22.2 us -> 10.4 us  [swap_x(): return lax.ppermute(value, 'rep', X_PAIRS)]
    ppermute x15, waiting for transfers between devices: 7.47 us -> 2.99 us  [along_z(): return lax.ppermute(value, 'tr', pairs)]
    pallas_call x2 -> x3, Pallas kernels: 32.9 us -> 35.7 us  [scan(): call(functools.partial(scan_kernel, slots), 1, count, [blocks(channels),...]
    unnamed x99 -> x97, local copies, waits for them, and re-layouts: 7.67 us -> 6.51 us
  transfers between devices with their start and end apart: 44 -> 44, of which waited for: 17 -> 16; matrix products, arithmetic and copies ran while one was open for 10% -> 10% of each run, Pallas kernels for 43% -> 46%
where the time goes in v4:
time: 291 us; the launch traced here: 286 us
  Pallas kernels  144 us (49%)
  starting transfers between devices  62.9 us (22%)
  waiting for transfers between devices  35.1 us (12%)
  local copies, waits for them, and re-layouts  21.3 us (7%)
  other arithmetic  20 us (7%)
    pallas_call x3, Pallas kernels, scan(): call(functools.partial(scan_kernel, slots), 1, count, [blocks(channels),...  35.7 us
    ppermute x15, starting transfers between devices, along_z(): return lax.ppermute(value, 'tr', pairs)  34.9 us
    pallas_call x2, Pallas kernels, ssm_out(): call(functools.partial(ssm_out_kernel, choices, section // len(choices)),...  18.3 us
    pallas_call x1, Pallas kernels, attention(): call(functools.partial(attention_kernel, slots, group_rows, kv_here, per_...  17.4 us
    pallas_call x1, Pallas kernels, convolve(): call(functools.partial(conv_kernel, slots, group_rows, len(pieces), half,...  15 us
    pallas_call x2, Pallas kernels, mix(): call(functools.partial(mixed_kernel, slots, part * here, sections, here),...  13.3 us
    pallas_call x1, Pallas kernels, gate(): call(functools.partial(gate_kernel, len(pieces), half, first_column), 1,...  13.1 us
    ppermute x10, waiting for transfers between devices, swap_y(): return lax.ppermute(value, 'rep', Y_PAIRS)  11.2 us
  transfers between devices with their start and end apart: 44, of which 16 were waited for; matrix products, arithmetic and copies ran while one was open for 10% of the time, Pallas kernels for 46%

profile of v4, /device:TPU:0, one launch (start us, length us, event | category | flops | bytes accessed | tf_op | source)
XLA Modules:
  0.0 286.4 jit_solution(3009140918650581820)
XLA Ops:
  1.0 4.0 %collective-permute-start.4 = (bf16[104,1600]{1,0:T(8,128)(2,1)S(1)}, bf16[104,1600]{1,0:T(8,128)(2,1)S(1)}, u32[]{:S(2)}, u32[]{:S(2)}) collective-permute-start(bf16[104,1600]{1,0:T(8,128)(2,1)S(1)} %pad.19), channel_id=1, source_target_pairs={{0,24},{24,0},{8,16},{16,8},{1,25},{25,1},{9,17},{17,9},{2,26},{26... | collective-permute-start | bytes 998408 | tf_op jit(solution)/shard_map/ppermute | solution.py:890
  5.0 2.5 fusion.25
  9.1 4.9 %collective-permute-start = (bf16[104,1600]{1,0:T(8,128)(2,1)S(1)}, bf16[104,1600]{1,0:T(8,128)(2,1)S(1)}, u32[]{:S(2)}, u32[]{:S(2)}) collective-permute-start(bf16[104,1600]{1,0:T(8,128)(2,1)S(1)} %pad.20), channel_id=1, source_target_pairs={{0,2},{2,0},{4,6},{6,4},{1,3},{3,1},{5,7},{7,5},{8,10},{10,8},{12,... | collective-permute-start | bytes 998408 | tf_op jit(solution)/shard_map/ppermute | solution.py:51
  15.2 2.5 psum.7
  17.7 2.9 collective-permute-done.3
  31.7 9.6 %spread_rows.1.rows_own = bf16[1024,896]{1,0:T(8,128)(2,1)} custom-call(s32[8]{0:T(128)} %select_reduce_fusion.1.proc, bf16[8,128,800]{2,1,0:T(8,128)(2,1)} %bitcast.23, f32[8,128,1]{2,1,0:T(8,128)} %copy.38.inv_rms, f32[1,800]{1,0:T(1,128)} %broadcast_in_dim.113.gain, bf16[800,896]{1,0:T(8,128)(2,1)} %fusion.1.pick), custom_call_target="tpu_custom_call" | custom-call | flops 80000000 | bytes 4096 | tf_op jit(solution)/shard_map/spread_rows/pallas_call | solution.py:612
  46.6 7.9 %collective-permute-start.12 = (bf16[104,2880]{1,0:T(8,128)(2,1)}, bf16[104,2880]{1,0:T(8,128)(2,1)}, u32[]{:S(2)}, u32[]{:S(2)}) collective-permute-start(bf16[104,2880]{1,0:T(8,128)(2,1)} %fusion.10), channel_id=1, source_target_pairs={{0,2},{2,0},{4,6},{6,4},{1,3},{3,1},{5,7},{7,5},{8,10},{10,8},{12,... | collective-permute-start | bytes 1797128 | tf_op jit(solution)/shard_map/ppermute | solution.py:51
  63.3 2.0 iota_compare_fusion.1
  66.6 2.5 collective-permute-done.12
  69.0 3.0 %collective-permute-done.11.rest_5_ = bf16[208,1600]{1,0:T(8,128)(2,1)} collective-permute-done((bf16[208,1600]{1,0:T(8,128)(2,1)S(1)}, bf16[208,1600]{1,0:T(8,128)(2,1)}, u32[]{:S(2)}, u32[]{:S(2)}) %collective-permute-start.11) | collective-permute-done | bytes 665632 | tf_op jit(solution)/shard_map/ppermute | solution.py:47
  80.4 9.1 %place_rows.1.x_keep = bf16[1024,1024]{1,0:T(8,128)(2,1)} custom-call(s32[8]{0:T(128)} %select_reduce_fusion.1.proc, bf16[8,128,800]{2,1,0:T(8,128)(2,1)} %bitcast.24, bf16[800,1024]{1,0:T(8,128)(2,1)} %get-tuple-element.137.pick), custom_call_target="tpu_custom_call" | custom-call | flops 80000000 | bytes 4096 | tf_op jit(solution)/shard_map/place_rows/pallas_call | solution.py:630
  91.8 15.0 %convolve.1 = (bf16[1024,1600]{1,0:T(8,128)(2,1)}, bf16[1024,256]{1,0:T(8,128)(2,1)}) custom-call(s32[8]{0:T(128)} %select_reduce_fusion.1.proc, s32[1]{0:T(128)} %bitcast.8.second, bf16[1024,896]{1,0:T(8,128)(2,1)} %spread_rows.1.rows_own, bf16[1024,896]{1,0:T(8,128)(2,1)} %collective-permute-done.14.rows_other, f32[8,3,1600]{2,1,0:T(4,128)} %copy.41.history, ...), custom_call_target="tpu_custom_call" | custom-call | flops 140000000 | bytes 4096 | tf_op jit(solution)/shard_map/convolve/pallas_call | solution.py:678
  112.3 6.3 %collective-permute-start.25 = (bf16[416,1600]{1,0:T(8,128)(2,1)S(1)}, bf16[416,1600]{1,0:T(8,128)(2,1)}, u32[]{:S(2)}, u32[]{:S(2)}) collective-permute-start(bf16[416,1600]{1,0:T(8,128)(2,1)S(1)} %pad_maximum_fusion.1.rest_0_), channel_id=1, source_target_pairs={{0,2},{2,0},{4,6},{6,4},{1,3},{3,1},{5,7},{7,5},{8,10},{10,8},{12,... | collective-permute-start | bytes 3993608 | tf_op jit(solution)/shard_map/ppermute | solution.py:51
  121.4 16.4 %scan_states.3.rest_0_ = f32[1024,1600]{1,0:T(8,128)} custom-call(s32[8]{0:T(128)} %select_reduce_fusion.1.proc, bf16[1024,1600]{1,0:T(8,128)(2,1)} %get-tuple-element.158.conv, bf16[1024,256]{1,0:T(8,128)(2,1)} %get-tuple-element.159.mix_own, bf16[1024,256]{1,0:T(8,128)(2,1)} %copy-done.11, bf16[100,1600]{1,0:T(8,128)(2,1)} %step_weight.5, ...), custom_call_target="tpu_custom_call" | custom-call | flops 160000000 | bytes 4096 | tf_op jit(solution)/shard_map/scan_states/pallas_call | solution.py:711
  143.5 9.6 %scan_states.4.rest_0_ = f32[1024,1600]{1,0:T(8,128)} custom-call(s32[8]{0:T(128)} %select_reduce_fusion.1.proc, bf16[1024,1600]{1,0:T(8,128)(2,1)} %get-tuple-element.158.conv, bf16[1024,256]{1,0:T(8,128)(2,1)} %get-tuple-element.159.mix_own, bf16[1024,256]{1,0:T(8,128)(2,1)} %copy-done.11, ...), custom_call_target="tpu_custom_call", output_to_operand_aliasing={{}: (9, {})} | custom-call | flops 80000000 | bytes 4096 | tf_op jit(solution)/shard_map/scan_states/pallas_call | solution.py:711
  154.4 1.8 collective-permute-start.29
  156.3 9.6 %scan_states.5.scanned = f32[1024,1600]{1,0:T(8,128)} custom-call(s32[8]{0:T(128)} %select_reduce_fusion.1.proc, bf16[1024,1600]{1,0:T(8,128)(2,1)} %get-tuple-element.158.conv, bf16[1024,256]{1,0:T(8,128)(2,1)} %get-tuple-element.159.mix_own, bf16[1024,256]{1,0:T(8,128)(2,1)} %copy-done.11, ...), custom_call_target="tpu_custom_call", output_to_operand_aliasing={{}: (9, {})} | custom-call | flops 80000000 | bytes 4096 | tf_op jit(solution)/shard_map/scan_states/pallas_call | solution.py:711
  167.9 13.1 %gate.1.gated = bf16[1024,1600]{1,0:T(8,128)(2,1)} custom-call(s32[1]{0:T(128)} %bitcast.8.second, bf16[1024,896]{1,0:T(8,128)(2,1)} %spread_rows.1.rows_own, bf16[1024,896]{1,0:T(8,128)(2,1)} %collective-permute-done.14.rows_other, f32[1024,1600]{1,0:T(8,128)} %scan_states.5.scanned, bf16[416,1600]{1,0:T(8,128)(2,1)} %copy-done.9, ...), custom_call_target="tpu_custom_call" | custom-call | flops 130000000 | bytes 4096 | tf_op jit(solution)/shard_map/gate/pallas_call | solution.py:748
  181.0 9.1 %ssm_out.2 = (bf16[1024,512]{1,0:T(8,128)(2,1)}, bf16[1024,512]{1,0:T(8,128)(2,1)}) custom-call(s32[2]{0:T(128)} %pad_add_fusion.scalars, bf16[1024,1600]{1,0:T(8,128)(2,1)} %gate.1.gated, bf16[416,1600]{1,0:T(8,128)(2,1)} %copy-done.8, bf16[416,1600]{1,0:T(8,128)(2,1)} %collective-permute-done.25.rest_1_), custom_call_target="tpu_custom_call" | custom-call | flops 80000000 | bytes 4096 | tf_op jit(solution)/shard_map/ssm_out/pallas_call | solution.py:791
  194.7 9.2 %collective-permute-done.32.rest_4_ = bf16[208,1280]{1,0:T(8,128)(2,1)S(1)} collective-permute-done((bf16[208,1280]{1,0:T(8,128)(2,1)S(1)}, bf16[208,1280]{1,0:T(8,128)(2,1)S(1)}, u32[]{:S(2)}, u32[]{:S(2)}) %collective-permute-start.32) | collective-permute-done | bytes 532512 | tf_op jit(solution)/shard_map/ppermute | solution.py:43
  205.5 17.4 %attention.1.heads = bf16[1024,512]{1,0:T(8,128)(2,1)} custom-call(s32[8]{0:T(128)} %select_reduce_fusion.1.proc, s32[8]{0:T(128)} %dynamic_slice.13.lengths, s32[1]{0:T(128)} %bitcast.8.second, bf16[1024,896]{1,0:T(8,128)(2,1)} %spread_rows.1.rows_own, bf16[1024,896]{1,0:T(8,128)(2,1)} %collective-permute-done.14.rows_other, bf16[8,256,256]{2,1,0:T(8,128)(2,1)} %cache.1, ...), custom_call_target="tpu_custom_call" | custom-call | flops 150000000 | bytes 4096 | tf_op jit(solution)/shard_map/attention/pallas_call | solution.py:643
  223.0 6.9 %attn_out.1 = (bf16[1024,1024]{1,0:T(8,128)(2,1)}, bf16[1024,1024]{1,0:T(8,128)(2,1)}) custom-call(s32[1]{0:T(128)} %bitcast.8.second, bf16[1024,512]{1,0:T(8,128)(2,1)} %attention.1.heads, bf16[416,1280]{1,0:T(8,128)(2,1)} %copy-done.3, bf16[416,1280]{1,0:T(8,128)(2,1)} %copy-done.7, bf16[416,1280]{1,0:T(8,128)(2,1)} %copy-done.6, ...), custom_call_target="tpu_custom_call" | custom-call | flops 60000000 | bytes 4096 | tf_op jit(solution)/shard_map/attn_out/pallas_call | solution.py:773
  231.0 9.1 %ssm_out.3 = (bf16[1024,512]{1,0:T(8,128)(2,1)}, bf16[1024,512]{1,0:T(8,128)(2,1)}) custom-call(s32[2]{0:T(128)} %pad_add_fusion.scalars, bf16[1024,1600]{1,0:T(8,128)(2,1)} %gate.1.gated, bf16[416,1600]{1,0:T(8,128)(2,1)} %collective-permute-done.26.rest_0_, bf16[416,1600]{1,0:T(8,128)(2,1)} %collective-permute-done.30.rest_1_, ...), custom_call_target="tpu_custom_call" | custom-call | flops 80000000 | bytes 4096 | tf_op jit(solution)/shard_map/ssm_out/pallas_call | solution.py:791
  240.2 2.8 collective-permute-done.36.refs_5_.rest_3_
  244.8 5.4 %squares.1.rest_4_ = f32[1024,2]{1,0:T(8,128)} custom-call(bf16[1024,1024]{1,0:T(8,128)(2,1)} %get-tuple-element.176.refs_0_.keep_attn, bf16[1024,1024]{1,0:T(8,128)(2,1)} %copy-done.1, bf16[1024,512]{1,0:T(8,128)(2,1)} %get-tuple-element.180.refs_2_.rest_0_, bf16[1024,512]{1,0:T(8,128)(2,1)} %copy-done.4, ...), custom_call_target="tpu_custom_call" | custom-call | flops 20000000 | bytes 4096 | tf_op jit(solution)/shard_map/squares/pallas_call | solution.py:807
  250.3 2.0 collective-permute-done.37.rest_5_
  253.1 6.7 %mixed_rows.3 = (bf16[128,800]{1,0:T(8,128)(2,1)}, bf16[128,800]{1,0:T(8,128)(2,1)}, bf16[128,800]{1,0:T(8,128)(2,1)}, bf16[128,800]{1,0:T(8,128)(2,1)}) custom-call(s32[8]{0:T(128)} %select_reduce_fusion.1.proc, s32[8]{0:T(128)} %dynamic_slice.14.sizes, bf16[1024,1024]{1,0:T(8,128)(2,1)} %place_rows.1.x_keep, ...), custom_call_target="tpu_custom_call" | custom-call | flops 40000000 | bytes 4096 | tf_op jit(solution)/shard_map/mixed_rows/pallas_call | solution.py:823
  259.7 1.8 collective-permute-start.39
  263.3 6.7 %mixed_rows.2 = (bf16[128,800]{1,0:T(8,128)(2,1)}, bf16[128,800]{1,0:T(8,128)(2,1)}, bf16[128,800]{1,0:T(8,128)(2,1)}, bf16[128,800]{1,0:T(8,128)(2,1)}) custom-call(s32[8]{0:T(128)} %select_reduce_fusion.1.proc, s32[8]{0:T(128)} %dynamic_slice.14.sizes, bf16[1024,1024]{1,0:T(8,128)(2,1)} %place_rows.1.x_keep, ...), custom_call_target="tpu_custom_call" | custom-call | flops 40000000 | bytes 4096 | tf_op jit(solution)/shard_map/mixed_rows/pallas_call | solution.py:823
  270.0 1.8 collective-permute-start.38
  274.0 5.7 %collective-permute-done.38 = bf16[128,800]{1,0:T(8,128)(2,1)S(1)} collective-permute-done((bf16[128,800]{1,0:T(8,128)(2,1)}, bf16[128,800]{1,0:T(8,128)(2,1)S(1)}, u32[]{:S(2)}, u32[]{:S(2)}) %collective-permute-start.38) | collective-permute-done | bytes 204832 | tf_op jit(solution)/shard_map/ppermute | solution.py:1006
  279.7 3.6 %collective-permute-done.40 = bf16[128,800]{1,0:T(8,128)(2,1)S(1)} collective-permute-done((bf16[128,800]{1,0:T(8,128)(2,1)}, bf16[128,800]{1,0:T(8,128)(2,1)S(1)}, u32[]{:S(2)}, u32[]{:S(2)}) %collective-permute-start.40) | collective-permute-done | bytes 204832 | tf_op jit(solution)/shard_map/ppermute | solution.py:47
  (223 shorter events, 74.7 us)
Async XLA Ops:
  1.0 16.6 %collective-permute-start.4 = (bf16[104,1600]{1,0:T(8,128)(2,1)S(1)}, bf16[104,1600]{1,0:T(8,128)(2,1)S(1)}, u32[]{:S(2)}, u32[]{:S(2)}) collective-permute-start(bf16[104,1600]{1,0:T(8,128)(2,1)S(1)} %pad.19), channel_id=1, source_target_pairs={{0,24},{24,0},{8,16},{16,8},{1,25},{25,1},{9,17},{17,9},{2,26},{26... | collective-permute-start | bytes 998408 | tf_op jit(solution)/shard_map/ppermute | solution.py:890
  7.6 12.9 %collective-permute-start.3 = (bf16[104,1600]{1,0:T(8,128)(2,1)S(1)}, bf16[104,1600]{1,0:T(8,128)(2,1)S(1)}, u32[]{:S(2)}, u32[]{:S(2)}) collective-permute-start(bf16[104,1600]{1,0:T(8,128)(2,1)S(1)} %pad.19), channel_id=1, source_target_pairs={{0,16},{16,0},{8,24},{24,8},{1,17},{17,1},{9,25},{25,9},{2,18},{18... | collective-permute-start | bytes 998408 | tf_op jit(solution)/shard_map/ppermute | solution.py:47
  8.2 12.7 %collective-permute-start.2 = (bf16[104,1600]{1,0:T(8,128)(2,1)S(1)}, bf16[104,1600]{1,0:T(8,128)(2,1)}, u32[]{:S(2)}, u32[]{:S(2)}) collective-permute-start(bf16[104,1600]{1,0:T(8,128)(2,1)S(1)} %pad.19), channel_id=1, source_target_pairs={{0,8},{8,0},{16,24},{24,16},{1,9},{9,1},{17,25},{25,17},{2,10},{10... | collective-permute-start | bytes 998408 | tf_op jit(solution)/shard_map/ppermute | solution.py:43
  8.4 12.5 %collective-permute-start.1 = (bf16[104,1600]{1,0:T(8,128)(2,1)S(1)}, bf16[104,1600]{1,0:T(8,128)(2,1)S(1)}, u32[]{:S(2)}, u32[]{:S(2)}) collective-permute-start(bf16[104,1600]{1,0:T(8,128)(2,1)S(1)} %pad.20), channel_id=1, source_target_pairs={{2,4},{4,2},{3,5},{5,3},{10,12},{12,10},{11,13},{13,11},{18,20},{2... | collective-permute-start | bytes 998408 | tf_op jit(solution)/shard_map/ppermute | solution.py:51
  21.0 22.7 %collective-permute-start.9 = (bf16[104,1600]{1,0:T(8,128)(2,1)S(1)}, bf16[104,1600]{1,0:T(8,128)(2,1)}, u32[]{:S(2)}, u32[]{:S(2)}) collective-permute-start(bf16[104,1600]{1,0:T(8,128)(2,1)S(1)} %collective-permute-done), channel_id=1, source_target_pairs={{4,0},{2,6},{5,1},{3,7},{12,8},{10,14},{13,9},{11,15},{20,16},{18,... | collective-permute-start | bytes 998408 | tf_op jit(solution)/shard_map/ppermute | solution.py:51
  22.4 21.4 %collective-permute-start.8 = (bf16[104,1600]{1,0:T(8,128)(2,1)S(1)}, bf16[104,1600]{1,0:T(8,128)(2,1)}, u32[]{:S(2)}, u32[]{:S(2)}) collective-permute-start(bf16[104,1600]{1,0:T(8,128)(2,1)S(1)} %collective-permute-done), channel_id=1, source_target_pairs={{2,4},{4,2},{3,5},{5,3},{10,12},{12,10},{11,13},{13,11},{18,20},{2... | collective-permute-start | bytes 998408 | tf_op jit(solution)/shard_map/ppermute | solution.py:51
  23.9 21.0 %collective-permute-start.6 = (bf16[208,1600]{1,0:T(8,128)(2,1)S(1)}, bf16[208,1600]{1,0:T(8,128)(2,1)}, u32[]{:S(2)}, u32[]{:S(2)}) collective-permute-start(bf16[208,1600]{1,0:T(8,128)(2,1)S(1)} %constant_dynamic-update-slice_fusion.rest_0_), channel_id=1, source_target_pairs={{0,16},{16,0},{8,24},{24,8},{1,17},{17,1},{9,25},{25,9},{2,18},{18... | collective-permute-start | bytes 1996808 | tf_op jit(solution)/shard_map/ppermute | solution.py:47
  25.2 19.6 %collective-permute-start.5 = (bf16[208,1600]{1,0:T(8,128)(2,1)S(1)}, bf16[208,1600]{1,0:T(8,128)(2,1)}, u32[]{:S(2)}, u32[]{:S(2)}) collective-permute-start(bf16[208,1600]{1,0:T(8,128)(2,1)S(1)} %constant_dynamic-update-slice_fusion.rest_0_), channel_id=1, source_target_pairs={{0,8},{8,0},{16,24},{24,16},{1,9},{9,1},{17,25},{25,17},{2,10},{10... | collective-permute-start | bytes 1996808 | tf_op jit(solution)/shard_map/ppermute | solution.py:43
  27.8 14.7 %collective-permute-start.7 = (bf16[104,1600]{1,0:T(8,128)(2,1)S(1)}, bf16[104,1600]{1,0:T(8,128)(2,1)}, u32[]{:S(2)}, u32[]{:S(2)}) collective-permute-start(bf16[104,1600]{1,0:T(8,128)(2,1)S(1)} %collective-permute-done.1), channel_id=1, source_target_pairs={{2,0},{4,6},{3,1},{5,7},{10,8},{12,14},{11,9},{13,15},{18,16},{20,... | collective-permute-start | bytes 998408 | tf_op jit(solution)/shard_map/ppermute | solution.py:51
  44.9 27.5 %collective-permute-start.14 = (bf16[1024,896]{1,0:T(8,128)(2,1)S(1)}, bf16[1024,896]{1,0:T(8,128)(2,1)}, u32[]{:S(2)}, u32[]{:S(2)}) collective-permute-start(bf16[1024,896]{1,0:T(8,128)(2,1)S(1)} %copy-done), channel_id=1, source_target_pairs={{0,1},{1,0},{2,3},{3,2},{4,5},{5,4},{6,7},{7,6},{8,9},{9,8},{10,11... | collective-permute-start | bytes 5505032 | tf_op jit(solution)/shard_map/ppermute | solution.py:55
  45.1 21.5 %collective-permute-start.13 = (bf16[104,2880]{1,0:T(8,128)(2,1)}, bf16[104,2880]{1,0:T(8,128)(2,1)}, u32[]{:S(2)}, u32[]{:S(2)}) collective-permute-start(bf16[104,2880]{1,0:T(8,128)(2,1)} %fusion.10), channel_id=1, source_target_pairs={{2,4},{4,2},{3,5},{5,3},{10,12},{12,10},{11,13},{13,11},{18,20},{2... | collective-permute-start | bytes 1797128 | tf_op jit(solution)/shard_map/ppermute | solution.py:51
  46.6 22.5 %collective-permute-start.12 = (bf16[104,2880]{1,0:T(8,128)(2,1)}, bf16[104,2880]{1,0:T(8,128)(2,1)}, u32[]{:S(2)}, u32[]{:S(2)}) collective-permute-start(bf16[104,2880]{1,0:T(8,128)(2,1)} %fusion.10), channel_id=1, source_target_pairs={{0,2},{2,0},{4,6},{6,4},{1,3},{3,1},{5,7},{7,5},{8,10},{10,8},{12,... | collective-permute-start | bytes 1797128 | tf_op jit(solution)/shard_map/ppermute | solution.py:51
  54.5 17.5 %collective-permute-start.11 = (bf16[208,1600]{1,0:T(8,128)(2,1)S(1)}, bf16[208,1600]{1,0:T(8,128)(2,1)}, u32[]{:S(2)}, u32[]{:S(2)}) collective-permute-start(bf16[208,1600]{1,0:T(8,128)(2,1)S(1)} %pad_maximum_fusion.4.rest_1_), channel_id=1, source_target_pairs={{0,16},{16,0},{8,24},{24,8},{1,17},{17,1},{9,25},{25,9},{2,18},{18... | collective-permute-start | bytes 1996808 | tf_op jit(solution)/shard_map/ppermute | solution.py:47
  55.2 17.2 %collective-permute-start.10 = (bf16[208,1600]{1,0:T(8,128)(2,1)S(1)}, bf16[208,1600]{1,0:T(8,128)(2,1)}, u32[]{:S(2)}, u32[]{:S(2)}) collective-permute-start(bf16[208,1600]{1,0:T(8,128)(2,1)S(1)} %pad_maximum_fusion.4.rest_1_), channel_id=1, source_target_pairs={{0,8},{8,0},{16,24},{24,16},{1,9},{9,1},{17,25},{25,17},{2,10},{10... | collective-permute-start | bytes 1996808 | tf_op jit(solution)/shard_map/ppermute | solution.py:43
  72.4 18.2 %collective-permute-start.15 = (bf16[208,1600]{1,0:T(8,128)(2,1)}, bf16[208,1600]{1,0:T(8,128)(2,1)S(1)}, u32[]{:S(2)}, u32[]{:S(2)}) collective-permute-start(bf16[208,1600]{1,0:T(8,128)(2,1)} %collective-permute-done.5.rest_2_), channel_id=1, source_target_pairs={{0,16},{16,0},{8,24},{24,8},{1,17},{17,1},{9,25},{25,9},{2,18},{18... | collective-permute-start | bytes 1996808 | tf_op jit(solution)/shard_map/ppermute | solution.py:47
  73.8 16.9 %collective-permute-start.16 = (bf16[208,1600]{1,0:T(8,128)(2,1)}, bf16[208,1600]{1,0:T(8,128)(2,1)S(1)}, u32[]{:S(2)}, u32[]{:S(2)}) collective-permute-start(bf16[208,1600]{1,0:T(8,128)(2,1)} %collective-permute-done.11.rest_5_), channel_id=1, source_target_pairs={{0,8},{8,0},{16,24},{24,16},{1,9},{9,1},{17,25},{25,17},{2,10},{10... | collective-permute-start | bytes 1996808 | tf_op jit(solution)/shard_map/ppermute | solution.py:43
  74.3 32.5 %collective-permute-start.18 = (bf16[104,2880]{1,0:T(8,128)(2,1)}, bf16[104,2880]{1,0:T(8,128)(2,1)S(1)}, u32[]{:S(2)}, u32[]{:S(2)}) collective-permute-start(bf16[104,2880]{1,0:T(8,128)(2,1)} %collective-permute-done.13), channel_id=1, source_target_pairs={{2,0},{4,6},{3,1},{5,7},{10,8},{12,14},{11,9},{13,15},{18,16},{20,... | collective-permute-start | bytes 1797128 | tf_op jit(solution)/shard_map/ppermute | solution.py:51
  75.6 31.2 %collective-permute-start.19 = (bf16[104,2880]{1,0:T(8,128)(2,1)}, bf16[104,2880]{1,0:T(8,128)(2,1)S(1)}, u32[]{:S(2)}, u32[]{:S(2)}) collective-permute-start(bf16[104,2880]{1,0:T(8,128)(2,1)} %collective-permute-done.12), channel_id=1, source_target_pairs={{4,0},{2,6},{5,1},{3,7},{12,8},{10,14},{13,9},{11,15},{20,16},{18,... | collective-permute-start | bytes 1797128 | tf_op jit(solution)/shard_map/ppermute | solution.py:51
  76.9 29.9 %collective-permute-start.17 = (bf16[104,2880]{1,0:T(8,128)(2,1)}, bf16[104,2880]{1,0:T(8,128)(2,1)S(1)}, u32[]{:S(2)}, u32[]{:S(2)}) collective-permute-start(bf16[104,2880]{1,0:T(8,128)(2,1)} %collective-permute-done.12), channel_id=1, source_target_pairs={{2,4},{4,2},{3,5},{5,3},{10,12},{12,10},{11,13},{13,11},{18,20},{2... | collective-permute-start | bytes 1797128 | tf_op jit(solution)/shard_map/ppermute | solution.py:51
  108.3 30.5 %collective-permute-start.21 = (bf16[416,1600]{1,0:T(8,128)(2,1)S(1)}, bf16[416,1600]{1,0:T(8,128)(2,1)S(1)}, u32[]{:S(2)}, u32[]{:S(2)}) collective-permute-start(bf16[416,1600]{1,0:T(8,128)(2,1)S(1)} %pad_maximum_fusion.2.rest_0_), channel_id=1, source_target_pairs={{0,16},{16,0},{8,24},{24,8},{1,17},{17,1},{9,25},{25,9},{2,18},{18... | collective-permute-start | bytes 3993608 | tf_op jit(solution)/shard_map/ppermute | solution.py:47
  109.1 30.2 %collective-permute-start.20 = (bf16[416,1600]{1,0:T(8,128)(2,1)S(1)}, bf16[416,1600]{1,0:T(8,128)(2,1)S(1)}, u32[]{:S(2)}, u32[]{:S(2)}) collective-permute-start(bf16[416,1600]{1,0:T(8,128)(2,1)S(1)} %pad_maximum_fusion.2.rest_0_), channel_id=1, source_target_pairs={{0,8},{8,0},{16,24},{24,16},{1,9},{9,1},{17,25},{25,17},{2,10},{10... | collective-permute-start | bytes 3993608 | tf_op jit(solution)/shard_map/ppermute | solution.py:43
  110.6 42.6 %collective-permute-start.26 = (bf16[416,1600]{1,0:T(8,128)(2,1)S(1)}, bf16[416,1600]{1,0:T(8,128)(2,1)}, u32[]{:S(2)}, u32[]{:S(2)}) collective-permute-start(bf16[416,1600]{1,0:T(8,128)(2,1)S(1)} %pad_maximum_fusion.1.rest_0_), channel_id=1, source_target_pairs={{2,4},{4,2},{3,5},{5,3},{10,12},{12,10},{11,13},{13,11},{18,20},{2... | collective-permute-start | bytes 3993608 | tf_op jit(solution)/shard_map/ppermute | solution.py:51
  112.3 40.8 %collective-permute-start.25 = (bf16[416,1600]{1,0:T(8,128)(2,1)S(1)}, bf16[416,1600]{1,0:T(8,128)(2,1)}, u32[]{:S(2)}, u32[]{:S(2)}) collective-permute-start(bf16[416,1600]{1,0:T(8,128)(2,1)S(1)} %pad_maximum_fusion.1.rest_0_), channel_id=1, source_target_pairs={{0,2},{2,0},{4,6},{6,4},{1,3},{3,1},{5,7},{7,5},{8,10},{10,8},{12,... | collective-permute-start | bytes 3993608 | tf_op jit(solution)/shard_map/ppermute | solution.py:51
  139.4 26.5 %collective-permute-start.24 = (bf16[208,1600]{1,0:T(8,128)(2,1)S(1)}, bf16[208,1600]{1,0:T(8,128)(2,1)}, u32[]{:S(2)}, u32[]{:S(2)}) collective-permute-start(bf16[208,1600]{1,0:T(8,128)(2,1)S(1)} %slice.72), channel_id=1, source_target_pairs={{0,8},{8,0},{16,24},{24,16},{1,9},{9,1},{17,25},{25,17},{2,10},{10... | collective-permute-start | bytes 1996808 | tf_op jit(solution)/shard_map/ppermute | solution.py:43
  140.9 25.0 %collective-permute-start.23 = (bf16[208,1600]{1,0:T(8,128)(2,1)S(1)}, bf16[208,1600]{1,0:T(8,128)(2,1)}, u32[]{:S(2)}, u32[]{:S(2)}) collective-permute-start(bf16[208,1600]{1,0:T(8,128)(2,1)S(1)} %slice.71), channel_id=1, source_target_pairs={{0,16},{16,0},{8,24},{24,8},{1,17},{17,1},{9,25},{25,9},{2,18},{18... | collective-permute-start | bytes 1996808 | tf_op jit(solution)/shard_map/ppermute | solution.py:47
  153.1 37.0 %collective-permute-start.30 = (bf16[416,1600]{1,0:T(8,128)(2,1)}, bf16[416,1600]{1,0:T(8,128)(2,1)}, u32[]{:S(2)}, u32[]{:S(2)}) collective-permute-start(bf16[416,1600]{1,0:T(8,128)(2,1)} %collective-permute-done.26.rest_0_), channel_id=1, source_target_pairs={{2,0},{4,6},{3,1},{5,7},{10,8},{12,14},{11,9},{13,15},{18,16},{20,... | collective-permute-start | bytes 3993608 | tf_op jit(solution)/shard_map/ppermute | solution.py:51
  154.4 35.7 %collective-permute-start.29 = (bf16[416,1600]{1,0:T(8,128)(2,1)}, bf16[416,1600]{1,0:T(8,128)(2,1)}, u32[]{:S(2)}, u32[]{:S(2)}) collective-permute-start(bf16[416,1600]{1,0:T(8,128)(2,1)} %collective-permute-done.25.rest_1_), channel_id=1, source_target_pairs={{2,4},{4,2},{3,5},{5,3},{10,12},{12,10},{11,13},{13,11},{18,20},{2... | collective-permute-start | bytes 3993608 | tf_op jit(solution)/shard_map/ppermute | solution.py:51
  165.9 24.2 %collective-permute-start.28 = (bf16[416,1280]{1,0:T(8,128)(2,1)S(1)}, bf16[416,1280]{1,0:T(8,128)(2,1)S(1)}, u32[]{:S(2)}, u32[]{:S(2)}) collective-permute-start(bf16[416,1280]{1,0:T(8,128)(2,1)S(1)} %pad_maximum_fusion.3.rest_0_), channel_id=1, source_target_pairs={{0,16},{16,0},{8,24},{24,8},{1,17},{17,1},{9,25},{25,9},{2,18},{18... | collective-permute-start | bytes 3194888 | tf_op jit(solution)/shard_map/ppermute | solution.py:47
  166.7 23.5 %collective-permute-start.27 = (bf16[416,1280]{1,0:T(8,128)(2,1)S(1)}, bf16[416,1280]{1,0:T(8,128)(2,1)S(1)}, u32[]{:S(2)}, u32[]{:S(2)}) collective-permute-start(bf16[416,1280]{1,0:T(8,128)(2,1)S(1)} %pad_maximum_fusion.3.rest_0_), channel_id=1, source_target_pairs={{0,8},{8,0},{16,24},{24,16},{1,9},{9,1},{17,25},{25,17},{2,10},{10... | collective-permute-start | bytes 3194888 | tf_op jit(solution)/shard_map/ppermute | solution.py:43
  190.2 39.7 %collective-permute-start.33 = (bf16[416,1600]{1,0:T(8,128)(2,1)}, bf16[416,1600]{1,0:T(8,128)(2,1)S(1)}, u32[]{:S(2)}, u32[]{:S(2)}) collective-permute-start(bf16[416,1600]{1,0:T(8,128)(2,1)} %collective-permute-done.25.rest_1_), channel_id=1, source_target_pairs={{4,0},{2,6},{5,1},{3,7},{12,8},{10,14},{13,9},{11,15},{20,16},{18,... | collective-permute-start | bytes 3993608 | tf_op jit(solution)/shard_map/ppermute | solution.py:51
  229.9 13.1 %collective-permute-start.34 = (bf16[1024,1024]{1,0:T(8,128)(2,1)}, bf16[1024,1024]{1,0:T(8,128)(2,1)S(1)}, u32[]{:S(2)}, u32[]{:S(2)}) collective-permute-start(bf16[1024,1024]{1,0:T(8,128)(2,1)} %get-tuple-element.179), channel_id=1, source_target_pairs={{0,1},{1,0},{2,3},{3,2},{4,5},{5,4},{6,7},{7,6},{8,9},{9,8},{10,11... | collective-permute-start | bytes 6291464 | tf_op jit(solution)/shard_map/ppermute | solution.py:55
  259.7 12.7 %collective-permute-start.39 = (bf16[128,800]{1,0:T(8,128)(2,1)}, bf16[128,800]{1,0:T(8,128)(2,1)S(1)}, u32[]{:S(2)}, u32[]{:S(2)}) collective-permute-start(bf16[128,800]{1,0:T(8,128)(2,1)} %get-tuple-element.190), channel_id=1, source_target_pairs={{0,24},{24,0},{8,16},{16,8},{1,25},{25,1},{9,17},{17,9},{2,26},{26... | collective-permute-start | bytes 614408 | tf_op jit(solution)/shard_map/ppermute | solution.py:1006
  (59 other events, 482.0 us)

commit v5 on v4

--- a/solution.py
+++ b/solution.py
@@ -974,12 +974,13 @@
         gated = gate(
             rows_own, rows_other, scanned, (gate_block,) + tuple(gate_p1) + tuple(gate_p2), 0
         )
+
+        attn_p1, gated = tie(attn_p1, gated)
+        attn_p2 = plane_second(attn_p1)
         keep_early, send_early = ssm_out(gated, (1, 1), (ssm_block, ssm_near))
-
-        attn_p1, keep_early, crossed, ends, ssm_near = tie(
-            attn_p1, keep_early, crossed, ends, ssm_near
-        )
-        attn_p2 = plane_second(attn_p1)
+        attn_p2, keep_early, crossed, ends, ssm_near = tie(
+            attn_p2, keep_early, crossed, ends, ssm_near
+        )
         far = along_z(ssm_near, Z_FAR)
         got_early = other_core(send_early)
         attn_pieces = (attn_block,) + tuple(attn_p1) + tuple(attn_p2)

time: 291 us -> 291 us (level); the launches traced: 286 us -> 289 us
  waiting for transfers between devices: 35.1 us -> 38.4 us
    ppermute x10, waiting for transfers between devices: 10.4 us -> 1.64 us  [swap_x(): return lax.ppermute(value, 'rep', X_PAIRS)]
    ppermute x15, waiting for transfers between devices: 2.99 us -> 9.41 us  [along_z(): return lax.ppermute(value, 'tr', pairs)]
    ppermute x10, waiting for transfers between devices: 11.2 us -> 16.8 us  [swap_y(): return lax.ppermute(value, 'rep', Y_PAIRS)]
    unnamed x97 -> x105, local copies, waits for them, and re-layouts: 6.51 us -> 5.3 us
  transfers between devices with their start and end apart: 44 -> 44, of which waited for: 16 -> 19; matrix products, arithmetic and copies ran while one was open for 10% -> 10% of each run, Pallas kernels for 46% -> 46%
where the time goes in v5:
time: 291 us; the launch traced here: 289 us
  Pallas kernels  144 us (49%)
  starting transfers between devices  63.1 us (22%)
  waiting for transfers between devices  38.4 us (13%)
  local copies, waits for them, and re-layouts  21.7 us (7%)
  other arithmetic  18.8 us (6%)
    pallas_call x3, Pallas kernels, scan(): call(functools.partial(scan_kernel, slots), 1, count, [blocks(channels),...  35.8 us
    ppermute x15, starting transfers between devices, along_z(): return lax.ppermute(value, 'tr', pairs)  35.7 us
    pallas_call x2, Pallas kernels, ssm_out(): call(functools.partial(ssm_out_kernel, choices, section // len(choices)),...  18.3 us
    pallas_call x1, Pallas kernels, attention(): call(functools.partial(attention_kernel, slots, group_rows, kv_here, per_...  17.4 us
    ppermute x10, waiting for transfers between devices, swap_y(): return lax.ppermute(value, 'rep', Y_PAIRS)  16.8 us
    pallas_call x1, Pallas kernels, convolve(): call(functools.partial(conv_kernel, slots, group_rows, len(pieces), half,...  15 us
    pallas_call x2, Pallas kernels, mix(): call(functools.partial(mixed_kernel, slots, part * here, sections, here),...  13.3 us
    pallas_call x1, Pallas kernels, gate(): call(functools.partial(gate_kernel, len(pieces), half, first_column), 1,...  13.1 us
  transfers between devices with their start and end apart: 44, of which 19 were waited for; matrix products, arithmetic and copies ran while one was open for 10% of the time, Pallas kernels for 46%

profile of v5, /device:TPU:0, one launch (start us, length us, event | category | flops | bytes accessed | tf_op | source)
XLA Modules:
  0.0 289.3 jit_solution(4672998259783904164)
XLA Ops:
  1.0 4.0 %collective-permute-start.4 = (bf16[104,1600]{1,0:T(8,128)(2,1)S(1)}, bf16[104,1600]{1,0:T(8,128)(2,1)S(1)}, u32[]{:S(2)}, u32[]{:S(2)}) collective-permute-start(bf16[104,1600]{1,0:T(8,128)(2,1)S(1)} %pad.19), channel_id=1, source_target_pairs={{0,24},{24,0},{8,16},{16,8},{1,25},{25,1},{9,17},{17,9},{2,26},{26... | collective-permute-start | bytes 998408 | tf_op jit(solution)/shard_map/ppermute | solution.py:890
  5.0 2.5 fusion.25
  9.8 4.2 %collective-permute-start = (bf16[104,1600]{1,0:T(8,128)(2,1)S(1)}, bf16[104,1600]{1,0:T(8,128)(2,1)S(1)}, u32[]{:S(2)}, u32[]{:S(2)}) collective-permute-start(bf16[104,1600]{1,0:T(8,128)(2,1)S(1)} %pad.20), channel_id=1, source_target_pairs={{0,2},{2,0},{4,6},{6,4},{1,3},{3,1},{5,7},{7,5},{8,10},{10,8},{12,... | collective-permute-start | bytes 998408 | tf_op jit(solution)/shard_map/ppermute | solution.py:51
  15.2 2.5 psum.7
  17.7 2.8 collective-permute-done.3
  31.7 9.6 %spread_rows.1.rows_own = bf16[1024,896]{1,0:T(8,128)(2,1)} custom-call(s32[8]{0:T(128)} %select_reduce_fusion.1.proc, bf16[8,128,800]{2,1,0:T(8,128)(2,1)} %bitcast.23, f32[8,128,1]{2,1,0:T(8,128)} %copy.38.inv_rms, f32[1,800]{1,0:T(1,128)} %broadcast_in_dim.113.gain, bf16[800,896]{1,0:T(8,128)(2,1)} %fusion.1.pick), custom_call_target="tpu_custom_call" | custom-call | flops 80000000 | bytes 4096 | tf_op jit(solution)/shard_map/spread_rows/pallas_call | solution.py:612
  46.6 8.7 %collective-permute-start.12 = (bf16[104,2880]{1,0:T(8,128)(2,1)}, bf16[104,2880]{1,0:T(8,128)(2,1)}, u32[]{:S(2)}, u32[]{:S(2)}) collective-permute-start(bf16[104,2880]{1,0:T(8,128)(2,1)} %fusion.10), channel_id=1, source_target_pairs={{0,2},{2,0},{4,6},{6,4},{1,3},{3,1},{5,7},{7,5},{8,10},{10,8},{12,... | collective-permute-start | bytes 1797128 | tf_op jit(solution)/shard_map/ppermute | solution.py:51
  64.0 2.0 iota_compare_fusion.1
  67.3 2.6 collective-permute-done.12
  69.8 3.0 %collective-permute-done.11.rest_5_ = bf16[208,1600]{1,0:T(8,128)(2,1)} collective-permute-done((bf16[208,1600]{1,0:T(8,128)(2,1)S(1)}, bf16[208,1600]{1,0:T(8,128)(2,1)}, u32[]{:S(2)}, u32[]{:S(2)}) %collective-permute-start.11) | collective-permute-done | bytes 665632 | tf_op jit(solution)/shard_map/ppermute | solution.py:47
  81.2 9.1 %place_rows.1.x_keep = bf16[1024,1024]{1,0:T(8,128)(2,1)} custom-call(s32[8]{0:T(128)} %select_reduce_fusion.1.proc, bf16[8,128,800]{2,1,0:T(8,128)(2,1)} %bitcast.24, bf16[800,1024]{1,0:T(8,128)(2,1)} %get-tuple-element.140.pick), custom_call_target="tpu_custom_call" | custom-call | flops 80000000 | bytes 4096 | tf_op jit(solution)/shard_map/place_rows/pallas_call | solution.py:630
  91.8 15.0 %convolve.1 = (bf16[1024,1600]{1,0:T(8,128)(2,1)}, bf16[1024,256]{1,0:T(8,128)(2,1)}) custom-call(s32[8]{0:T(128)} %select_reduce_fusion.1.proc, s32[1]{0:T(128)} %bitcast.8.second, bf16[1024,896]{1,0:T(8,128)(2,1)} %spread_rows.1.rows_own, bf16[1024,896]{1,0:T(8,128)(2,1)} %collective-permute-done.14.rows_other, f32[8,3,1600]{2,1,0:T(4,128)} %copy.41.history, ...), custom_call_target="tpu_custom_call" | custom-call | flops 140000000 | bytes 4096 | tf_op jit(solution)/shard_map/convolve/pallas_call | solution.py:678
  110.3 1.8 collective-permute-start.26
  112.1 6.3 %collective-permute-start.25 = (bf16[416,1600]{1,0:T(8,128)(2,1)S(1)}, bf16[416,1600]{1,0:T(8,128)(2,1)}, u32[]{:S(2)}, u32[]{:S(2)}) collective-permute-start(bf16[416,1600]{1,0:T(8,128)(2,1)S(1)} %pad_maximum_fusion.1.rest_0_), channel_id=1, source_target_pairs={{0,2},{2,0},{4,6},{6,4},{1,3},{3,1},{5,7},{7,5},{8,10},{10,8},{12,... | collective-permute-start | bytes 3993608 | tf_op jit(solution)/shard_map/ppermute | solution.py:51
  121.2 16.4 %scan_states.3.rest_0_ = f32[1024,1600]{1,0:T(8,128)} custom-call(s32[8]{0:T(128)} %select_reduce_fusion.1.proc, bf16[1024,1600]{1,0:T(8,128)(2,1)} %get-tuple-element.161.conv, bf16[1024,256]{1,0:T(8,128)(2,1)} %get-tuple-element.162.mix_own, bf16[1024,256]{1,0:T(8,128)(2,1)} %copy-done.11, bf16[100,1600]{1,0:T(8,128)(2,1)} %step_weight.5, ...), custom_call_target="tpu_custom_call" | custom-call | flops 160000000 | bytes 4096 | tf_op jit(solution)/shard_map/scan_states/pallas_call | solution.py:711
  143.5 9.7 %scan_states.4.rest_0_ = f32[1024,1600]{1,0:T(8,128)} custom-call(s32[8]{0:T(128)} %select_reduce_fusion.1.proc, bf16[1024,1600]{1,0:T(8,128)(2,1)} %get-tuple-element.161.conv, bf16[1024,256]{1,0:T(8,128)(2,1)} %get-tuple-element.162.mix_own, bf16[1024,256]{1,0:T(8,128)(2,1)} %copy-done.11, ...), custom_call_target="tpu_custom_call", output_to_operand_aliasing={{}: (9, {})} | custom-call | flops 80000000 | bytes 4096 | tf_op jit(solution)/shard_map/scan_states/pallas_call | solution.py:711
  153.2 9.6 %scan_states.5.scanned = f32[1024,1600]{1,0:T(8,128)} custom-call(s32[8]{0:T(128)} %select_reduce_fusion.1.proc, bf16[1024,1600]{1,0:T(8,128)(2,1)} %get-tuple-element.161.conv, bf16[1024,256]{1,0:T(8,128)(2,1)} %get-tuple-element.162.mix_own, bf16[1024,256]{1,0:T(8,128)(2,1)} %copy-done.11, ...), custom_call_target="tpu_custom_call", output_to_operand_aliasing={{}: (9, {})} | custom-call | flops 80000000 | bytes 4096 | tf_op jit(solution)/shard_map/scan_states/pallas_call | solution.py:711
  165.3 1.8 collective-permute-start.31
  167.1 13.1 %gate.1.gated = bf16[1024,1600]{1,0:T(8,128)(2,1)} custom-call(s32[1]{0:T(128)} %bitcast.8.second, bf16[1024,896]{1,0:T(8,128)(2,1)} %spread_rows.1.rows_own, bf16[1024,896]{1,0:T(8,128)(2,1)} %collective-permute-done.14.rows_other, f32[1024,1600]{1,0:T(8,128)} %scan_states.5.scanned, bf16[416,1600]{1,0:T(8,128)(2,1)} %copy-done.9, ...), custom_call_target="tpu_custom_call" | custom-call | flops 130000000 | bytes 4096 | tf_op jit(solution)/shard_map/gate/pallas_call | solution.py:748
  180.2 5.8 %collective-permute-done.28.rest_2_ = bf16[416,1280]{1,0:T(8,128)(2,1)S(1)} collective-permute-done((bf16[416,1280]{1,0:T(8,128)(2,1)S(1)}, bf16[416,1280]{1,0:T(8,128)(2,1)S(1)}, u32[]{:S(2)}, u32[]{:S(2)}) %collective-permute-start.28) | collective-permute-done | bytes 1064992 | tf_op jit(solution)/shard_map/ppermute | solution.py:47
  191.5 9.1 %ssm_out.2 = (bf16[1024,512]{1,0:T(8,128)(2,1)}, bf16[1024,512]{1,0:T(8,128)(2,1)}) custom-call(s32[2]{0:T(128)} %pad_add_fusion.scalars, bf16[1024,1600]{1,0:T(8,128)(2,1)} %gate.1.gated, bf16[416,1600]{1,0:T(8,128)(2,1)} %copy-done.8, bf16[416,1600]{1,0:T(8,128)(2,1)} %collective-permute-done.25.rest_1_), custom_call_target="tpu_custom_call" | custom-call | flops 80000000 | bytes 4096 | tf_op jit(solution)/shard_map/ssm_out/pallas_call | solution.py:791
  202.5 17.4 %attention.1.heads = bf16[1024,512]{1,0:T(8,128)(2,1)} custom-call(s32[8]{0:T(128)} %select_reduce_fusion.1.proc, s32[8]{0:T(128)} %dynamic_slice.13.lengths, s32[1]{0:T(128)} %bitcast.8.second, bf16[1024,896]{1,0:T(8,128)(2,1)} %spread_rows.1.rows_own, bf16[1024,896]{1,0:T(8,128)(2,1)} %collective-permute-done.14.rows_other, bf16[8,256,256]{2,1,0:T(8,128)(2,1)} %cache.1, ...), custom_call_target="tpu_custom_call" | custom-call | flops 150000000 | bytes 4096 | tf_op jit(solution)/shard_map/attention/pallas_call | solution.py:643
  219.9 7.0 %attn_out.1 = (bf16[1024,1024]{1,0:T(8,128)(2,1)}, bf16[1024,1024]{1,0:T(8,128)(2,1)}) custom-call(s32[1]{0:T(128)} %bitcast.8.second, bf16[1024,512]{1,0:T(8,128)(2,1)} %attention.1.heads, bf16[416,1280]{1,0:T(8,128)(2,1)} %copy-done.3, bf16[416,1280]{1,0:T(8,128)(2,1)} %copy-done.7, bf16[416,1280]{1,0:T(8,128)(2,1)} %copy-done.6, ...), custom_call_target="tpu_custom_call" | custom-call | flops 60000000 | bytes 4096 | tf_op jit(solution)/shard_map/attn_out/pallas_call | solution.py:773
  226.9 6.0 %collective-permute-done.33.rest_3_ = bf16[416,1600]{1,0:T(8,128)(2,1)S(1)} collective-permute-done((bf16[416,1600]{1,0:T(8,128)(2,1)}, bf16[416,1600]{1,0:T(8,128)(2,1)S(1)}, u32[]{:S(2)}, u32[]{:S(2)}) %collective-permute-start.33) | collective-permute-done | bytes 1331232 | tf_op jit(solution)/shard_map/ppermute | solution.py:51
  234.0 9.1 %ssm_out.3 = (bf16[1024,512]{1,0:T(8,128)(2,1)}, bf16[1024,512]{1,0:T(8,128)(2,1)}) custom-call(s32[2]{0:T(128)} %pad_add_fusion.scalars, bf16[1024,1600]{1,0:T(8,128)(2,1)} %gate.1.gated, bf16[416,1600]{1,0:T(8,128)(2,1)} %collective-permute-done.26.rest_0_, bf16[416,1600]{1,0:T(8,128)(2,1)} %collective-permute-done.32.rest_1_, ...), custom_call_target="tpu_custom_call" | custom-call | flops 80000000 | bytes 4096 | tf_op jit(solution)/shard_map/ssm_out/pallas_call | solution.py:791
  243.3 2.8 collective-permute-done.36.refs_5_.rest_3_
  247.8 5.3 %squares.1.rest_4_ = f32[1024,2]{1,0:T(8,128)} custom-call(bf16[1024,1024]{1,0:T(8,128)(2,1)} %get-tuple-element.182.refs_0_.keep_attn, bf16[1024,1024]{1,0:T(8,128)(2,1)} %copy-done.1, bf16[1024,512]{1,0:T(8,128)(2,1)} %get-tuple-element.186.refs_2_.rest_0_, bf16[1024,512]{1,0:T(8,128)(2,1)} %copy-done.4, ...), custom_call_target="tpu_custom_call" | custom-call | flops 20000000 | bytes 4096 | tf_op jit(solution)/shard_map/squares/pallas_call | solution.py:807
  253.3 2.0 collective-permute-done.37.rest_5_
  256.1 6.7 %mixed_rows.3 = (bf16[128,800]{1,0:T(8,128)(2,1)}, bf16[128,800]{1,0:T(8,128)(2,1)}, bf16[128,800]{1,0:T(8,128)(2,1)}, bf16[128,800]{1,0:T(8,128)(2,1)}) custom-call(s32[8]{0:T(128)} %select_reduce_fusion.1.proc, s32[8]{0:T(128)} %dynamic_slice.14.sizes, bf16[1024,1024]{1,0:T(8,128)(2,1)} %place_rows.1.x_keep, ...), custom_call_target="tpu_custom_call" | custom-call | flops 40000000 | bytes 4096 | tf_op jit(solution)/shard_map/mixed_rows/pallas_call | solution.py:823
  266.3 6.7 %mixed_rows.2 = (bf16[128,800]{1,0:T(8,128)(2,1)}, bf16[128,800]{1,0:T(8,128)(2,1)}, bf16[128,800]{1,0:T(8,128)(2,1)}, bf16[128,800]{1,0:T(8,128)(2,1)}) custom-call(s32[8]{0:T(128)} %select_reduce_fusion.1.proc, s32[8]{0:T(128)} %dynamic_slice.14.sizes, bf16[1024,1024]{1,0:T(8,128)(2,1)} %place_rows.1.x_keep, ...), custom_call_target="tpu_custom_call" | custom-call | flops 40000000 | bytes 4096 | tf_op jit(solution)/shard_map/mixed_rows/pallas_call | solution.py:823
  277.0 5.8 %collective-permute-done.38 = bf16[128,800]{1,0:T(8,128)(2,1)S(1)} collective-permute-done((bf16[128,800]{1,0:T(8,128)(2,1)}, bf16[128,800]{1,0:T(8,128)(2,1)S(1)}, u32[]{:S(2)}, u32[]{:S(2)}) %collective-permute-start.38) | collective-permute-done | bytes 204832 | tf_op jit(solution)/shard_map/ppermute | solution.py:1007
  282.8 3.5 %collective-permute-done.40 = bf16[128,800]{1,0:T(8,128)(2,1)S(1)} collective-permute-done((bf16[128,800]{1,0:T(8,128)(2,1)}, bf16[128,800]{1,0:T(8,128)(2,1)S(1)}, u32[]{:S(2)}, u32[]{:S(2)}) %collective-permute-start.40) | collective-permute-done | bytes 204832 | tf_op jit(solution)/shard_map/ppermute | solution.py:47
  (231 shorter events, 76.7 us)
Async XLA Ops:
  1.0 16.6 %collective-permute-start.4 = (bf16[104,1600]{1,0:T(8,128)(2,1)S(1)}, bf16[104,1600]{1,0:T(8,128)(2,1)S(1)}, u32[]{:S(2)}, u32[]{:S(2)}) collective-permute-start(bf16[104,1600]{1,0:T(8,128)(2,1)S(1)} %pad.19), channel_id=1, source_target_pairs={{0,24},{24,0},{8,16},{16,8},{1,25},{25,1},{9,17},{17,9},{2,26},{26... | collective-permute-start | bytes 998408 | tf_op jit(solution)/shard_map/ppermute | solution.py:890
  7.6 12.9 %collective-permute-start.3 = (bf16[104,1600]{1,0:T(8,128)(2,1)S(1)}, bf16[104,1600]{1,0:T(8,128)(2,1)S(1)}, u32[]{:S(2)}, u32[]{:S(2)}) collective-permute-start(bf16[104,1600]{1,0:T(8,128)(2,1)S(1)} %pad.19), channel_id=1, source_target_pairs={{0,16},{16,0},{8,24},{24,8},{1,17},{17,1},{9,25},{25,9},{2,18},{18... | collective-permute-start | bytes 998408 | tf_op jit(solution)/shard_map/ppermute | solution.py:47
  8.2 12.6 %collective-permute-start.2 = (bf16[104,1600]{1,0:T(8,128)(2,1)S(1)}, bf16[104,1600]{1,0:T(8,128)(2,1)S(1)}, u32[]{:S(2)}, u32[]{:S(2)}) collective-permute-start(bf16[104,1600]{1,0:T(8,128)(2,1)S(1)} %pad.19), channel_id=1, source_target_pairs={{0,8},{8,0},{16,24},{24,16},{1,9},{9,1},{17,25},{25,17},{2,10},{10... | collective-permute-start | bytes 998408 | tf_op jit(solution)/shard_map/ppermute | solution.py:43
  21.0 22.7 %collective-permute-start.9 = (bf16[104,1600]{1,0:T(8,128)(2,1)S(1)}, bf16[104,1600]{1,0:T(8,128)(2,1)}, u32[]{:S(2)}, u32[]{:S(2)}) collective-permute-start(bf16[104,1600]{1,0:T(8,128)(2,1)S(1)} %collective-permute-done), channel_id=1, source_target_pairs={{4,0},{2,6},{5,1},{3,7},{12,8},{10,14},{13,9},{11,15},{20,16},{18,... | collective-permute-start | bytes 998408 | tf_op jit(solution)/shard_map/ppermute | solution.py:51
  22.4 21.4 %collective-permute-start.8 = (bf16[104,1600]{1,0:T(8,128)(2,1)S(1)}, bf16[104,1600]{1,0:T(8,128)(2,1)}, u32[]{:S(2)}, u32[]{:S(2)}) collective-permute-start(bf16[104,1600]{1,0:T(8,128)(2,1)S(1)} %collective-permute-done), channel_id=1, source_target_pairs={{2,4},{4,2},{3,5},{5,3},{10,12},{12,10},{11,13},{13,11},{18,20},{2... | collective-permute-start | bytes 998408 | tf_op jit(solution)/shard_map/ppermute | solution.py:51
  23.9 21.0 %collective-permute-start.6 = (bf16[208,1600]{1,0:T(8,128)(2,1)S(1)}, bf16[208,1600]{1,0:T(8,128)(2,1)}, u32[]{:S(2)}, u32[]{:S(2)}) collective-permute-start(bf16[208,1600]{1,0:T(8,128)(2,1)S(1)} %constant_dynamic-update-slice_fusion.rest_0_), channel_id=1, source_target_pairs={{0,16},{16,0},{8,24},{24,8},{1,17},{17,1},{9,25},{25,9},{2,18},{18... | collective-permute-start | bytes 1996808 | tf_op jit(solution)/shard_map/ppermute | solution.py:47
  25.2 19.7 %collective-permute-start.5 = (bf16[208,1600]{1,0:T(8,128)(2,1)S(1)}, bf16[208,1600]{1,0:T(8,128)(2,1)}, u32[]{:S(2)}, u32[]{:S(2)}) collective-permute-start(bf16[208,1600]{1,0:T(8,128)(2,1)S(1)} %constant_dynamic-update-slice_fusion.rest_0_), channel_id=1, source_target_pairs={{0,8},{8,0},{16,24},{24,16},{1,9},{9,1},{17,25},{25,17},{2,10},{10... | collective-permute-start | bytes 1996808 | tf_op jit(solution)/shard_map/ppermute | solution.py:43
  27.8 14.9 %collective-permute-start.7 = (bf16[104,1600]{1,0:T(8,128)(2,1)}, bf16[104,1600]{1,0:T(8,128)(2,1)}, u32[]{:S(2)}, u32[]{:S(2)}) collective-permute-start(bf16[104,1600]{1,0:T(8,128)(2,1)} %collective-permute-done.1), channel_id=1, source_target_pairs={{2,0},{4,6},{3,1},{5,7},{10,8},{12,14},{11,9},{13,15},{18,16},{20,... | collective-permute-start | bytes 998408 | tf_op jit(solution)/shard_map/ppermute | solution.py:51
  44.9 28.2 %collective-permute-start.14 = (bf16[1024,896]{1,0:T(8,128)(2,1)S(1)}, bf16[1024,896]{1,0:T(8,128)(2,1)}, u32[]{:S(2)}, u32[]{:S(2)}) collective-permute-start(bf16[1024,896]{1,0:T(8,128)(2,1)S(1)} %copy-done), channel_id=1, source_target_pairs={{0,1},{1,0},{2,3},{3,2},{4,5},{5,4},{6,7},{7,6},{8,9},{9,8},{10,11... | collective-permute-start | bytes 5505032 | tf_op jit(solution)/shard_map/ppermute | solution.py:55
  45.1 22.2 %collective-permute-start.13 = (bf16[104,2880]{1,0:T(8,128)(2,1)}, bf16[104,2880]{1,0:T(8,128)(2,1)}, u32[]{:S(2)}, u32[]{:S(2)}) collective-permute-start(bf16[104,2880]{1,0:T(8,128)(2,1)} %fusion.10), channel_id=1, source_target_pairs={{2,4},{4,2},{3,5},{5,3},{10,12},{12,10},{11,13},{13,11},{18,20},{2... | collective-permute-start | bytes 1797128 | tf_op jit(solution)/shard_map/ppermute | solution.py:51
  46.6 23.2 %collective-permute-start.12 = (bf16[104,2880]{1,0:T(8,128)(2,1)}, bf16[104,2880]{1,0:T(8,128)(2,1)}, u32[]{:S(2)}, u32[]{:S(2)}) collective-permute-start(bf16[104,2880]{1,0:T(8,128)(2,1)} %fusion.10), channel_id=1, source_target_pairs={{0,2},{2,0},{4,6},{6,4},{1,3},{3,1},{5,7},{7,5},{8,10},{10,8},{12,... | collective-permute-start | bytes 1797128 | tf_op jit(solution)/shard_map/ppermute | solution.py:51
  55.3 17.5 %collective-permute-start.11 = (bf16[208,1600]{1,0:T(8,128)(2,1)S(1)}, bf16[208,1600]{1,0:T(8,128)(2,1)}, u32[]{:S(2)}, u32[]{:S(2)}) collective-permute-start(bf16[208,1600]{1,0:T(8,128)(2,1)S(1)} %pad_maximum_fusion.4.rest_1_), channel_id=1, source_target_pairs={{0,16},{16,0},{8,24},{24,8},{1,17},{17,1},{9,25},{25,9},{2,18},{18... | collective-permute-start | bytes 1996808 | tf_op jit(solution)/shard_map/ppermute | solution.py:47
  55.9 17.2 %collective-permute-start.10 = (bf16[208,1600]{1,0:T(8,128)(2,1)S(1)}, bf16[208,1600]{1,0:T(8,128)(2,1)}, u32[]{:S(2)}, u32[]{:S(2)}) collective-permute-start(bf16[208,1600]{1,0:T(8,128)(2,1)S(1)} %pad_maximum_fusion.4.rest_1_), channel_id=1, source_target_pairs={{0,8},{8,0},{16,24},{24,16},{1,9},{9,1},{17,25},{25,17},{2,10},{10... | collective-permute-start | bytes 1996808 | tf_op jit(solution)/shard_map/ppermute | solution.py:43
  73.1 17.3 %collective-permute-start.15 = (bf16[208,1600]{1,0:T(8,128)(2,1)}, bf16[208,1600]{1,0:T(8,128)(2,1)S(1)}, u32[]{:S(2)}, u32[]{:S(2)}) collective-permute-start(bf16[208,1600]{1,0:T(8,128)(2,1)} %collective-permute-done.5.rest_2_), channel_id=1, source_target_pairs={{0,16},{16,0},{8,24},{24,8},{1,17},{17,1},{9,25},{25,9},{2,18},{18... | collective-permute-start | bytes 1996808 | tf_op jit(solution)/shard_map/ppermute | solution.py:47
  74.6 16.1 %collective-permute-start.16 = (bf16[208,1600]{1,0:T(8,128)(2,1)}, bf16[208,1600]{1,0:T(8,128)(2,1)S(1)}, u32[]{:S(2)}, u32[]{:S(2)}) collective-permute-start(bf16[208,1600]{1,0:T(8,128)(2,1)} %collective-permute-done.11.rest_5_), channel_id=1, source_target_pairs={{0,8},{8,0},{16,24},{24,16},{1,9},{9,1},{17,25},{25,17},{2,10},{10... | collective-permute-start | bytes 1996808 | tf_op jit(solution)/shard_map/ppermute | solution.py:43
  75.1 31.8 %collective-permute-start.18 = (bf16[104,2880]{1,0:T(8,128)(2,1)}, bf16[104,2880]{1,0:T(8,128)(2,1)S(1)}, u32[]{:S(2)}, u32[]{:S(2)}) collective-permute-start(bf16[104,2880]{1,0:T(8,128)(2,1)} %collective-permute-done.13), channel_id=1, source_target_pairs={{2,0},{4,6},{3,1},{5,7},{10,8},{12,14},{11,9},{13,15},{18,16},{20,... | collective-permute-start | bytes 1797128 | tf_op jit(solution)/shard_map/ppermute | solution.py:51
  76.4 30.5 %collective-permute-start.19 = (bf16[104,2880]{1,0:T(8,128)(2,1)}, bf16[104,2880]{1,0:T(8,128)(2,1)S(1)}, u32[]{:S(2)}, u32[]{:S(2)}) collective-permute-start(bf16[104,2880]{1,0:T(8,128)(2,1)} %collective-permute-done.12), channel_id=1, source_target_pairs={{4,0},{2,6},{5,1},{3,7},{12,8},{10,14},{13,9},{11,15},{20,16},{18,... | collective-permute-start | bytes 1797128 | tf_op jit(solution)/shard_map/ppermute | solution.py:51
  77.7 29.2 %collective-permute-start.17 = (bf16[104,2880]{1,0:T(8,128)(2,1)}, bf16[104,2880]{1,0:T(8,128)(2,1)S(1)}, u32[]{:S(2)}, u32[]{:S(2)}) collective-permute-start(bf16[104,2880]{1,0:T(8,128)(2,1)} %collective-permute-done.12), channel_id=1, source_target_pairs={{2,4},{4,2},{3,5},{5,3},{10,12},{12,10},{11,13},{13,11},{18,20},{2... | collective-permute-start | bytes 1797128 | tf_op jit(solution)/shard_map/ppermute | solution.py:51
  108.4 30.3 %collective-permute-start.21 = (bf16[416,1600]{1,0:T(8,128)(2,1)S(1)}, bf16[416,1600]{1,0:T(8,128)(2,1)S(1)}, u32[]{:S(2)}, u32[]{:S(2)}) collective-permute-start(bf16[416,1600]{1,0:T(8,128)(2,1)S(1)} %pad_maximum_fusion.2.rest_0_), channel_id=1, source_target_pairs={{0,16},{16,0},{8,24},{24,8},{1,17},{17,1},{9,25},{25,9},{2,18},{18... | collective-permute-start | bytes 3993608 | tf_op jit(solution)/shard_map/ppermute | solution.py:47
  109.1 29.9 %collective-permute-start.20 = (bf16[416,1600]{1,0:T(8,128)(2,1)S(1)}, bf16[416,1600]{1,0:T(8,128)(2,1)S(1)}, u32[]{:S(2)}, u32[]{:S(2)}) collective-permute-start(bf16[416,1600]{1,0:T(8,128)(2,1)S(1)} %pad_maximum_fusion.2.rest_0_), channel_id=1, source_target_pairs={{0,8},{8,0},{16,24},{24,16},{1,9},{9,1},{17,25},{25,17},{2,10},{10... | collective-permute-start | bytes 3993608 | tf_op jit(solution)/shard_map/ppermute | solution.py:43
  110.3 42.8 %collective-permute-start.26 = (bf16[416,1600]{1,0:T(8,128)(2,1)S(1)}, bf16[416,1600]{1,0:T(8,128)(2,1)}, u32[]{:S(2)}, u32[]{:S(2)}) collective-permute-start(bf16[416,1600]{1,0:T(8,128)(2,1)S(1)} %pad_maximum_fusion.1.rest_0_), channel_id=1, source_target_pairs={{2,4},{4,2},{3,5},{5,3},{10,12},{12,10},{11,13},{13,11},{18,20},{2... | collective-permute-start | bytes 3993608 | tf_op jit(solution)/shard_map/ppermute | solution.py:51
  112.1 41.0 %collective-permute-start.25 = (bf16[416,1600]{1,0:T(8,128)(2,1)S(1)}, bf16[416,1600]{1,0:T(8,128)(2,1)}, u32[]{:S(2)}, u32[]{:S(2)}) collective-permute-start(bf16[416,1600]{1,0:T(8,128)(2,1)S(1)} %pad_maximum_fusion.1.rest_0_), channel_id=1, source_target_pairs={{0,2},{2,0},{4,6},{6,4},{1,3},{3,1},{5,7},{7,5},{8,10},{10,8},{12,... | collective-permute-start | bytes 3993608 | tf_op jit(solution)/shard_map/ppermute | solution.py:51
  139.1 23.7 %collective-permute-start.24 = (bf16[208,1600]{1,0:T(8,128)(2,1)S(1)}, bf16[208,1600]{1,0:T(8,128)(2,1)S(1)}, u32[]{:S(2)}, u32[]{:S(2)}) collective-permute-start(bf16[208,1600]{1,0:T(8,128)(2,1)S(1)} %slice.72), channel_id=1, source_target_pairs={{0,8},{8,0},{16,24},{24,16},{1,9},{9,1},{17,25},{25,17},{2,10},{10... | collective-permute-start | bytes 1996808 | tf_op jit(solution)/shard_map/ppermute | solution.py:43
  140.7 22.1 %collective-permute-start.23 = (bf16[208,1600]{1,0:T(8,128)(2,1)S(1)}, bf16[208,1600]{1,0:T(8,128)(2,1)}, u32[]{:S(2)}, u32[]{:S(2)}) collective-permute-start(bf16[208,1600]{1,0:T(8,128)(2,1)S(1)} %slice.71), channel_id=1, source_target_pairs={{0,16},{16,0},{8,24},{24,8},{1,17},{17,1},{9,25},{25,9},{2,18},{18... | collective-permute-start | bytes 1996808 | tf_op jit(solution)/shard_map/ppermute | solution.py:47
  162.8 23.1 %collective-permute-start.28 = (bf16[416,1280]{1,0:T(8,128)(2,1)S(1)}, bf16[416,1280]{1,0:T(8,128)(2,1)S(1)}, u32[]{:S(2)}, u32[]{:S(2)}) collective-permute-start(bf16[416,1280]{1,0:T(8,128)(2,1)S(1)} %pad_maximum_fusion.3.rest_0_), channel_id=1, source_target_pairs={{0,16},{16,0},{8,24},{24,8},{1,17},{17,1},{9,25},{25,9},{2,18},{18... | collective-permute-start | bytes 3194888 | tf_op jit(solution)/shard_map/ppermute | solution.py:47
  163.5 22.9 %collective-permute-start.27 = (bf16[416,1280]{1,0:T(8,128)(2,1)S(1)}, bf16[416,1280]{1,0:T(8,128)(2,1)S(1)}, u32[]{:S(2)}, u32[]{:S(2)}) collective-permute-start(bf16[416,1280]{1,0:T(8,128)(2,1)S(1)} %pad_maximum_fusion.3.rest_0_), channel_id=1, source_target_pairs={{0,8},{8,0},{16,24},{24,16},{1,9},{9,1},{17,25},{25,17},{2,10},{10... | collective-permute-start | bytes 3194888 | tf_op jit(solution)/shard_map/ppermute | solution.py:43
  164.0 36.7 %collective-permute-start.32 = (bf16[416,1600]{1,0:T(8,128)(2,1)}, bf16[416,1600]{1,0:T(8,128)(2,1)}, u32[]{:S(2)}, u32[]{:S(2)}) collective-permute-start(bf16[416,1600]{1,0:T(8,128)(2,1)} %collective-permute-done.26.rest_0_), channel_id=1, source_target_pairs={{2,0},{4,6},{3,1},{5,7},{10,8},{12,14},{11,9},{13,15},{18,16},{20,... | collective-permute-start | bytes 3993608 | tf_op jit(solution)/shard_map/ppermute | solution.py:51
  165.3 35.4 %collective-permute-start.31 = (bf16[416,1600]{1,0:T(8,128)(2,1)}, bf16[416,1600]{1,0:T(8,128)(2,1)}, u32[]{:S(2)}, u32[]{:S(2)}) collective-permute-start(bf16[416,1600]{1,0:T(8,128)(2,1)} %collective-permute-done.25.rest_1_), channel_id=1, source_target_pairs={{2,4},{4,2},{3,5},{5,3},{10,12},{12,10},{11,13},{13,11},{18,20},{2... | collective-permute-start | bytes 3993608 | tf_op jit(solution)/shard_map/ppermute | solution.py:51
  188.2 12.6 %collective-permute-start.30 = (bf16[208,1280]{1,0:T(8,128)(2,1)}, bf16[208,1280]{1,0:T(8,128)(2,1)S(1)}, u32[]{:S(2)}, u32[]{:S(2)}) collective-permute-start(bf16[208,1280]{1,0:T(8,128)(2,1)} %slice.80), channel_id=1, source_target_pairs={{0,8},{8,0},{16,24},{24,16},{1,9},{9,1},{17,25},{25,17},{2,10},{10... | collective-permute-start | bytes 1597448 | tf_op jit(solution)/shard_map/ppermute | solution.py:43
  201.0 32.0 %collective-permute-start.33 = (bf16[416,1600]{1,0:T(8,128)(2,1)}, bf16[416,1600]{1,0:T(8,128)(2,1)S(1)}, u32[]{:S(2)}, u32[]{:S(2)}) collective-permute-start(bf16[416,1600]{1,0:T(8,128)(2,1)} %collective-permute-done.25.rest_1_), channel_id=1, source_target_pairs={{4,0},{2,6},{5,1},{3,7},{12,8},{10,14},{13,9},{11,15},{20,16},{18,... | collective-permute-start | bytes 3993608 | tf_op jit(solution)/shard_map/ppermute | solution.py:51
  233.0 13.2 %collective-permute-start.34 = (bf16[1024,1024]{1,0:T(8,128)(2,1)}, bf16[1024,1024]{1,0:T(8,128)(2,1)S(1)}, u32[]{:S(2)}, u32[]{:S(2)}) collective-permute-start(bf16[1024,1024]{1,0:T(8,128)(2,1)} %get-tuple-element.185), channel_id=1, source_target_pairs={{0,1},{1,0},{2,3},{3,2},{4,5},{5,4},{6,7},{7,6},{8,9},{9,8},{10,11... | collective-permute-start | bytes 6291464 | tf_op jit(solution)/shard_map/ppermute | solution.py:55
  263.9 13.1 %collective-permute-start.41 = (bf16[128,800]{1,0:T(8,128)(2,1)}, bf16[128,800]{1,0:T(8,128)(2,1)S(1)}, u32[]{:S(2)}, u32[]{:S(2)}) collective-permute-start(bf16[128,800]{1,0:T(8,128)(2,1)} %get-tuple-element.198), channel_id=1, source_target_pairs={{0,16},{16,0},{8,24},{24,8},{1,17},{17,1},{9,25},{25,9},{2,18},{18... | collective-permute-start | bytes 614408 | tf_op jit(solution)/shard_map/ppermute | solution.py:47
  (63 other events, 519.6 us)
